TPU v7x, 256 devices: a whole 4x4x8 slice. The times are simulated.
256 devices in a mesh: dp: 32 (over y, z_lo, core), tensor: 8 (over x, z_hi).
Axes of the slice: x: 4, y: 4, z: 8 (z_hi: 2, z_lo: 4; z = z_hi * 4 + z_lo), core: 2. Of those that a mesh axis runs over, the one named last changes fastest.
Arguments:
- acts: bfloat16 [32, 256, 8192], P('dp', None, 'tensor'), may hold values from -6 to 6
- out_grads: bfloat16 [32, 256, 14336], P('dp'), may hold values from -24 to 24
- projector: bfloat16 [8192, 128], P('tensor')
- weight: bfloat16 [8192, 14336], P('tensor', 'dp')
- first_moment: float32 [128, 14336], P(None, 'dp')
- second_moment: float32 [128, 14336], P(None, 'dp'), as said below
Outputs:
- new_weight: float32 [8192, 14336], P('tensor', 'dp')
- new_first: float32 [128, 14336], P(None, 'dp')
- new_second: float32 [128, 14336], P(None, 'dp')
Inputs may be any that keep to these rules, and one draw needn't show every extreme that they name: `second_moment`: positive.
All inputs are finite; a program needn't handle non-finite values.
Results may differ from a plain program's by a relative error of at most 0.0033.
Values sent between devices are 32-bit elements; how exact they have to be, the bound alone decides.
No kernel may reach another device: no remote copies, remote signals or barrier semaphores. Data moves between devices by JAX's collectives and lax.ppermute only.
A program may use at most 128 MiB of HBM per device.

v0:
```python
import math

import jax
import jax.numpy as jnp
from jax import lax
from jax.sharding import PartitionSpec as P

STEP = 10


def per_device(acts, out_grads, projector, weight, first_moment, second_moment):
    replicas = lax.axis_size("dp")
    total = acts.shape[1] * replicas
    columns_all = out_grads.shape[2]
    width = math.gcd(columns_all, 2048)
    pieces = []
    for begin in range(0, columns_all, width):
        block = out_grads[0][:, begin : begin + width]
        grad = (
            lax.dot_general(
                acts[0], block, (((0,), (0,)), ((), ())), preferred_element_type=jnp.float32
            )
            / total
        ).astype(jnp.bfloat16)
        pieces.append(
            lax.dot_general(
                projector, grad, (((0,), (0,)), ((), ())), preferred_element_type=jnp.float32
            )
        )
    partial_sum = jnp.concatenate(pieces, axis=1)
    mine_cols = first_moment.shape[1]
    summed = lax.psum(partial_sum, ("dp", "tensor"))
    squares = jnp.sum(summed * summed)
    start = lax.axis_index("dp") * mine_cols
    mine = lax.dynamic_slice_in_dim(summed, start, mine_cols, 1)
    factor = jnp.minimum(jnp.float32(1.0), 1.0 / jnp.sqrt(squares + 1e-12))
    clipped = factor * mine
    new_first = 0.9 * first_moment + 0.1 * clipped
    new_second = 0.999 * second_moment + 0.001 * clipped * clipped
    fix_one = 1.0 - 0.9**STEP
    fix_two = 1.0 - 0.999**STEP
    direction = (new_first / fix_one / (jnp.sqrt(new_second / fix_two) + 1e-08)).astype(
        jnp.bfloat16
    )
    delta = jnp.dot(projector, direction, preferred_element_type=jnp.float32)
    new_weight = weight.astype(jnp.float32) - 0.04 * 0.25 * delta
    return (new_weight, new_first, new_second)


def solution(mesh):
    placed = (
        P("dp", None, "tensor"),
        P("dp", None, None),
        P("tensor", None),
        P("tensor", "dp"),
        P(None, "dp"),
        P(None, "dp"),
    )
    return jax.shard_map(
        per_device,
        mesh=mesh,
        in_specs=placed,
        out_specs=(P("tensor", "dp"), P(None, "dp"), P(None, "dp")),
        check_vma=False,
    )
```

profile of v0, /device:TPU:8, one launch (start us, length us, event | category | flops | bytes accessed | tf_op | source)
XLA Modules:
  0.0 334.7 jit_solution(17462584970889935475)
XLA Ops:
  7.2 0.0 copy-start
  7.2 0.0 copy-start.4
  7.2 0.0 all-reduce.2.cloned.1.call-start
  7.2 1.0 copy-done
  8.2 4.7 %fusion.6 = f32[128,14336]{0,1:T(8,128)} fusion(bf16[1024,128]{1,0:T(8,128)(2,1)} %param.8, bf16[256,14336]{1,0:T(8,128)(2,1)} %bitcast.61, bf16[1,256,1024]{2,1,0:T(8,128)(2,1)S(1)} %copy-done), kind=kOutput, calls=%fused_computation.21 | convolution fusion | flops 1614807040 | bytes 2883584 | tf_op jit(solution)/shard_map/dot_general | solution.py:26
  12.9 0.0 copy-done.4
  12.9 4.7 %fusion.5 = f32[128,14336]{0,1:T(8,128)} fusion(f32[128,14336]{0,1:T(8,128)} %fusion.6, bf16[1024,128]{1,0:T(8,128)(2,1)S(1)} %copy-done.4, bf16[256,14336]{1,0:T(8,128)(2,1)} %bitcast.62, bf16[1,256,1024]{2,1,0:T(8,128)(2,1)S(1)} %copy-done), kind=kOutput, calls=%fused_computation.19 | convolution fusion | flops 1614807040 | bytes 2883584 | tf_op jit(solution)/shard_map/dot_general | solution.py:26
  17.5 4.6 %fusion.4 = f32[128,14336]{0,1:T(8,128)} fusion(f32[128,14336]{0,1:T(8,128)} %fusion.5, bf16[1024,128]{1,0:T(8,128)(2,1)S(1)} %copy-done.4, bf16[256,14336]{1,0:T(8,128)(2,1)} %bitcast.63, bf16[1,256,1024]{2,1,0:T(8,128)(2,1)S(1)} %copy-done), kind=kOutput, calls=%fused_computation.17 | convolution fusion | flops 1614807040 | bytes 2883584 | tf_op jit(solution)/shard_map/dot_general | solution.py:26
  22.1 4.6 %fusion.3 = f32[128,14336]{0,1:T(8,128)} fusion(f32[128,14336]{0,1:T(8,128)} %fusion.4, bf16[1024,128]{1,0:T(8,128)(2,1)S(1)} %copy-done.4, bf16[256,14336]{1,0:T(8,128)(2,1)} %bitcast.64, bf16[1,256,1024]{2,1,0:T(8,128)(2,1)S(1)} %copy-done), kind=kOutput, calls=%fused_computation.15 | convolution fusion | flops 1614807040 | bytes 2883584 | tf_op jit(solution)/shard_map/dot_general | solution.py:26
  26.7 4.6 %fusion.2 = f32[128,14336]{0,1:T(8,128)} fusion(f32[128,14336]{0,1:T(8,128)} %fusion.3, bf16[1024,128]{1,0:T(8,128)(2,1)S(1)} %copy-done.4, bf16[256,14336]{1,0:T(8,128)(2,1)} %bitcast.65, bf16[1,256,1024]{2,1,0:T(8,128)(2,1)S(1)} %copy-done), kind=kOutput, calls=%fused_computation.13 | convolution fusion | flops 1614807040 | bytes 2883584 | tf_op jit(solution)/shard_map/dot_general | solution.py:26
  31.3 4.6 %fusion.1 = f32[128,14336]{0,1:T(8,128)} fusion(f32[128,14336]{0,1:T(8,128)} %fusion.2, bf16[1024,128]{1,0:T(8,128)(2,1)S(1)} %copy-done.4, bf16[256,14336]{1,0:T(8,128)(2,1)} %bitcast.66, bf16[1,256,1024]{2,1,0:T(8,128)(2,1)S(1)} %copy-done), kind=kOutput, calls=%fused_computation.11 | convolution fusion | flops 1614807040 | bytes 2883584 | tf_op jit(solution)/shard_map/dot_general | solution.py:26
  35.9 4.6 %fusion = f32[128,14336]{0,1:T(8,128)} fusion(f32[128,14336]{0,1:T(8,128)} %fusion.1, bf16[1024,128]{1,0:T(8,128)(2,1)S(1)} %copy-done.4, bf16[256,14336]{1,0:T(8,128)(2,1)} %bitcast.67, bf16[1,256,1024]{2,1,0:T(8,128)(2,1)S(1)} %copy-done), kind=kOutput, calls=%fused_computation.9 | convolution fusion | flops 1614807040 | bytes 2883584 | tf_op jit(solution)/shard_map/dot_general | solution.py:26
  40.5 0.0 copy-start.5
  40.5 0.0 copy-start.6
  40.5 0.0 copy-start.1
  40.5 0.0 all-reduce.2.cloned.1.call-update
  40.6 279.2 %all-reduce.2.cloned.1.call-done = f32[128,14336]{0,1:T(8,128)} async-done(((f32[128,14336]{0,1:T(8,128)}), f32[128,14336]{0,1:T(8,128)}) %all-reduce.2.cloned.1.call-update) | async-done | bytes 7340048 | tf_op jit(solution)/shard_map/psum | solution.py:32
  319.7 4.7 %multiply_reduce_fusion = f32[]{:T(128)} fusion(f32[128,14336]{0,1:T(8,128)} %all-reduce.2.cloned.1.call-done), kind=kLoop, calls=%fused_computation.7 | loop fusion | flops 3670015 | bytes 7340036 | tf_op jit(solution)/shard_map/reduce_sum | solution.py:33
  325.1 0.0 copy-done.5
  325.2 0.0 copy-done.6
  325.2 1.0 multiply_add_fusion
  326.2 0.0 copy-start.2
  326.2 0.0 copy-start.3
  326.2 0.0 copy-done.1
  326.2 1.6 bitcast_subtract_fusion
  327.9 0.0 copy-done.2
  327.9 0.0 copy-done.3
Async XLA Ops:
  7.2 1.0 copy-start
  7.2 5.7 %copy-start.4 = (bf16[1024,128]{1,0:T(8,128)(2,1)S(1)}, bf16[1024,128]{1,0:T(8,128)(2,1)}, u32[]{:S(2)}) copy-start(bf16[1024,128]{1,0:T(8,128)(2,1)} %param.8) | copy-start | bytes 786436
  7.2 312.6 %all-reduce.2.cloned.1.call-start = ((), (), s32[]{:S(2)}) async-start(), calls=%async_computation | async-start | bytes 14680064 | tf_op jit(solution)/shard_map/psum | solution.py:32
  40.5 284.6 %copy-start.5 = (f32[128,448]{0,1:T(8,128)S(1)}, f32[128,448]{0,1:T(8,128)}, u32[]{:S(2)}) copy-start(f32[128,448]{0,1:T(8,128)} %param.10) | copy-start | bytes 688132
  40.5 284.6 %copy-start.6 = (f32[128,448]{0,1:T(8,128)S(1)}, f32[128,448]{0,1:T(8,128)}, u32[]{:S(2)}) copy-start(f32[128,448]{0,1:T(8,128)} %param.11) | copy-start | bytes 688132
  40.5 285.7 %copy-start.1 = (bf16[1024,448]{0,1:T(8,128)(2,1)S(1)}, bf16[1024,448]{0,1:T(8,128)(2,1)}, u32[]{:S(2)}) copy-start(bf16[1024,448]{0,1:T(8,128)(2,1)} %param.9) | copy-start | bytes 2752516
  326.2 1.7 copy-start.2
  326.2 1.7 copy-start.3
Sparse Core Ops, SparseCore 0:
  40.7 279.0 all-reduce.1
where the time goes:
time: 335 us
  waiting for transfers between devices  279 us (83%)
  matrix products  34 us (10%)
  between operations  14.8 us (4%)
  other arithmetic  5.72 us (2%)
    psum x1, waiting for transfers between devices, per_device(): summed = lax.psum(partial_sum, ('dp', 'tensor'))  279 us
    dot_general x7, matrix products, per_device(): lax.dot_general(projector, grad, (((0,), (0,)), ((), ())), preferred_elem...  32.3 us
  transfers between devices with their start and end apart: 1, of which 1 were waited for; matrix products, arithmetic and copies ran while one was open for 0% of the time, Pallas kernels for 0%

commit v1 on v0

v1 whole, which is shorter than its diff:
```python
import jax
import jax.numpy as jnp
from jax import lax
from jax.sharding import Mesh
from jax.sharding import PartitionSpec as P

STEP = 10
FINE = ("y", "zl", "c", "x", "zh")
SIZES = (4, 4, 2, 4, 2)
DP = ("y", "zl", "c")
TENSOR = ("x", "zh")


def swap(value, axis):
    return lax.ppermute(value, axis, [(0, 1), (1, 0)])


def per_device(acts, out_grads, projector, weight, first_moment, second_moment):
    tokens = acts.shape[1]
    total = tokens * 32
    rank = projector.shape[1]
    columns = out_grads.shape[2]
    mine_cols = first_moment.shape[1]
    pair_cols = 2 * mine_cols
    chips = columns // pair_cols
    core = lax.axis_index("c")

    y_part = lax.dot_general(
        projector, acts[0], (((0,), (1,)), ((), ())), preferred_element_type=jnp.float32
    )
    mine = rank // 8
    blocks = y_part.reshape(2, 4, mine, tokens).transpose(1, 0, 2, 3).reshape(8, mine, tokens)
    blocks = lax.all_to_all(blocks, TENSOR, 0, 0, tiled=True)
    y = jnp.sum(blocks, axis=0) / total
    half = mine // 2
    own = lax.dynamic_slice_in_dim(y, core * half, half, 0)
    other = lax.dynamic_slice_in_dim(y, (1 - core) * half, half, 0)
    y = jnp.concatenate([own, other], axis=0)
    high = y.astype(jnp.bfloat16)
    low = (y - high.astype(jnp.float32)).astype(jnp.bfloat16)
    both = jnp.concatenate([high, low], axis=0)
    out = jnp.dot(both, out_grads[0], preferred_element_type=jnp.float32)
    out = out[:mine] + out[mine:]
    part = out[:half] + swap(out[half:], "c")
    part = part.reshape(half, chips, pair_cols).transpose(1, 0, 2)
    part = lax.all_to_all(part, ("y", "zl"), 0, 0, tiled=True)
    done = jnp.sum(part, axis=0)
    squares = jnp.sum(done * done)
    left, right = done[:, :mine_cols], done[:, mine_cols:]
    keep = jnp.where(core == 0, left, right)
    give = jnp.where(core == 0, right, left)
    give = jnp.concatenate([give, jnp.broadcast_to(squares, (half, 512 - mine_cols))], axis=1)
    got = swap(give, "c")
    squares = squares + got[0, mine_cols]
    got = got[:, :mine_cols]
    ranks = jnp.where(core == 0, jnp.concatenate([keep, got]), jnp.concatenate([got, keep]))
    send = jnp.concatenate([ranks, jnp.broadcast_to(squares, (mine, 512 - mine_cols))], axis=1)
    send = jnp.broadcast_to(send[None], (4,) + send.shape)
    rows = lax.all_to_all(send, "x", 0, 0, tiled=True)
    squares = jnp.sum(rows[:, 0, mine_cols])
    rows = rows[:, :, :mine_cols].reshape(4 * mine, mine_cols)
    far = swap(rows, "zh")
    zh = lax.axis_index("zh")
    projected = jnp.where(zh == 0, jnp.concatenate([rows, far]), jnp.concatenate([far, rows]))
    spread = jnp.broadcast_to(squares, (32, 8, 128))
    spread = lax.all_to_all(spread, ("y", "zl", "zh"), 0, 0, tiled=True)
    squares = jnp.sum(spread[:, 0, 0])

    factor = jnp.minimum(jnp.float32(1.0), 1.0 / jnp.sqrt(squares + 1e-12))
    clipped = factor * projected
    new_first = 0.9 * first_moment + 0.1 * clipped
    new_second = 0.999 * second_moment + 0.001 * clipped * clipped
    fix_one = 1.0 - 0.9**STEP
    fix_two = 1.0 - 0.999**STEP
    direction = (new_first / fix_one / (jnp.sqrt(new_second / fix_two) + 1e-08)).astype(
        jnp.bfloat16
    )
    delta = jnp.dot(projector, direction, preferred_element_type=jnp.float32)
    new_weight = weight.astype(jnp.float32) - 0.04 * 0.25 * delta
    return (new_weight, new_first, new_second)


def solution(mesh):
    fine = Mesh(mesh.devices.reshape(SIZES), FINE)
    placed = (
        P(DP, None, TENSOR),
        P(DP, None, None),
        P(TENSOR, None),
        P(TENSOR, DP),
        P(None, DP),
        P(None, DP),
    )
    return jax.shard_map(
        per_device,
        mesh=fine,
        in_specs=placed,
        out_specs=(P(TENSOR, DP), P(None, DP), P(None, DP)),
        check_vma=False,
    )
```

time: 335 us -> 89.1 us (0.27)
  waiting for transfers between devices: 279 us -> 32 us
  starting transfers between devices: 0.04 us -> 29.2 us
  matrix products: 34 us -> 6.46 us
  between operations: 14.8 us -> 2.83 us
  blocking collectives: 0 us -> 8.36 us
  local copies, waits for them, and re-layouts: 1.01 us -> 6.44 us
    psum x1 -> x0, waiting for transfers between devices: 279 us -> none  [per_device(): summed = lax.psum(partial_sum, ('dp', 'tensor'))]
    all_to_all x0 -> x3, waiting for transfers between devices: none -> 29 us  [the longest x1 12.8 us: per_device(): part = lax.all_to_all(part, ('y', 'zl'), 0, 0, tiled=True)]
    dot_general x7 -> x2, matrix products: 32.3 us -> 4.77 us  [the longest x1 4.46 us: per_device(): out = jnp.dot(both, out_grads[0], preferred_element_type=jnp.float32)]
    all_to_all x0 -> x3, starting transfers between devices: none -> 23.6 us  [the longest x1 10.9 us: per_device(): blocks = lax.all_to_all(blocks, TENSOR, 0, 0, tiled=True)]
    all_to_all x0 -> x1, blocking collectives: none -> 8.36 us  [per_device(): rows = lax.all_to_all(send, 'x', 0, 0, tiled=True)]
    ppermute x0 -> x3, starting transfers between devices: none -> 5.65 us  [swap(): return lax.ppermute(value, axis, [(0, 1), (1, 0)])]
  transfers between devices with their start and end apart: 1 -> 6, of which waited for: 1 -> 5; matrix products, arithmetic and copies ran while one was open for 0% -> 1% of each run, Pallas kernels for 0% -> 0%
where the time goes in v1:
time: 89.1 us; the launch traced here: 88.4 us
  waiting for transfers between devices  32 us (36%)
  starting transfers between devices  29.2 us (33%)
  blocking collectives  8.36 us (9%)
  matrix products  6.46 us (7%)
  local copies, waits for them, and re-layouts  6.44 us (7%)
  other arithmetic  3.09 us (3%)
  between operations  2.83 us (3%)
    all_to_all x1, waiting for transfers between devices, per_device(): part = lax.all_to_all(part, ('y', 'zl'), 0, 0, tiled=True)  12.8 us
    all_to_all x1, starting transfers between devices, per_device(): blocks = lax.all_to_all(blocks, TENSOR, 0, 0, tiled=True)  10.9 us
    all_to_all x1, waiting for transfers between devices, per_device(): blocks = lax.all_to_all(blocks, TENSOR, 0, 0, tiled=True)  10.6 us
    all_to_all x1, blocking collectives, per_device(): rows = lax.all_to_all(send, 'x', 0, 0, tiled=True)  8.36 us
    all_to_all x1, starting transfers between devices, per_device(): part = lax.all_to_all(part, ('y', 'zl'), 0, 0, tiled=True)  6.43 us
    all_to_all x1, starting transfers between devices, per_device(): spread = lax.all_to_all(spread, ('y', 'zl', 'zh'), 0, 0, tiled=True)  6.24 us
    ppermute x3, starting transfers between devices, swap(): return lax.ppermute(value, axis, [(0, 1), (1, 0)])  5.65 us
    all_to_all x1, waiting for transfers between devices, per_device(): spread = lax.all_to_all(spread, ('y', 'zl', 'zh'), 0, 0, tiled=True)  5.62 us
  transfers between devices with their start and end apart: 6, of which 5 were waited for; matrix products, arithmetic and copies ran while one was open for 1% of the time, Pallas kernels for 0%

profile of v1, /device:TPU:8, one launch (start us, length us, event | category | flops | bytes accessed | tf_op | source)
XLA Modules:
  0.0 88.4 jit_solution(7443183208999532321)
XLA Ops:
  0.6 0.0 copy-start
  0.6 1.1 %copy.23 = bf16[1024,128]{0,1:T(8,128)(2,1)S(1)} copy(bf16[1024,128]{1,0:T(8,128)(2,1)} %param.8) | data formatting | bytes 524288 | tf_op args[2]
  1.8 0.0 copy-done
  1.8 0.3 convolution_bitcast_fusion
  2.1 0.7 copy.24
  2.8 10.9 %all-to-all-start = ((f32[8,16,256]{2,1,0:T(8,128)}), f32[8,16,256]{2,1,0:T(8,128)S(1)}, u32[]{:S(2)}, u32[]{:S(2)}) async-start(f32[8,16,256]{2,1,0:T(8,128)} %bitcast.6), calls=%async_computation | async-start | bytes 262144 | tf_op jit(solution)/shard_map/all_to_all | solution.py:33
  13.7 10.6 %all-to-all-done = f32[8,16,256]{2,1,0:T(8,128)S(1)} async-done(((f32[8,16,256]{2,1,0:T(8,128)}), f32[8,16,256]{2,1,0:T(8,128)S(1)}, u32[]{:S(2)}, u32[]{:S(2)}) %all-to-all-start) | async-done | bytes 131104 | tf_op jit(solution)/shard_map/all_to_all | solution.py:33
  24.4 4.5 %fusion = f32[32,14336]{1,0:T(8,128)S(1)} fusion(bf16[1,256,14336]{2,1,0:T(8,128)(2,1)} %param.7, bf16[16,256]{1,0:T(8,128)(2,1)S(1)} %subtract_convert_fusion, bf16[16,256]{1,0:T(8,128)(2,1)S(1)} %fusion.11), kind=kOutput, calls=%fused_computation | convolution fusion | flops 234913792 | bytes 9191424 | tf_op jit(solution)/shard_map/dot_general | solution.py:42
  28.9 0.1 slice_add_fusion
  29.0 0.0 copy-start.3
  29.0 0.1 collective-permute-start
  29.1 1.8 %collective-permute-done = f32[8,14336]{1,0:T(8,128)S(1)} collective-permute-done((f32[8,14336]{1,0:T(8,128)S(1)}, f32[8,14336]{1,0:T(8,128)S(1)}, u32[]{:S(2)}, u32[]{:S(2)}) %collective-permute-start) | collective-permute-done | bytes 458784 | tf_op jit(solution)/shard_map/ppermute | solution.py:15
  30.9 0.8 slice_add_fusion.1
  31.8 0.0 copy-start.4
  31.8 6.4 %all-to-all-start.1 = ((f32[16,8,896]{2,1,0:T(8,128)}), f32[16,8,896]{2,1,0:T(8,128)S(1)}, u32[]{:S(2)}, u32[]{:S(2)}) async-start(f32[16,8,896]{2,1,0:T(8,128)} %bitcast.9), calls=%async_computation.1 | async-start | bytes 917504 | tf_op jit(solution)/shard_map/all_to_all | solution.py:46
  38.2 12.8 %all-to-all-done.1 = f32[16,8,896]{2,1,0:T(8,128)S(1)} async-done(((f32[16,8,896]{2,1,0:T(8,128)}), f32[16,8,896]{2,1,0:T(8,128)S(1)}, u32[]{:S(2)}, u32[]{:S(2)}) %all-to-all-start.1) | async-done | bytes 458784 | tf_op jit(solution)/shard_map/all_to_all | solution.py:46
  51.0 0.6 multiply_reduce_fusion
  51.6 0.1 slice_select_fusion.1
  51.7 0.7 concatenate.26
  52.4 0.1 collective-permute-start.1
  52.5 1.2 %collective-permute-done.1 = f32[8,512]{1,0:T(8,128)S(1)} collective-permute-done((f32[8,512]{1,0:T(8,128)S(1)}, f32[8,512]{1,0:T(8,128)S(1)}, u32[]{:S(2)}, u32[]{:S(2)}) %collective-permute-start.1) | collective-permute-done | bytes 16416 | tf_op jit(solution)/shard_map/ppermute | solution.py:15
  53.6 0.6 slice.51
  55.6 8.4 %all_to_all.20 = f32[4,16,512]{2,1,0:T(8,128)S(1)} all-to-all(f32[4,16,512]{2,1,0:T(8,128)S(1)} %broadcast_in_dim.4), channel_id=1, replica_groups=mesh['y'=4,'zl'=4,'c'=2,'x'=4,'zh'=2] {'x'}, dimensions={0} | all-to-all | bytes 262144 | tf_op jit(solution)/shard_map/all_to_all | solution.py:59
  63.9 0.7 slice_reduce_fusion.1
  64.6 0.0 copy-start.1
  64.6 0.0 copy-start.2
  64.6 1.4 %broadcast_in_dim.5 = f32[32,8,128]{2,1,0:T(8,128)} broadcast(f32[]{:T(128)} %slice_reduce_fusion.1), dimensions={} | broadcast | bytes 131076 | tf_op jit(solution)/shard_map/broadcast_in_dim | solution.py:65
  66.0 6.2 %all-to-all-start.3 = ((f32[32,8,128]{2,1,0:T(8,128)}), f32[32,8,128]{2,1,0:T(8,128)S(1)}, u32[]{:S(2)}, u32[]{:S(2)}) async-start(f32[32,8,128]{2,1,0:T(8,128)} %broadcast_in_dim.5), calls=%async_computation.3 | async-start | bytes 262144 | tf_op jit(solution)/shard_map/all_to_all | solution.py:66
  72.3 0.0 copy-done.3
  72.3 0.1 copy.22
  72.4 0.0 copy-done.4
  72.4 0.1 copy.26
  72.6 5.5 %collective-permute-start.2 = (f32[64,448]{1,0:T(8,128)S(1)}, f32[64,448]{1,0:T(8,128)S(1)}, u32[]{:S(2)}, u32[]{:S(2)}) collective-permute-start(f32[64,448]{1,0:T(8,128)S(1)} %bitcast.28), channel_id=1, source_target_pairs={{0,1},{1,0},{2,3},{3,2},{4,5},{5,4},{6,7},{7,6},{8,9},{9,8},{10,11... | collective-permute-start | bytes 344072 | tf_op jit(solution)/shard_map/ppermute | solution.py:15
  78.0 5.6 %all-to-all-done.3 = f32[32,8,128]{2,1,0:T(8,128)S(1)} async-done(((f32[32,8,128]{2,1,0:T(8,128)}), f32[32,8,128]{2,1,0:T(8,128)S(1)}, u32[]{:S(2)}, u32[]{:S(2)}) %all-to-all-start.3) | async-done | bytes 131104 | tf_op jit(solution)/shard_map/all_to_all | solution.py:66
  83.6 0.6 slice_reduce_fusion
  85.0 0.0 collective-permute-done.2
  85.0 0.1 multiply_add_fusion
  85.1 0.8 copy.27
  85.9 0.8 copy.28
  86.7 0.0 copy-done.1
  86.7 0.0 copy-done.2
  86.7 1.7 %bitcast_subtract_fusion = f32[1024,448]{0,1:T(8,128)} fusion(bf16[1024,448]{0,1:T(8,128)(2,1)S(1)} %copy-done.2, bf16[1024,128]{1,0:T(8,128)(2,1)S(1)} %copy-done.1, f32[128,448]{1,0:T(8,128)S(1)} %get-tuple-element.13, f32[128,448]{1,0:T(8,128)S(1)} %get-tuple-element.12), kind=kOutput, calls=%fused_computation.2 | convolution fusion | flops 119103488 | bytes 3473408 | tf_op jit(solution)/shard_map/dot_general | solution.py:78
  (10 shorter events, 0.1 us)
Async XLA Ops:
  0.6 1.2 %copy-start = (bf16[1,256,1024]{2,1,0:T(8,128)(2,1)S(1)}, bf16[1,256,1024]{2,1,0:T(8,128)(2,1)}, u32[]{:S(2)}) copy-start(bf16[1,256,1024]{2,1,0:T(8,128)(2,1)} %param.6) | copy-start | bytes 1572868
  2.8 21.5 %all-to-all-start = ((f32[8,16,256]{2,1,0:T(8,128)}), f32[8,16,256]{2,1,0:T(8,128)S(1)}, u32[]{:S(2)}, u32[]{:S(2)}) async-start(f32[8,16,256]{2,1,0:T(8,128)} %bitcast.6), calls=%async_computation | async-start | bytes 262144 | tf_op jit(solution)/shard_map/all_to_all | solution.py:33
  29.0 43.3 %copy-start.3 = (f32[128,448]{0,1:T(8,128)S(1)}, f32[128,448]{0,1:T(8,128)}, u32[]{:S(2)}) copy-start(f32[128,448]{0,1:T(8,128)} %param.10) | copy-start | bytes 688132
  29.0 1.9 %collective-permute-start = (f32[8,14336]{1,0:T(8,128)S(1)}, f32[8,14336]{1,0:T(8,128)S(1)}, u32[]{:S(2)}, u32[]{:S(2)}) collective-permute-start(f32[8,14336]{1,0:T(8,128)S(1)} %slice.47), channel_id=1, source_target_pairs={{0,8},{8,0},{1,9},{9,1},{2,10},{10,2},{3,11},{11,3},{4,12},{12,4},... | collective-permute-start | bytes 1376264 | tf_op jit(solution)/shard_map/ppermute | solution.py:15
  31.8 40.7 %copy-start.4 = (f32[128,448]{0,1:T(8,128)S(1)}, f32[128,448]{0,1:T(8,128)}, u32[]{:S(2)}) copy-start(f32[128,448]{0,1:T(8,128)} %param.11) | copy-start | bytes 688132
  31.8 19.2 %all-to-all-start.1 = ((f32[16,8,896]{2,1,0:T(8,128)}), f32[16,8,896]{2,1,0:T(8,128)S(1)}, u32[]{:S(2)}, u32[]{:S(2)}) async-start(f32[16,8,896]{2,1,0:T(8,128)} %bitcast.9), calls=%async_computation.1 | async-start | bytes 917504 | tf_op jit(solution)/shard_map/all_to_all | solution.py:46
  52.4 1.3 %collective-permute-start.1 = (f32[8,512]{1,0:T(8,128)S(1)}, f32[8,512]{1,0:T(8,128)S(1)}, u32[]{:S(2)}, u32[]{:S(2)}) collective-permute-start(f32[8,512]{1,0:T(8,128)S(1)} %concatenate.26), channel_id=1, source_target_pairs={{0,8},{8,0},{1,9},{9,1},{2,10},{10,2},{3,11},{11,3},{4,12},{12,4},... | collective-permute-start | bytes 49160 | tf_op jit(solution)/shard_map/ppermute | solution.py:15
  64.6 22.1 %copy-start.1 = (bf16[1024,128]{1,0:T(8,128)(2,1)S(1)}, bf16[1024,128]{1,0:T(8,128)(2,1)}, u32[]{:S(2)}) copy-start(bf16[1024,128]{1,0:T(8,128)(2,1)} %param.8) | copy-start | bytes 786436
  64.6 22.1 %copy-start.2 = (bf16[1024,448]{0,1:T(8,128)(2,1)S(1)}, bf16[1024,448]{0,1:T(8,128)(2,1)}, u32[]{:S(2)}) copy-start(bf16[1024,448]{0,1:T(8,128)(2,1)} %param.9) | copy-start | bytes 2752516
  66.0 17.6 %all-to-all-start.3 = ((f32[32,8,128]{2,1,0:T(8,128)}), f32[32,8,128]{2,1,0:T(8,128)S(1)}, u32[]{:S(2)}, u32[]{:S(2)}) async-start(f32[32,8,128]{2,1,0:T(8,128)} %broadcast_in_dim.5), calls=%async_computation.3 | async-start | bytes 262144 | tf_op jit(solution)/shard_map/all_to_all | solution.py:66
  72.6 12.4 %collective-permute-start.2 = (f32[64,448]{1,0:T(8,128)S(1)}, f32[64,448]{1,0:T(8,128)S(1)}, u32[]{:S(2)}, u32[]{:S(2)}) collective-permute-start(f32[64,448]{1,0:T(8,128)S(1)} %bitcast.28), channel_id=1, source_target_pairs={{0,1},{1,0},{2,3},{3,2},{4,5},{5,4},{6,7},{7,6},{8,9},{9,8},{10,11... | collective-permute-start | bytes 344072 | tf_op jit(solution)/shard_map/ppermute | solution.py:15

commit v2 on v1

v2 whole, which is shorter than its diff:
```python
import functools

import jax
import jax.numpy as jnp
from jax import lax
from jax.experimental import pallas as pl
from jax.experimental.pallas import tpu as pltpu
from jax.sharding import Mesh
from jax.sharding import PartitionSpec as P

STEP = 10
FINE = ("y", "zl", "c", "x", "zh")
SIZES = (4, 4, 2, 4, 2)
DP = ("y", "zl", "c")
TENSOR = ("x", "zh")
VMEM = pl.BlockSpec(memory_space=pltpu.VMEM)
SMEM = pl.BlockSpec(memory_space=pltpu.SMEM)
LIMIT = 32 << 20


def swap(value, axis):
    return lax.ppermute(value, axis, [(0, 1), (1, 0)])


def in_vmem(value):
    return pltpu.with_memory_space_constraint(value, pltpu.VMEM)


def call(body, outs, flops=0, nbytes=1 << 20):
    single = not isinstance(outs, list)
    made = [pltpu.VMEM(s, t) for s, t in ([outs] if single else outs)]
    return functools.partial(
        pl.pallas_call,
        body,
        out_shape=made[0] if single else tuple(made),
        out_specs=VMEM if single else tuple(VMEM for _ in made),
        compiler_params=pltpu.CompilerParams(vmem_limit_bytes=LIMIT),
        cost_estimate=pl.CostEstimate(flops=flops, bytes_accessed=nbytes, transcendentals=0),
    )


def first_body(acts_ref, proj_ref, out_ref):
    y = jnp.dot(acts_ref[...], proj_ref[...], preferred_element_type=jnp.float32)
    y = y.T
    mine = out_ref.shape[1]
    for x in range(4):
        for zh in range(2):
            begin = (zh * 4 + x) * mine
            out_ref[x * 2 + zh] = y[begin : begin + mine]


def second_body(total, core_ref, blocks_ref, og_ref, keep_ref, give_ref):
    y = blocks_ref[0]
    for i in range(1, blocks_ref.shape[0]):
        y = y + blocks_ref[i]
    y = y / total
    half = y.shape[0] // 2
    low_half, high_half = y[:half], y[half:]
    is_first = core_ref[0] == 0
    y = jnp.concatenate(
        [
            jnp.where(is_first, low_half, high_half),
            jnp.where(is_first, high_half, low_half),
        ]
    )
    high = y.astype(jnp.bfloat16)
    low = (y - high.astype(jnp.float32)).astype(jnp.bfloat16)
    both = jnp.concatenate([high, low])
    chips, _, width = keep_ref.shape
    for i in range(chips):
        out = jnp.dot(
            both, og_ref[:, i * width : (i + 1) * width], preferred_element_type=jnp.float32
        )
        out = out[: 2 * half] + out[2 * half :]
        keep_ref[i] = out[:half]
        give_ref[i] = out[half:]


def add_body(a_ref, b_ref, out_ref):
    out_ref[...] = a_ref[...] + b_ref[...]


def reduce_body(cols, core_ref, parts_ref, keep_ref, give_ref):
    done = parts_ref[0]
    for i in range(1, parts_ref.shape[0]):
        done = done + parts_ref[i]
    squares = jnp.sum(jnp.sum(done * done, axis=0, keepdims=True), axis=1, keepdims=True)
    wide = keep_ref.shape[1]
    left = done[:, :wide]
    right = pltpu.roll(done, cols, 1)[:, :wide]
    is_first = core_ref[0] == 0
    lane = lax.broadcasted_iota(jnp.int32, left.shape, 1)
    keep_ref[...] = jnp.where(lane < cols, jnp.where(is_first, left, right), squares)
    give_ref[...] = jnp.where(lane < cols, jnp.where(is_first, right, left), squares)


def pair_body(cols, core_ref, keep_ref, got_ref, out_ref):
    keep, got = keep_ref[...], got_ref[...]
    is_first = core_ref[0] == 0
    rows = jnp.concatenate([jnp.where(is_first, keep, got), jnp.where(is_first, got, keep)])
    both = keep + got
    both = jnp.concatenate([both, both])
    lane = lax.broadcasted_iota(jnp.int32, rows.shape, 1)
    rows = jnp.where(lane < cols, rows, both)
    for i in range(out_ref.shape[0]):
        out_ref[i] = rows


def norm_body(rows_ref, out_ref):
    wide = rows_ref.shape[2]
    total = rows_ref[0, 0:1, wide - 1 : wide]
    for i in range(1, rows_ref.shape[0]):
        total = total + rows_ref[i, 0:1, wide - 1 : wide]
    line = jnp.broadcast_to(total, (1, out_ref.shape[2]))
    for i in range(out_ref.shape[0]):
        out_ref[i] = line


def last_body(
    chunk,
    squares_ref,
    rows_ref,
    first_ref,
    second_ref,
    proj_ref,
    weight_ref,
    new_weight_ref,
    new_first_ref,
    new_second_ref,
    turned_ref,
):
    step = pl.program_id(0)

    @pl.when(step == 0)
    def _():
        rows = jnp.concatenate([rows_ref[x * 2 + zh] for zh in range(2) for x in range(4)])
        turned_ref[...] = rows.T

    squares = squares_ref[0]
    for i in range(1, squares_ref.shape[0]):
        squares = squares + squares_ref[i]
    factor = jnp.minimum(jnp.float32(1.0), 1.0 / jnp.sqrt(squares + 1e-12))
    clipped = factor * turned_ref[pl.ds(pl.multiple_of(step * chunk, 16), chunk), :]
    new_first = 0.9 * first_ref[...] + 0.1 * clipped
    new_second = 0.999 * second_ref[...] + 0.001 * clipped * clipped
    new_first_ref[...] = new_first
    new_second_ref[...] = new_second
    fix_one = 1.0 - 0.9**STEP
    fix_two = 1.0 - 0.999**STEP
    direction = (new_first / fix_one / (jnp.sqrt(new_second / fix_two) + 1e-08)).astype(
        jnp.bfloat16
    )
    delta = lax.dot_general(
        direction, proj_ref[...], (((1,), (1,)), ((), ())), preferred_element_type=jnp.float32
    )
    new_weight_ref[...] = weight_ref[...].astype(jnp.float32) - 0.04 * 0.25 * delta


def per_device(acts, out_grads, projector, weight, first_moment, second_moment):
    tokens = acts.shape[1]
    total = tokens * 32
    rows, rank = projector.shape
    columns = out_grads.shape[2]
    cols = first_moment.shape[1]
    chips = columns // (2 * cols)
    mine = rank // 8
    half = mine // 2
    wide = 512
    f32 = jnp.float32
    core = lax.axis_index("c").reshape(1)

    blocks = call(first_body, ((8, mine, tokens), f32))(in_specs=[VMEM, VMEM])(acts[0], projector)
    blocks = lax.all_to_all(blocks, TENSOR, 0, 0, tiled=True)
    block = ((chips, half, 2 * cols), f32)
    keep, give = call(functools.partial(second_body, float(total)), [block, block])(
        in_specs=[SMEM, VMEM, VMEM]
    )(core, blocks, in_vmem(out_grads[0]))
    part = call(add_body, block)(in_specs=[VMEM, VMEM])(keep, swap(give, "c"))
    part = lax.all_to_all(part, ("y", "zl"), 0, 0, tiled=True)
    small = ((half, wide), f32)
    keep, give = call(functools.partial(reduce_body, cols), [small, small])(
        in_specs=[SMEM, VMEM]
    )(core, part)
    sent = call(functools.partial(pair_body, cols), ((8, mine, wide), f32))(
        in_specs=[SMEM, VMEM, VMEM]
    )(core, keep, swap(give, "c"))
    got = lax.all_to_all(sent, TENSOR, 0, 0, tiled=True)
    squares = call(norm_body, ((chips, 1, 128), f32))(in_specs=[VMEM])(got)
    squares = lax.all_to_all(squares, ("y", "zl"), 0, 0, tiled=True)

    steps = 4
    chunk = cols // steps
    whole = lambda *shape: pl.BlockSpec(shape, lambda i: (0,) * len(shape))
    piece = lambda width: pl.BlockSpec((chunk, width), lambda i: (i, 0))
    new_weight, new_first, new_second = pl.pallas_call(
        functools.partial(last_body, chunk),
        grid=(steps,),
        in_specs=[
            whole(chips, 1, 128),
            whole(8, mine, wide),
            piece(rank),
            piece(rank),
            whole(rows, rank),
            piece(rows),
        ],
        out_specs=(piece(rows), piece(rank), piece(rank)),
        out_shape=(
            jax.ShapeDtypeStruct((cols, rows), f32),
            jax.ShapeDtypeStruct((cols, rank), f32),
            jax.ShapeDtypeStruct((cols, rank), f32),
        ),
        scratch_shapes=[pltpu.VMEM((wide, rank), f32)],
        compiler_params=pltpu.CompilerParams(vmem_limit_bytes=LIMIT),
        cost_estimate=pl.CostEstimate(
            flops=2 * cols * rows * rank, bytes_accessed=4 << 20, transcendentals=0
        ),
    )(squares, got, first_moment.T, second_moment.T, projector, weight.T)
    return (new_weight.T, new_first.T, new_second.T)


def solution(mesh):
    fine = Mesh(mesh.devices.reshape(SIZES), FINE)
    placed = (
        P(DP, None, TENSOR),
        P(DP, None, None),
        P(TENSOR, None),
        P(TENSOR, DP),
        P(None, DP),
        P(None, DP),
    )
    return jax.shard_map(
        per_device,
        mesh=fine,
        in_specs=placed,
        out_specs=(P(TENSOR, DP), P(None, DP), P(None, DP)),
        check_vma=False,
    )
```

time: 89.1 us -> 83 us (0.932)
  blocking collectives: 8.36 us -> 47.2 us
  waiting for transfers between devices: 32 us -> 13.6 us
  starting transfers between devices: 29.2 us -> 11.1 us
  matrix products: 6.46 us -> 0 us
  Pallas kernels: 0 us -> 4.94 us
  other arithmetic: 3.09 us -> 0 us
  between operations: 2.83 us -> 0.7 us
  local copies, waits for them, and re-layouts: 6.44 us -> 5.08 us
    all_to_all x1 -> x3, blocking collectives: 8.36 us -> 47.2 us  [the longest x1 18.9 us: per_device(): part = lax.all_to_all(part, ('y', 'zl'), 0, 0, tiled=True)]
    all_to_all x2 -> x0, waiting for transfers between devices: 18.4 us -> none  [the longest x1 12.8 us: per_device(): part = lax.all_to_all(part, ('y', 'zl'), 0, 0, tiled=True)]
    all_to_all x2 -> x0, starting transfers between devices: 12.7 us -> none  [the longest x1 6.43 us: per_device(): part = lax.all_to_all(part, ('y', 'zl'), 0, 0, tiled=True)]
    dot_general x3 -> x0, matrix products: 6.46 us -> none  [the longest x1 4.46 us: per_device(): out = jnp.dot(both, out_grads[0], preferred_element_type=jnp.float32)]
    ppermute x3 -> x2, starting transfers between devices: 5.65 us -> 0.19 us  [swap(): return lax.ppermute(value, axis, [(0, 1), (1, 0)])]
    pallas_call x0 -> x7, Pallas kernels: none -> 4.94 us  [the longest x1 2.5 us: per_device(): pl.pallas_call(functools.partial(last_body, chunk), grid=(steps,), in_spe...]
    unnamed x15 -> x14, local copies, waits for them, and re-layouts: 3.07 us -> 5.08 us
    reduce_sum x5 -> x0, other arithmetic: 1.96 us -> none  [the longest x1 0.67 us: per_device(): squares = jnp.sum(rows[:, 0, mine_cols])]
  transfers between devices with their start and end apart: 6 -> 3, of which waited for: 5 -> 3; matrix products, arithmetic and copies ran while one was open for 1% -> 0% of each run, Pallas kernels for 0% -> 0%
where the time goes in v2:
time: 83 us; the launch traced here: 82.6 us
  blocking collectives  47.2 us (57%)
  waiting for transfers between devices  13.6 us (16%)
  starting transfers between devices  11.1 us (13%)
  local copies, waits for them, and re-layouts  5.08 us (6%)
  Pallas kernels  4.94 us (6%)
    all_to_all x1, blocking collectives, per_device(): part = lax.all_to_all(part, ('y', 'zl'), 0, 0, tiled=True)  18.9 us
    all_to_all x1, blocking collectives, per_device(): got = lax.all_to_all(sent, TENSOR, 0, 0, tiled=True)  14.3 us
    all_to_all x1, blocking collectives, per_device(): squares = lax.all_to_all(squares, ('y', 'zl'), 0, 0, tiled=True)  14 us
    all_to_all x1, starting transfers between devices, per_device(): blocks = lax.all_to_all(blocks, TENSOR, 0, 0, tiled=True)  10.9 us
    all_to_all x1, waiting for transfers between devices, per_device(): blocks = lax.all_to_all(blocks, TENSOR, 0, 0, tiled=True)  10.6 us
    unnamed x14, local copies, waits for them, and re-layouts  5.08 us
    ppermute x2, waiting for transfers between devices, swap(): return lax.ppermute(value, axis, [(0, 1), (1, 0)])  2.97 us
    pallas_call x1, Pallas kernels, per_device(): pl.pallas_call(functools.partial(last_body, chunk), grid=(steps,), in_spe...  2.5 us
  transfers between devices with their start and end apart: 3, of which 3 were waited for; matrix products, arithmetic and copies ran while one was open for 0% of the time, Pallas kernels for 0%

profile of v2, /device:TPU:8, one launch (start us, length us, event | category | flops | bytes accessed | tf_op | source)
XLA Modules:
  0.0 82.6 jit_solution(13455331392318141016)
XLA Ops:
  0.6 0.0 copy-start.1
  0.6 0.9 %copy-done.1 = bf16[1024,128]{1,0:T(8,128)(2,1)S(1)} copy-done((bf16[1024,128]{1,0:T(8,128)(2,1)S(1)}, bf16[1024,128]{1,0:T(8,128)(2,1)}, u32[]{:S(2)}) %copy-start.1) | copy-done | bytes 262168
  1.6 0.0 copy-start.4
  1.6 1.0 %copy-done.4 = bf16[1,256,1024]{2,1,0:T(8,128)(2,1)S(1)} copy-done((bf16[1,256,1024]{2,1,0:T(8,128)(2,1)S(1)}, bf16[1,256,1024]{2,1,0:T(8,128)(2,1)}, u32[]{:S(2)}) %copy-start.4) | copy-done | bytes 524312
  2.6 0.0 copy-start.2
  2.6 0.0 copy-start.3
  2.6 1.0 %shard_map.85 = f32[8,16,256]{2,1,0:T(8,128)} custom-call(bf16[256,1024]{1,0:T(8,128)(2,1)S(1)} %bitcast.11, bf16[1024,128]{1,0:T(8,128)(2,1)S(1)} %copy-done.1), custom_call_target="tpu_custom_call" | custom-call | bytes 1048576 | tf_op jit(solution)/shard_map/pallas_call | solution.py:172
  3.6 10.9 %all-to-all-start = ((f32[8,16,256]{2,1,0:T(8,128)}), f32[8,16,256]{2,1,0:T(8,128)S(1)}, u32[]{:S(2)}, u32[]{:S(2)}) async-start(f32[8,16,256]{2,1,0:T(8,128)} %shard_map.85), calls=%async_computation | async-start | bytes 262144 | tf_op jit(solution)/shard_map/all_to_all | solution.py:173
  14.6 10.6 %all-to-all-done.blocks_ref = f32[8,16,256]{2,1,0:T(8,128)S(1)} async-done(((f32[8,16,256]{2,1,0:T(8,128)}), f32[8,16,256]{2,1,0:T(8,128)S(1)}, u32[]{:S(2)}, u32[]{:S(2)}) %all-to-all-start) | async-done | bytes 131104 | tf_op jit(solution)/shard_map/all_to_all | solution.py:173
  25.2 0.0 copy-start
  25.2 3.1 %copy-done = bf16[1,256,14336]{2,1,0:T(8,128)(2,1)S(1)} copy-done((bf16[1,256,14336]{2,1,0:T(8,128)(2,1)S(1)}, bf16[1,256,14336]{2,1,0:T(8,128)(2,1)}, u32[]{:S(2)}) %copy-start) | copy-done | bytes 7340056
  28.3 0.0 copy-start.5
  28.3 0.0 copy-start.6
  28.3 1.2 %shard_map.86 = (f32[16,8,896]{2,1,0:T(8,128)S(1)}, f32[16,8,896]{2,1,0:T(8,128)S(1)}) custom-call(s32[1]{0:T(128)} %bitcast.core_ref, f32[8,16,256]{2,1,0:T(8,128)S(1)} %all-to-all-done.blocks_ref, bf16[256,14336]{1,0:T(8,128)(2,1)S(1)} %bitcast.9), custom_call_target="tpu_custom_call" | custom-call | bytes 1048576 | tf_op jit(solution)/shard_map/pallas_call | solution.py:175
  29.5 0.1 collective-permute-start
  29.6 1.8 %collective-permute-done.b_ref = f32[16,8,896]{2,1,0:T(8,128)S(1)} collective-permute-done((f32[16,8,896]{2,1,0:T(8,128)S(1)}, f32[16,8,896]{2,1,0:T(8,128)S(1)}, u32[]{:S(2)}, u32[]{:S(2)}) %collective-permute-start) | collective-permute-done | bytes 458784 | tf_op jit(solution)/shard_map/ppermute | solution.py:22
  31.4 18.9 %all_to_all.20.parts_ref = f32[16,8,896]{2,1,0:T(8,128)S(1)} all-to-all(f32[16,8,896]{2,1,0:T(8,128)S(1)} %shard_map.87), channel_id=1, replica_groups=mesh['y'=4,'zl'=4,'c'=2,'x'=4,'zh'=2] {'y','zl'}, dimensions={0} | all-to-all | bytes 917504 | tf_op jit(solution)/shard_map/all_to_all | solution.py:179
  50.3 0.1 shard_map.88
  50.4 0.1 collective-permute-start.1
  50.5 1.2 %collective-permute-done.1.got_ref = f32[8,512]{1,0:T(8,128)S(1)} collective-permute-done((f32[8,512]{1,0:T(8,128)S(1)}, f32[8,512]{1,0:T(8,128)S(1)}, u32[]{:S(2)}, u32[]{:S(2)}) %collective-permute-start.1) | collective-permute-done | bytes 16416 | tf_op jit(solution)/shard_map/ppermute | solution.py:22
  51.7 14.3 %all_to_all.21.rows_ref = f32[8,16,512]{2,1,0:T(8,128)S(1)} all-to-all(f32[8,16,512]{2,1,0:T(8,128)S(1)} %shard_map.89), channel_id=1, replica_groups=mesh['y'=4,'zl'=4,'c'=2,'x'=4,'zh'=2] {'x','zh'}, dimensions={0} | all-to-all | bytes 524288 | tf_op jit(solution)/shard_map/all_to_all | solution.py:187
  66.0 0.1 shard_map.90
  66.1 14.0 %all_to_all.22.squares_ref = f32[16,1,128]{2,1,0:T(1,128)S(1)} all-to-all(f32[16,1,128]{2,1,0:T(1,128)S(1)} %shard_map.90), channel_id=1, replica_groups=mesh['y'=4,'zl'=4,'c'=2,'x'=4,'zh'=2] {'y','zl'}, dimensions={0} | all-to-all | bytes 16384 | tf_op jit(solution)/shard_map/all_to_all | solution.py:189
  80.1 0.0 copy-done.2
  80.1 0.0 copy-done.3
  80.1 0.0 copy-done.5
  80.1 0.0 copy-done.6
  80.1 2.5 %shard_map.91 = (f32[448,1024]{1,0:T(8,128)}, f32[448,128]{1,0:T(8,128)}, f32[448,128]{1,0:T(8,128)}) custom-call(f32[16,1,128]{2,1,0:T(1,128)S(1)} %all_to_all.22.squares_ref, f32[8,16,512]{2,1,0:T(8,128)S(1)} %all_to_all.21.rows_ref, f32[448,128]{1,0:T(8,128)S(1)} %bitcast.12, f32[448,128]{1,0:T(8,128)S(1)} %bitcast.13, bf16[1024,128]{1,0:T(8,128)(2,1)S(1)} %copy-done.2, ...), custom_call_target="tpu_custom_call" | custom-call | flops 117440512 | bytes 4194304 | tf_op jit(solution)/shard_map/pallas_call | solution.py:195
  (2 shorter events, 0.1 us)
Async XLA Ops:
  0.6 1.0 %copy-start.1 = (bf16[1024,128]{1,0:T(8,128)(2,1)S(1)}, bf16[1024,128]{1,0:T(8,128)(2,1)}, u32[]{:S(2)}) copy-start(bf16[1024,128]{1,0:T(8,128)(2,1)} %proj_ref.3) | copy-start | bytes 786436
  1.6 1.0 %copy-start.4 = (bf16[1,256,1024]{2,1,0:T(8,128)(2,1)S(1)}, bf16[1,256,1024]{2,1,0:T(8,128)(2,1)}, u32[]{:S(2)}) copy-start(bf16[1,256,1024]{2,1,0:T(8,128)(2,1)} %param.6) | copy-start | bytes 1572868
  2.6 77.5 %copy-start.2 = (bf16[1024,128]{1,0:T(8,128)(2,1)S(1)}, bf16[1024,128]{1,0:T(8,128)(2,1)}, u32[]{:S(2)}) copy-start(bf16[1024,128]{1,0:T(8,128)(2,1)} %proj_ref.3) | copy-start | bytes 786436
  2.6 77.5 %copy-start.3 = (bf16[1024,448]{0,1:T(8,128)(2,1)S(1)}, bf16[1024,448]{0,1:T(8,128)(2,1)}, u32[]{:S(2)}) copy-start(bf16[1024,448]{0,1:T(8,128)(2,1)} %param.9) | copy-start | bytes 2752516
  3.6 21.5 %all-to-all-start = ((f32[8,16,256]{2,1,0:T(8,128)}), f32[8,16,256]{2,1,0:T(8,128)S(1)}, u32[]{:S(2)}, u32[]{:S(2)}) async-start(f32[8,16,256]{2,1,0:T(8,128)} %shard_map.85), calls=%async_computation | async-start | bytes 262144 | tf_op jit(solution)/shard_map/all_to_all | solution.py:173
  25.2 3.1 %copy-start = (bf16[1,256,14336]{2,1,0:T(8,128)(2,1)S(1)}, bf16[1,256,14336]{2,1,0:T(8,128)(2,1)}, u32[]{:S(2)}) copy-start(bf16[1,256,14336]{2,1,0:T(8,128)(2,1)} %param.7) | copy-start | bytes 22020100
  28.3 51.9 %copy-start.5 = (f32[128,448]{0,1:T(8,128)S(1)}, f32[128,448]{0,1:T(8,128)}, u32[]{:S(2)}) copy-start(f32[128,448]{0,1:T(8,128)} %param.10) | copy-start | bytes 688132
  28.3 51.9 %copy-start.6 = (f32[128,448]{0,1:T(8,128)S(1)}, f32[128,448]{0,1:T(8,128)}, u32[]{:S(2)}) copy-start(f32[128,448]{0,1:T(8,128)} %param.11) | copy-start | bytes 688132
  29.5 1.9 %collective-permute-start = (f32[16,8,896]{2,1,0:T(8,128)S(1)}, f32[16,8,896]{2,1,0:T(8,128)S(1)}, u32[]{:S(2)}, u32[]{:S(2)}) collective-permute-start(f32[16,8,896]{2,1,0:T(8,128)S(1)} %get-tuple-element.11), channel_id=1, source_target_pairs={{0,8},{8,0},{1,9},{9,1},{2,10},{10,2},{3,11},{11,3},{4,12},{12,4},... | collective-permute-start | bytes 1376264 | tf_op jit(solution)/shard_map/ppermute | solution.py:22
  50.4 1.3 %collective-permute-start.1 = (f32[8,512]{1,0:T(8,128)S(1)}, f32[8,512]{1,0:T(8,128)S(1)}, u32[]{:S(2)}, u32[]{:S(2)}) collective-permute-start(f32[8,512]{1,0:T(8,128)S(1)} %get-tuple-element.13), channel_id=1, source_target_pairs={{0,8},{8,0},{1,9},{9,1},{2,10},{10,2},{3,11},{11,3},{4,12},{12,4},... | collective-permute-start | bytes 49160 | tf_op jit(solution)/shard_map/ppermute | solution.py:22

commit v3 on v1

v3 whole, which is shorter than its diff:
```python
import functools

import jax
import jax.numpy as jnp
from jax import lax
from jax.experimental import pallas as pl
from jax.experimental.pallas import tpu as pltpu
from jax.sharding import Mesh
from jax.sharding import PartitionSpec as P

STEP = 10
FINE = ("y", "zl", "c", "x", "zh")
SIZES = (4, 4, 2, 4, 2)
DP = ("y", "zl", "c")
TENSOR = ("x", "zh")
VMEM = pl.BlockSpec(memory_space=pltpu.VMEM)
SMEM = pl.BlockSpec(memory_space=pltpu.SMEM)
HBM = pl.BlockSpec(memory_space=pl.ANY)
LIMIT = 6 << 20
F32 = jnp.float32
BF16 = jnp.bfloat16


def swap(value, axis):
    return lax.ppermute(value, axis, [(0, 1), (1, 0)])


def trade(values, axis):
    out = [values[0]]
    for k in (1, 2, 3):
        out.append(lax.ppermute(values[k], axis, [(i, i ^ k) for i in range(4)]))
    return out


def in_hbm(value):
    return pltpu.with_memory_space_constraint(value, pltpu.HBM)


def run(body, outs, specs, args, scratch=(), flops=0, nbytes=1 << 20):
    single = not isinstance(outs, list)
    made = [
        pltpu.VMEM(*(s if isinstance(s[0], tuple) else (s, F32))) for s in ([outs] if single else outs)
    ]
    return pl.pallas_call(
        body,
        in_specs=specs,
        out_shape=made[0] if single else tuple(made),
        out_specs=VMEM if single else tuple(VMEM for _ in made),
        scratch_shapes=list(scratch),
        compiler_params=pltpu.CompilerParams(vmem_limit_bytes=LIMIT),
        cost_estimate=pl.CostEstimate(flops=flops, bytes_accessed=nbytes, transcendentals=0),
    )(*args)


def total_of(refs):
    total = refs[0][...]
    for ref in refs[1:]:
        total = total + ref[...]
    return total


def first_body(x_ref, acts_hbm, proj_hbm, *rest):
    outs, (acts_ref, proj_ref, turned_ref, sems) = rest[:-4], rest[-4:]
    one = pltpu.make_async_copy(acts_hbm, acts_ref, sems.at[0])
    two = pltpu.make_async_copy(proj_hbm, proj_ref, sems.at[1])
    two.start()
    one.start()
    two.wait()
    one.wait()
    y = jnp.dot(acts_ref[...], proj_ref[...], preferred_element_type=F32)
    turned_ref[...] = y.T
    for k in range(4):
        begin = pl.multiple_of((x_ref[0] ^ k) * 32, 32)
        outs[k][...] = turned_ref[pl.ds(begin, 32), :]


def fetch_body(og_hbm, after_ref, og_ref, sems):
    rows = og_hbm.shape[0] // sems.shape[0]
    copies = []
    for n in range(sems.shape[0]):
        part = pl.ds(n * rows, rows)
        copies.append(pltpu.make_async_copy(og_hbm.at[part], og_ref.at[part], sems.at[n]))
        copies[-1].start()
    for copy in copies:
        copy.wait()


def split_body(zh_ref, *refs):
    ins, (keep_ref, give_ref) = refs[:4], refs[4:]
    y = total_of(ins)
    low = jnp.concatenate([y[0:8], y[16:24]])
    high = jnp.concatenate([y[8:16], y[24:32]])
    is_first = zh_ref[0] == 0
    keep_ref[...] = jnp.where(is_first, low, high)
    give_ref[...] = jnp.where(is_first, high, low)


def second_body(total, c_ref, one_ref, two_ref, og_ref, keep_ref, give_ref):
    y = (one_ref[...] + two_ref[...]) / total
    low_half, high_half = y[:8], y[8:]
    is_first = c_ref[0] == 0
    y = jnp.concatenate(
        [
            jnp.where(is_first, low_half, high_half),
            jnp.where(is_first, high_half, low_half),
        ]
    )
    high = y.astype(BF16)
    low = (y - high.astype(F32)).astype(BF16)
    both = jnp.concatenate([high, low])
    chips, _, width = keep_ref.shape
    for i in range(chips):
        columns = og_ref[:, i * width : (i + 1) * width]
        out = jnp.dot(both, columns, preferred_element_type=F32)
        out = out[:16] + out[16:]
        keep_ref[i] = out[:8]
        give_ref[i] = out[8:]


def by_y_body(y_ref, a_ref, b_ref, *outs):
    for k in range(4):
        begin = (y_ref[0] ^ k) * 4
        outs[k][...] = a_ref[pl.ds(begin, 4)] + b_ref[pl.ds(begin, 4)]


def by_zl_body(zl_ref, *refs):
    ins, outs = refs[:4], refs[4:]
    for k in range(4):
        at = zl_ref[0] ^ k
        outs[k][...] = ins[0][at] + ins[1][at] + ins[2][at] + ins[3][at]


def squares_body(*refs):
    ins, (done_ref, line_ref) = refs[:-2], refs[-2:]
    done = total_of(ins)
    width = done.shape[1]
    squares = jnp.sum(jnp.sum(done * done, axis=0, keepdims=True), axis=1, keepdims=True)
    done_ref[:, :width] = done
    done_ref[:, width:] = jnp.broadcast_to(squares, done_ref[:, width:].shape)
    line_ref[...] = jnp.broadcast_to(squares, line_ref.shape)


def both_cores_body(done_ref, line_ref, out_ref):
    width = out_ref.shape[1] - 128
    out_ref[:, :width] = done_ref[:, :width]
    out_ref[:, width:] = done_ref[:, width:] + line_ref[0:1, :]


def by_column_body(cols, zh_ref, c_ref, keep_ref, got_ref, squares_ref, own_ref, give_ref):
    keep, got = keep_ref[...], got_ref[...]
    width = keep.shape[1] - 128
    is_first = zh_ref[0] == 0
    rows = jnp.concatenate([jnp.where(is_first, keep, got), jnp.where(is_first, got, keep)])
    squares_ref[...] = jnp.broadcast_to(
        keep[0:1, width:] + got[0:1, width:], squares_ref.shape
    )
    wide = own_ref.shape[1]
    left = rows[:, :wide]
    right = pltpu.roll(rows[:, :width], cols, 1)[:, :wide]
    is_first = c_ref[0] == 0
    own_ref[...] = jnp.where(is_first, left, right)
    give_ref[...] = jnp.where(is_first, right, left)


def by_core_body(c_ref, keep_ref, got_ref, out_ref):
    keep, got = keep_ref[...], got_ref[...]
    is_first = c_ref[0] == 0
    out_ref[:16] = jnp.where(is_first, keep, got)
    out_ref[16:] = jnp.where(is_first, got, keep)


def last_body(
    steps,
    x_ref,
    squares_ref,
    lines0_ref,
    lines1_ref,
    lines2_ref,
    lines3_ref,
    first_ref,
    second_ref,
    proj_ref,
    weight_ref,
    new_weight_hbm,
    new_first_hbm,
    new_second_hbm,
    rows_ref,
    turned_ref,
    new_weight_ref,
    new_first_ref,
    new_second_ref,
    sems,
):
    for k, ref in enumerate((lines0_ref, lines1_ref, lines2_ref, lines3_ref)):
        begin = pl.multiple_of((x_ref[0] ^ k) * 32, 32)
        rows_ref[pl.ds(begin, 32), :] = ref[...]
    turned_ref[...] = rows_ref[...].T
    squares = jnp.sum(squares_ref[...], axis=0)[0:1]
    factor = jnp.minimum(jnp.float32(1.0), 1.0 / jnp.sqrt(squares + 1e-12))
    fix_one = 1.0 - 0.9**STEP
    fix_two = 1.0 - 0.999**STEP
    chunk = first_ref.shape[0] // steps
    copies = []
    for i in range(steps):
        here = pl.ds(i * chunk, chunk)
        clipped = factor * turned_ref[here, :]
        new_first = 0.9 * first_ref[here, :] + 0.1 * clipped
        new_second = 0.999 * second_ref[here, :] + 0.001 * clipped * clipped
        new_first_ref[here, :] = new_first
        new_second_ref[here, :] = new_second
        direction = new_first / fix_one / (jnp.sqrt(new_second / fix_two) + 1e-08)
        delta = lax.dot_general(
            direction.astype(BF16),
            proj_ref[...],
            (((1,), (1,)), ((), ())),
            preferred_element_type=F32,
        )
        new_weight_ref[here, :] = weight_ref[here, :].astype(F32) - 0.04 * 0.25 * delta
        for n, (src, dst) in enumerate(
            (
                (new_weight_ref, new_weight_hbm),
                (new_first_ref, new_first_hbm),
                (new_second_ref, new_second_hbm),
            )
        ):
            copies.append(pltpu.make_async_copy(src.at[here], dst.at[here], sems.at[i, n]))
            copies[-1].start()
    for copy in copies:
        copy.wait()


def per_device(acts, out_grads, projector, weight, first_moment, second_moment):
    tokens = acts.shape[1]
    total = float(tokens * 32)
    rows, rank = projector.shape
    columns = out_grads.shape[2]
    cols = first_moment.shape[1]
    width = 2 * cols
    chips = columns // width
    wide = 512
    me_y, me_zl, me_c, me_x, me_zh = [lax.axis_index(name).reshape(1) for name in FINE]

    y = run(
        first_body,
        [(32, tokens)] * 4,
        [SMEM, HBM, HBM],
        (me_x, in_hbm(acts[0]), in_hbm(projector)),
        [
            pltpu.VMEM((tokens, rows), BF16),
            pltpu.VMEM((rows, rank), BF16),
            pltpu.VMEM((rank, tokens), F32),
            pltpu.SemaphoreType.DMA((2,)),
        ],
    )
    y = trade(y, "x")
    keep, give = run(split_body, [(16, tokens)] * 2, [SMEM] + [VMEM] * 4, (me_zh, *y))
    got = swap(give, "zh")
    og = run(
        fetch_body,
        ((tokens, columns), BF16),
        [HBM, HBM],
        (in_hbm(out_grads[0]), keep),
        [pltpu.SemaphoreType.DMA((4,))],
        nbytes=16 << 20,
    )
    keep, give = run(
        functools.partial(second_body, total),
        [(chips, 8, width)] * 2,
        [SMEM] + [VMEM] * 3,
        (me_c, keep, got, og),
        flops=2 * 32 * tokens * columns,
        nbytes=8 << 20,
    )
    parts = run(by_y_body, [(4, 8, width)] * 4, [SMEM, VMEM, VMEM], (me_y, keep, swap(give, "c")))
    parts = trade(parts, "y")
    parts = run(by_zl_body, [(8, width)] * 4, [SMEM] + [VMEM] * 4, (me_zl, *parts))
    parts = trade(parts, "zl")
    done, line = run(squares_body, [(8, width + 128), (8, 128)], [VMEM] * 4, tuple(parts))
    done = run(both_cores_body, (8, width + 128), [VMEM] * 2, (done, swap(line, "c")))
    squares, keep, give = run(
        functools.partial(by_column_body, cols),
        [(64, 2, 128), (16, wide), (16, wide)],
        [SMEM, SMEM, VMEM, VMEM],
        (me_zh, me_c, done, swap(done, "zh")),
    )
    squares = lax.all_to_all(squares, ("y", "zl", "x"), 0, 0, tiled=True)
    lines = run(by_core_body, (32, wide), [SMEM, VMEM, VMEM], (me_c, keep, swap(give, "c")))
    lines = trade([lines] * 4, "x")

    steps = 4
    outs = [(cols, rows), (cols, rank), (cols, rank)]
    new_weight, new_first, new_second = pl.pallas_call(
        functools.partial(last_body, steps),
        in_specs=[SMEM] + [VMEM] * 9,
        out_specs=(HBM,) * 3,
        out_shape=tuple(jax.ShapeDtypeStruct(shape, F32) for shape in outs),
        scratch_shapes=[
            pltpu.VMEM((rank, wide), F32),
            pltpu.VMEM((wide, rank), F32),
            *[pltpu.VMEM(shape, F32) for shape in outs],
            pltpu.SemaphoreType.DMA((steps, 3)),
        ],
        compiler_params=pltpu.CompilerParams(vmem_limit_bytes=LIMIT),
        cost_estimate=pl.CostEstimate(
            flops=2 * cols * rows * rank, bytes_accessed=4 << 20, transcendentals=0
        ),
    )(me_x, squares, *lines, first_moment.T, second_moment.T, projector, weight.T)
    return (new_weight.T, new_first.T, new_second.T)


def solution(mesh):
    fine = Mesh(mesh.devices.reshape(SIZES), FINE)
    placed = (
        P(DP, None, TENSOR),
        P(DP, None, None),
        P(TENSOR, None),
        P(TENSOR, DP),
        P(None, DP),
        P(None, DP),
    )
    return jax.shard_map(
        per_device,
        mesh=fine,
        in_specs=placed,
        out_specs=(P(TENSOR, DP), P(None, DP), P(None, DP)),
        check_vma=False,
    )
```

time: 89.1 us -> 72.4 us (0.81)
  Pallas kernels: 0 us -> 8.54 us
  blocking collectives: 8.36 us -> 0 us
  starting transfers between devices: 29.2 us -> 36.6 us
  matrix products: 6.46 us -> 0 us
  local copies, waits for them, and re-layouts: 6.44 us -> 0.03 us
  waiting for transfers between devices: 32 us -> 26.2 us
  other arithmetic: 3.09 us -> 0 us
  between operations: 2.83 us -> 0.78 us
    all_to_all x3 -> x1, waiting for transfers between devices: 29 us -> 0.01 us  [per_device(): squares = lax.all_to_all(squares, ('y', 'zl', 'x'), 0, 0, tiled=True)]
    ppermute x0 -> x12, waiting for transfers between devices: none -> 18.6 us  [trade(): out.append(lax.ppermute(values[k], axis, [(i, i ^ k) for i in range(4)]))]
    ppermute x0 -> x12, starting transfers between devices: none -> 17.6 us  [trade(): out.append(lax.ppermute(values[k], axis, [(i, i ^ k) for i in range(4)]))]
    all_to_all x3 -> x1, starting transfers between devices: 23.6 us -> 7.12 us  [per_device(): squares = lax.all_to_all(squares, ('y', 'zl', 'x'), 0, 0, tiled=True)]
    pallas_call x0 -> x11, Pallas kernels: none -> 8.54 us  [the longest x10 6.72 us: run(): pl.pallas_call(body, in_specs=specs, out_shape=made[0] if single else tup...]
    all_to_all x1 -> x0, blocking collectives: 8.36 us -> none  [per_device(): rows = lax.all_to_all(send, 'x', 0, 0, tiled=True)]
    dot_general x3 -> x0, matrix products: 6.46 us -> none  [the longest x1 4.46 us: per_device(): out = jnp.dot(both, out_grads[0], preferred_element_type=jnp.float32)]
    ppermute x3 -> x5, starting transfers between devices: 5.65 us -> 11.9 us  [swap(): return lax.ppermute(value, axis, [(0, 1), (1, 0)])]
  transfers between devices with their start and end apart: 6 -> 18, of which waited for: 5 -> 14; matrix products, arithmetic and copies ran while one was open for 1% -> 0% of each run, Pallas kernels for 0% -> 4%
where the time goes in v3:
time: 72.4 us; the launch traced here: 72.2 us
  starting transfers between devices  36.6 us (51%)
  waiting for transfers between devices  26.2 us (36%)
  Pallas kernels  8.54 us (12%)
  between operations  0.78 us (1%)
    ppermute x12, waiting for transfers between devices, trade(): out.append(lax.ppermute(values[k], axis, [(i, i ^ k) for i in range(4)]))  18.6 us
    ppermute x12, starting transfers between devices, trade(): out.append(lax.ppermute(values[k], axis, [(i, i ^ k) for i in range(4)]))  17.6 us
    ppermute x5, starting transfers between devices, swap(): return lax.ppermute(value, axis, [(0, 1), (1, 0)])  11.9 us
    ppermute x5, waiting for transfers between devices, swap(): return lax.ppermute(value, axis, [(0, 1), (1, 0)])  7.58 us
    all_to_all x1, starting transfers between devices, per_device(): squares = lax.all_to_all(squares, ('y', 'zl', 'x'), 0, 0, tiled=True)  7.12 us
    pallas_call x10, Pallas kernels, run(): pl.pallas_call(body, in_specs=specs, out_shape=made[0] if single else tup...  6.72 us
    pallas_call x1, Pallas kernels, per_device(): pl.pallas_call(functools.partial(last_body, steps), in_specs=[SMEM] + [VM...  1.82 us
  transfers between devices with their start and end apart: 18, of which 14 were waited for; matrix products, arithmetic and copies ran while one was open for 0% of the time, Pallas kernels for 4%

profile of v3, /device:TPU:8, one launch (start us, length us, event | category | flops | bytes accessed | tf_op | source)
XLA Modules:
  0.0 72.2 jit_solution(16759779489308694808)
XLA Ops:
  0.6 1.5 %shard_map.85 = (f32[32,256]{1,0:T(8,128)S(1)}, f32[32,256]{1,0:T(8,128)S(1)}, f32[32,256]{1,0:T(8,128)S(1)}, f32[32,256]{1,0:T(8,128)S(1)}) custom-call(s32[1]{0:T(128)} %bitcast.x_ref, bf16[256,1024]{1,0:T(8,128)(2,1)} %bitcast.17, bf16[1024,128]{1,0:T(8,128)(2,1)} %proj_ref.1), custom_call_target="tpu_custom_call" | custom-call | bytes 1048576 | tf_op jit(solution)/shard_map/pallas_call | solution.py:44
  2.2 1.6 %collective-permute-start = (f32[32,256]{1,0:T(8,128)S(1)}, f32[32,256]{1,0:T(8,128)S(1)}, u32[]{:S(2)}, u32[]{:S(2)}) collective-permute-start(f32[32,256]{1,0:T(8,128)S(1)} %get-tuple-element.28), channel_id=1, source_target_pairs={{0,2},{2,0},{4,6},{6,4},{1,3},{3,1},{5,7},{7,5},{8,10},{10,8},{12,... | collective-permute-start | bytes 98312 | tf_op jit(solution)/shard_map/ppermute | solution.py:31
  3.7 2.7 %collective-permute-start.1 = (f32[32,256]{1,0:T(8,128)S(1)}, f32[32,256]{1,0:T(8,128)S(1)}, u32[]{:S(2)}, u32[]{:S(2)}) collective-permute-start(f32[32,256]{1,0:T(8,128)S(1)} %get-tuple-element.29), channel_id=1, source_target_pairs={{0,4},{2,6},{4,0},{6,2},{1,5},{3,7},{5,1},{7,3},{8,12},{10,14},{12... | collective-permute-start | bytes 98312 | tf_op jit(solution)/shard_map/ppermute | solution.py:31
  6.5 0.5 collective-permute-start.2
  6.9 0.0 collective-permute-done.refs_1_
  6.9 2.2 %collective-permute-done.1.refs_2_ = f32[32,256]{1,0:T(8,128)S(1)} collective-permute-done((f32[32,256]{1,0:T(8,128)S(1)}, f32[32,256]{1,0:T(8,128)S(1)}, u32[]{:S(2)}, u32[]{:S(2)}) %collective-permute-start.1) | collective-permute-done | bytes 32800 | tf_op jit(solution)/shard_map/ppermute | solution.py:31
  9.1 2.4 %collective-permute-done.2.refs_3_ = f32[32,256]{1,0:T(8,128)S(1)} collective-permute-done((f32[32,256]{1,0:T(8,128)S(1)}, f32[32,256]{1,0:T(8,128)S(1)}, u32[]{:S(2)}, u32[]{:S(2)}) %collective-permute-start.2) | collective-permute-done | bytes 32800 | tf_op jit(solution)/shard_map/ppermute | solution.py:31
  11.6 7.3 %collective-permute-start.3 = (f32[16,256]{1,0:T(8,128)S(1)}, f32[16,256]{1,0:T(8,128)S(1)}, u32[]{:S(2)}, u32[]{:S(2)}) collective-permute-start(f32[16,256]{1,0:T(8,128)S(1)} %get-tuple-element.32), channel_id=1, source_target_pairs={{0,1},{1,0},{2,3},{3,2},{4,5},{5,4},{6,7},{7,6},{8,9},{9,8},{10,11... | collective-permute-start | bytes 49160 | tf_op jit(solution)/shard_map/ppermute | solution.py:25
  18.9 3.2 %shard_map.87.og_ref = bf16[256,14336]{1,0:T(8,128)(2,1)S(1)} custom-call(bf16[256,14336]{1,0:T(8,128)(2,1)} %bitcast.16, f32[16,256]{1,0:T(8,128)S(1)} %get-tuple-element.31.after_ref.one_ref), custom_call_target="tpu_custom_call" | custom-call | bytes 16777216 | tf_op jit(solution)/shard_map/pallas_call | solution.py:44
  22.1 0.0 copy-start
  22.1 0.0 copy-start.1
  22.1 0.0 copy-start.2
  22.1 0.0 copy-start.3
  22.1 0.0 collective-permute-done.3.two_ref
  22.1 1.2 %shard_map.88 = (f32[16,8,896]{2,1,0:T(8,128)S(1)}, f32[16,8,896]{2,1,0:T(8,128)S(1)}) custom-call(s32[1]{0:T(128)} %bitcast.2.c_ref, f32[16,256]{1,0:T(8,128)S(1)} %get-tuple-element.31.after_ref.one_ref, f32[16,256]{1,0:T(8,128)S(1)} %collective-permute-done.3.two_ref, bf16[256,14336]{1,0:T(8,128)(2,1)S(1)} %shard_map.87.og_ref), custom_call_target="tpu_custom_call" | custom-call | flops 234881024 | bytes 8388608 | tf_op jit(solution)/shard_map/pallas_call | solution.py:44
  23.3 0.1 collective-permute-start.4
  23.4 1.8 %collective-permute-done.4.b_ref = f32[16,8,896]{2,1,0:T(8,128)S(1)} collective-permute-done((f32[16,8,896]{2,1,0:T(8,128)S(1)}, f32[16,8,896]{2,1,0:T(8,128)S(1)}, u32[]{:S(2)}, u32[]{:S(2)}) %collective-permute-start.4) | collective-permute-done | bytes 458784 | tf_op jit(solution)/shard_map/ppermute | solution.py:25
  25.3 0.5 collective-permute-start.5
  25.8 2.6 %collective-permute-start.6 = (f32[4,8,896]{2,1,0:T(8,128)S(1)}, f32[4,8,896]{2,1,0:T(8,128)S(1)}, u32[]{:S(2)}, u32[]{:S(2)}) collective-permute-start(f32[4,8,896]{2,1,0:T(8,128)S(1)} %get-tuple-element.37), channel_id=1, source_target_pairs={{0,128},{64,192},{128,0},{192,64},{1,129},{65,193},{129,1},{193,65... | collective-permute-start | bytes 344072 | tf_op jit(solution)/shard_map/ppermute | solution.py:31
  28.4 0.5 collective-permute-start.7
  28.9 1.7 %collective-permute-done.5.refs_1_ = f32[4,8,896]{2,1,0:T(8,128)S(1)} collective-permute-done((f32[4,8,896]{2,1,0:T(8,128)S(1)}, f32[4,8,896]{2,1,0:T(8,128)S(1)}, u32[]{:S(2)}, u32[]{:S(2)}) %collective-permute-start.5) | collective-permute-done | bytes 114720 | tf_op jit(solution)/shard_map/ppermute | solution.py:31
  30.5 3.6 %collective-permute-done.6.refs_2_ = f32[4,8,896]{2,1,0:T(8,128)S(1)} collective-permute-done((f32[4,8,896]{2,1,0:T(8,128)S(1)}, f32[4,8,896]{2,1,0:T(8,128)S(1)}, u32[]{:S(2)}, u32[]{:S(2)}) %collective-permute-start.6) | collective-permute-done | bytes 114720 | tf_op jit(solution)/shard_map/ppermute | solution.py:31
  34.1 1.4 %collective-permute-done.7.refs_3_ = f32[4,8,896]{2,1,0:T(8,128)S(1)} collective-permute-done((f32[4,8,896]{2,1,0:T(8,128)S(1)}, f32[4,8,896]{2,1,0:T(8,128)S(1)}, u32[]{:S(2)}, u32[]{:S(2)}) %collective-permute-start.7) | collective-permute-done | bytes 114720 | tf_op jit(solution)/shard_map/ppermute | solution.py:31
  35.5 2.0 %collective-permute-start.10 = (f32[8,896]{1,0:T(8,128)S(1)}, f32[8,896]{1,0:T(8,128)S(1)}, u32[]{:S(2)}, u32[]{:S(2)}) collective-permute-start(f32[8,896]{1,0:T(8,128)S(1)} %get-tuple-element.42), channel_id=1, source_target_pairs={{0,48},{16,32},{32,16},{48,0},{1,49},{17,33},{33,17},{49,1},{2,50}... | collective-permute-start | bytes 86024 | tf_op jit(solution)/shard_map/ppermute | solution.py:31
  37.5 0.1 collective-permute-start.8
  37.6 2.4 %collective-permute-start.9 = (f32[8,896]{1,0:T(8,128)S(1)}, f32[8,896]{1,0:T(8,128)S(1)}, u32[]{:S(2)}, u32[]{:S(2)}) collective-permute-start(f32[8,896]{1,0:T(8,128)S(1)} %get-tuple-element.41), channel_id=1, source_target_pairs={{0,32},{16,48},{32,0},{48,16},{1,33},{17,49},{33,1},{49,17},{2,34}... | collective-permute-start | bytes 86024 | tf_op jit(solution)/shard_map/ppermute | solution.py:31
  40.0 1.4 %collective-permute-done.10.refs_3_ = f32[8,896]{1,0:T(8,128)S(1)} collective-permute-done((f32[8,896]{1,0:T(8,128)S(1)}, f32[8,896]{1,0:T(8,128)S(1)}, u32[]{:S(2)}, u32[]{:S(2)}) %collective-permute-start.10) | collective-permute-done | bytes 28704 | tf_op jit(solution)/shard_map/ppermute | solution.py:31
  41.3 0.2 collective-permute-done.8.refs_1_
  41.6 0.8 %collective-permute-done.9.refs_2_ = f32[8,896]{1,0:T(8,128)S(1)} collective-permute-done((f32[8,896]{1,0:T(8,128)S(1)}, f32[8,896]{1,0:T(8,128)S(1)}, u32[]{:S(2)}, u32[]{:S(2)}) %collective-permute-start.9) | collective-permute-done | bytes 28704 | tf_op jit(solution)/shard_map/ppermute | solution.py:31
  42.4 0.1 shard_map.91
  42.5 0.0 collective-permute-start.11
  42.5 1.2 %collective-permute-done.11.line_ref = f32[8,128]{1,0:T(8,128)S(1)} collective-permute-done((f32[8,128]{1,0:T(8,128)S(1)}, f32[8,128]{1,0:T(8,128)S(1)}, u32[]{:S(2)}, u32[]{:S(2)}) %collective-permute-start.11) | collective-permute-done | bytes 4128 | tf_op jit(solution)/shard_map/ppermute | solution.py:25
  43.7 4.4 %collective-permute-start.12 = (f32[8,1024]{1,0:T(8,128)S(1)}, f32[8,1024]{1,0:T(8,128)S(1)}, u32[]{:S(2)}, u32[]{:S(2)}) collective-permute-start(f32[8,1024]{1,0:T(8,128)S(1)} %shard_map.92.keep_ref), channel_id=1, source_target_pairs={{0,1},{1,0},{2,3},{3,2},{4,5},{5,4},{6,7},{7,6},{8,9},{9,8},{10,11... | collective-permute-start | bytes 98312 | tf_op jit(solution)/shard_map/ppermute | solution.py:25
  48.1 3.4 %collective-permute-done.12.got_ref = f32[8,1024]{1,0:T(8,128)S(1)} collective-permute-done((f32[8,1024]{1,0:T(8,128)S(1)}, f32[8,1024]{1,0:T(8,128)S(1)}, u32[]{:S(2)}, u32[]{:S(2)}) %collective-permute-start.12) | collective-permute-done | bytes 32800 | tf_op jit(solution)/shard_map/ppermute | solution.py:25
  51.5 0.7 shard_map.93
  52.2 7.1 %all-to-all-start = ((f32[64,2,128]{2,1,0:T(2,128)}), f32[64,2,128]{2,1,0:T(2,128)S(1)}, u32[]{:S(2)}, u32[]{:S(2)}) async-start(f32[64,2,128]{2,1,0:T(2,128)} %get-tuple-element.45), calls=%async_computation | async-start | bytes 131072 | tf_op jit(solution)/shard_map/all_to_all | solution.py:286
  59.3 0.1 collective-permute-start.13
  59.4 1.2 %collective-permute-done.13.got_ref = f32[16,512]{1,0:T(8,128)S(1)} collective-permute-done((f32[16,512]{1,0:T(8,128)S(1)}, f32[16,512]{1,0:T(8,128)S(1)}, u32[]{:S(2)}, u32[]{:S(2)}) %collective-permute-start.13) | collective-permute-done | bytes 32800 | tf_op jit(solution)/shard_map/ppermute | solution.py:25
  60.6 1.6 %collective-permute-start.14 = (f32[32,512]{1,0:T(8,128)S(1)}, f32[32,512]{1,0:T(8,128)S(1)}, u32[]{:S(2)}, u32[]{:S(2)}) collective-permute-start(f32[32,512]{1,0:T(8,128)S(1)} %shard_map.94.lines0_ref), channel_id=1, source_target_pairs={{0,2},{2,0},{4,6},{6,4},{1,3},{3,1},{5,7},{7,5},{8,10},{10,8},{12,... | collective-permute-start | bytes 196616 | tf_op jit(solution)/shard_map/ppermute | solution.py:31
  62.2 2.7 %collective-permute-start.15 = (f32[32,512]{1,0:T(8,128)S(1)}, f32[32,512]{1,0:T(8,128)S(1)}, u32[]{:S(2)}, u32[]{:S(2)}) collective-permute-start(f32[32,512]{1,0:T(8,128)S(1)} %shard_map.94.lines0_ref), channel_id=1, source_target_pairs={{0,4},{2,6},{4,0},{6,2},{1,5},{3,7},{5,1},{7,3},{8,12},{10,14},{12... | collective-permute-start | bytes 196616 | tf_op jit(solution)/shard_map/ppermute | solution.py:31
  64.8 0.6 collective-permute-start.16
  65.4 0.0 collective-permute-done.14.lines1_ref
  65.4 3.2 %collective-permute-done.15.lines2_ref = f32[32,512]{1,0:T(8,128)S(1)} collective-permute-done((f32[32,512]{1,0:T(8,128)S(1)}, f32[32,512]{1,0:T(8,128)S(1)}, u32[]{:S(2)}, u32[]{:S(2)}) %collective-permute-start.15) | collective-permute-done | bytes 65568 | tf_op jit(solution)/shard_map/ppermute | solution.py:31
  68.6 1.7 %collective-permute-done.16.lines3_ref = f32[32,512]{1,0:T(8,128)S(1)} collective-permute-done((f32[32,512]{1,0:T(8,128)S(1)}, f32[32,512]{1,0:T(8,128)S(1)}, u32[]{:S(2)}, u32[]{:S(2)}) %collective-permute-start.16) | collective-permute-done | bytes 65568 | tf_op jit(solution)/shard_map/ppermute | solution.py:31
  70.3 0.0 all-to-all-done.squares_ref
  70.3 0.0 copy-done
  70.3 0.0 copy-done.1
  70.3 0.0 copy-done.2
  70.3 0.0 copy-done.3
  70.3 1.8 %shard_map.95 = (f32[448,1024]{1,0:T(8,128)}, f32[448,128]{1,0:T(8,128)}, f32[448,128]{1,0:T(8,128)}) custom-call(s32[1]{0:T(128)} %bitcast.x_ref, f32[64,2,128]{2,1,0:T(2,128)S(1)} %all-to-all-done.squares_ref, f32[32,512]{1,0:T(8,128)S(1)} %shard_map.94.lines0_ref, f32[32,512]{1,0:T(8,128)S(1)} %collective-permute-done.14.lines1_ref, ...), custom_call_target="tpu_custom_call" | custom-call | flops 117440512 | bytes 4194304 | tf_op jit(solution)/shard_map/pallas_call | solution.py:292
  (5 shorter events, 0.1 us)
Async XLA Ops:
  2.2 4.8 %collective-permute-start = (f32[32,256]{1,0:T(8,128)S(1)}, f32[32,256]{1,0:T(8,128)S(1)}, u32[]{:S(2)}, u32[]{:S(2)}) collective-permute-start(f32[32,256]{1,0:T(8,128)S(1)} %get-tuple-element.28), channel_id=1, source_target_pairs={{0,2},{2,0},{4,6},{6,4},{1,3},{3,1},{5,7},{7,5},{8,10},{10,8},{12,... | collective-permute-start | bytes 98312 | tf_op jit(solution)/shard_map/ppermute | solution.py:31
  3.7 5.4 %collective-permute-start.1 = (f32[32,256]{1,0:T(8,128)S(1)}, f32[32,256]{1,0:T(8,128)S(1)}, u32[]{:S(2)}, u32[]{:S(2)}) collective-permute-start(f32[32,256]{1,0:T(8,128)S(1)} %get-tuple-element.29), channel_id=1, source_target_pairs={{0,4},{2,6},{4,0},{6,2},{1,5},{3,7},{5,1},{7,3},{8,12},{10,14},{12... | collective-permute-start | bytes 98312 | tf_op jit(solution)/shard_map/ppermute | solution.py:31
  6.5 5.1 %collective-permute-start.2 = (f32[32,256]{1,0:T(8,128)S(1)}, f32[32,256]{1,0:T(8,128)S(1)}, u32[]{:S(2)}, u32[]{:S(2)}) collective-permute-start(f32[32,256]{1,0:T(8,128)S(1)} %get-tuple-element.30), channel_id=1, source_target_pairs={{0,6},{2,4},{4,2},{6,0},{1,7},{3,5},{5,3},{7,1},{8,14},{10,12},{12... | collective-permute-start | bytes 98312 | tf_op jit(solution)/shard_map/ppermute | solution.py:31
  11.6 10.5 %collective-permute-start.3 = (f32[16,256]{1,0:T(8,128)S(1)}, f32[16,256]{1,0:T(8,128)S(1)}, u32[]{:S(2)}, u32[]{:S(2)}) collective-permute-start(f32[16,256]{1,0:T(8,128)S(1)} %get-tuple-element.32), channel_id=1, source_target_pairs={{0,1},{1,0},{2,3},{3,2},{4,5},{5,4},{6,7},{7,6},{8,9},{9,8},{10,11... | collective-permute-start | bytes 49160 | tf_op jit(solution)/shard_map/ppermute | solution.py:25
  22.1 48.2 %copy-start = (bf16[1024,128]{1,0:T(8,128)(2,1)S(1)}, bf16[1024,128]{1,0:T(8,128)(2,1)}, u32[]{:S(2)}) copy-start(bf16[1024,128]{1,0:T(8,128)(2,1)} %proj_ref.1) | copy-start | bytes 786436
  22.1 48.2 %copy-start.1 = (bf16[1024,448]{0,1:T(8,128)(2,1)S(1)}, bf16[1024,448]{0,1:T(8,128)(2,1)}, u32[]{:S(2)}) copy-start(bf16[1024,448]{0,1:T(8,128)(2,1)} %param.9) | copy-start | bytes 2752516
  22.1 48.2 %copy-start.2 = (f32[128,448]{0,1:T(8,128)S(1)}, f32[128,448]{0,1:T(8,128)}, u32[]{:S(2)}) copy-start(f32[128,448]{0,1:T(8,128)} %param.10) | copy-start | bytes 688132
  22.1 48.2 %copy-start.3 = (f32[128,448]{0,1:T(8,128)S(1)}, f32[128,448]{0,1:T(8,128)}, u32[]{:S(2)}) copy-start(f32[128,448]{0,1:T(8,128)} %param.11) | copy-start | bytes 688132
  23.3 1.9 %collective-permute-start.4 = (f32[16,8,896]{2,1,0:T(8,128)S(1)}, f32[16,8,896]{2,1,0:T(8,128)S(1)}, u32[]{:S(2)}, u32[]{:S(2)}) collective-permute-start(f32[16,8,896]{2,1,0:T(8,128)S(1)} %get-tuple-element.34), channel_id=1, source_target_pairs={{0,8},{8,0},{1,9},{9,1},{2,10},{10,2},{3,11},{11,3},{4,12},{12,4},... | collective-permute-start | bytes 1376264 | tf_op jit(solution)/shard_map/ppermute | solution.py:25
  25.3 5.3 %collective-permute-start.5 = (f32[4,8,896]{2,1,0:T(8,128)S(1)}, f32[4,8,896]{2,1,0:T(8,128)S(1)}, u32[]{:S(2)}, u32[]{:S(2)}) collective-permute-start(f32[4,8,896]{2,1,0:T(8,128)S(1)} %get-tuple-element.36), channel_id=1, source_target_pairs={{0,64},{64,0},{128,192},{192,128},{1,65},{65,1},{129,193},{193,129... | collective-permute-start | bytes 344072 | tf_op jit(solution)/shard_map/ppermute | solution.py:31
  25.8 8.3 %collective-permute-start.6 = (f32[4,8,896]{2,1,0:T(8,128)S(1)}, f32[4,8,896]{2,1,0:T(8,128)S(1)}, u32[]{:S(2)}, u32[]{:S(2)}) collective-permute-start(f32[4,8,896]{2,1,0:T(8,128)S(1)} %get-tuple-element.37), channel_id=1, source_target_pairs={{0,128},{64,192},{128,0},{192,64},{1,129},{65,193},{129,1},{193,65... | collective-permute-start | bytes 344072 | tf_op jit(solution)/shard_map/ppermute | solution.py:31
  28.4 7.1 %collective-permute-start.7 = (f32[4,8,896]{2,1,0:T(8,128)S(1)}, f32[4,8,896]{2,1,0:T(8,128)S(1)}, u32[]{:S(2)}, u32[]{:S(2)}) collective-permute-start(f32[4,8,896]{2,1,0:T(8,128)S(1)} %get-tuple-element.38), channel_id=1, source_target_pairs={{0,192},{64,128},{128,64},{192,0},{1,193},{65,129},{129,65},{193,1... | collective-permute-start | bytes 344072 | tf_op jit(solution)/shard_map/ppermute | solution.py:31
  35.5 5.8 %collective-permute-start.10 = (f32[8,896]{1,0:T(8,128)S(1)}, f32[8,896]{1,0:T(8,128)S(1)}, u32[]{:S(2)}, u32[]{:S(2)}) collective-permute-start(f32[8,896]{1,0:T(8,128)S(1)} %get-tuple-element.42), channel_id=1, source_target_pairs={{0,48},{16,32},{32,16},{48,0},{1,49},{17,33},{33,17},{49,1},{2,50}... | collective-permute-start | bytes 86024 | tf_op jit(solution)/shard_map/ppermute | solution.py:31
  37.5 4.0 %collective-permute-start.8 = (f32[8,896]{1,0:T(8,128)S(1)}, f32[8,896]{1,0:T(8,128)S(1)}, u32[]{:S(2)}, u32[]{:S(2)}) collective-permute-start(f32[8,896]{1,0:T(8,128)S(1)} %get-tuple-element.40), channel_id=1, source_target_pairs={{0,16},{16,0},{32,48},{48,32},{1,17},{17,1},{33,49},{49,33},{2,18}... | collective-permute-start | bytes 86024 | tf_op jit(solution)/shard_map/ppermute | solution.py:31
  37.6 4.8 %collective-permute-start.9 = (f32[8,896]{1,0:T(8,128)S(1)}, f32[8,896]{1,0:T(8,128)S(1)}, u32[]{:S(2)}, u32[]{:S(2)}) collective-permute-start(f32[8,896]{1,0:T(8,128)S(1)} %get-tuple-element.41), channel_id=1, source_target_pairs={{0,32},{16,48},{32,0},{48,16},{1,33},{17,49},{33,1},{49,17},{2,34}... | collective-permute-start | bytes 86024 | tf_op jit(solution)/shard_map/ppermute | solution.py:31
  42.5 1.2 %collective-permute-start.11 = (f32[8,128]{1,0:T(8,128)S(1)}, f32[8,128]{1,0:T(8,128)S(1)}, u32[]{:S(2)}, u32[]{:S(2)}) collective-permute-start(f32[8,128]{1,0:T(8,128)S(1)} %get-tuple-element.44), channel_id=1, source_target_pairs={{0,8},{8,0},{1,9},{9,1},{2,10},{10,2},{3,11},{11,3},{4,12},{12,4},... | collective-permute-start | bytes 12296 | tf_op jit(solution)/shard_map/ppermute | solution.py:25
  43.7 7.8 %collective-permute-start.12 = (f32[8,1024]{1,0:T(8,128)S(1)}, f32[8,1024]{1,0:T(8,128)S(1)}, u32[]{:S(2)}, u32[]{:S(2)}) collective-permute-start(f32[8,1024]{1,0:T(8,128)S(1)} %shard_map.92.keep_ref), channel_id=1, source_target_pairs={{0,1},{1,0},{2,3},{3,2},{4,5},{5,4},{6,7},{7,6},{8,9},{9,8},{10,11... | collective-permute-start | bytes 98312 | tf_op jit(solution)/shard_map/ppermute | solution.py:25
  52.2 18.1 %all-to-all-start = ((f32[64,2,128]{2,1,0:T(2,128)}), f32[64,2,128]{2,1,0:T(2,128)S(1)}, u32[]{:S(2)}, u32[]{:S(2)}) async-start(f32[64,2,128]{2,1,0:T(2,128)} %get-tuple-element.45), calls=%async_computation | async-start | bytes 131072 | tf_op jit(solution)/shard_map/all_to_all | solution.py:286
  59.3 1.3 %collective-permute-start.13 = (f32[16,512]{1,0:T(8,128)S(1)}, f32[16,512]{1,0:T(8,128)S(1)}, u32[]{:S(2)}, u32[]{:S(2)}) collective-permute-start(f32[16,512]{1,0:T(8,128)S(1)} %get-tuple-element.47), channel_id=1, source_target_pairs={{0,8},{8,0},{1,9},{9,1},{2,10},{10,2},{3,11},{11,3},{4,12},{12,4},... | collective-permute-start | bytes 98312 | tf_op jit(solution)/shard_map/ppermute | solution.py:25
  60.6 4.8 %collective-permute-start.14 = (f32[32,512]{1,0:T(8,128)S(1)}, f32[32,512]{1,0:T(8,128)S(1)}, u32[]{:S(2)}, u32[]{:S(2)}) collective-permute-start(f32[32,512]{1,0:T(8,128)S(1)} %shard_map.94.lines0_ref), channel_id=1, source_target_pairs={{0,2},{2,0},{4,6},{6,4},{1,3},{3,1},{5,7},{7,5},{8,10},{10,8},{12,... | collective-permute-start | bytes 196616 | tf_op jit(solution)/shard_map/ppermute | solution.py:31
  62.2 6.4 %collective-permute-start.15 = (f32[32,512]{1,0:T(8,128)S(1)}, f32[32,512]{1,0:T(8,128)S(1)}, u32[]{:S(2)}, u32[]{:S(2)}) collective-permute-start(f32[32,512]{1,0:T(8,128)S(1)} %shard_map.94.lines0_ref), channel_id=1, source_target_pairs={{0,4},{2,6},{4,0},{6,2},{1,5},{3,7},{5,1},{7,3},{8,12},{10,14},{12... | collective-permute-start | bytes 196616 | tf_op jit(solution)/shard_map/ppermute | solution.py:31
  64.8 5.5 %collective-permute-start.16 = (f32[32,512]{1,0:T(8,128)S(1)}, f32[32,512]{1,0:T(8,128)S(1)}, u32[]{:S(2)}, u32[]{:S(2)}) collective-permute-start(f32[32,512]{1,0:T(8,128)S(1)} %shard_map.94.lines0_ref), channel_id=1, source_target_pairs={{0,6},{2,4},{4,2},{6,0},{1,7},{3,5},{5,3},{7,1},{8,14},{10,12},{12... | collective-permute-start | bytes 196616 | tf_op jit(solution)/shard_map/ppermute | solution.py:31

commit v4 on v3

--- a/solution.py
+++ b/solution.py
@@ -17,6 +17,7 @@
 SMEM = pl.BlockSpec(memory_space=pltpu.SMEM)
 HBM = pl.BlockSpec(memory_space=pl.ANY)
 LIMIT = 6 << 20
+ORDER = (3, 2, 1, 0)
 F32 = jnp.float32
 BF16 = jnp.bfloat16
 
@@ -26,10 +27,9 @@
 
 
 def trade(values, axis):
-    out = [values[0]]
-    for k in (1, 2, 3):
-        out.append(lax.ppermute(values[k], axis, [(i, i ^ k) for i in range(4)]))
-    return out
+    return [lax.ppermute(values[k], axis, [(i, i ^ k) for i in range(4)]) for k in ORDER[:3]] + [
+        values[0]
+    ]
 
 
 def in_hbm(value):
@@ -88,8 +88,7 @@
 def split_body(zh_ref, *refs):
     ins, (keep_ref, give_ref) = refs[:4], refs[4:]
     y = total_of(ins)
-    low = jnp.concatenate([y[0:8], y[16:24]])
-    high = jnp.concatenate([y[8:16], y[24:32]])
+    low, high = y[:16], y[16:]
     is_first = zh_ref[0] == 0
     keep_ref[...] = jnp.where(is_first, low, high)
     give_ref[...] = jnp.where(is_first, high, low)
@@ -130,43 +129,40 @@
         outs[k][...] = ins[0][at] + ins[1][at] + ins[2][at] + ins[3][at]
 
 
-def squares_body(*refs):
-    ins, (done_ref, line_ref) = refs[:-2], refs[-2:]
-    done = total_of(ins)
-    width = done.shape[1]
+def reduce_body(cols, c_ref, *refs):
+    ins, (keep_ref, give_ref) = refs[:-2], refs[-2:]
+    if len(ins) == 1:
+        parts_ref = ins[0]
+        done = []
+        for zh in range(2):
+            plane = parts_ref[4 * zh]
+            for zl in range(1, 4):
+                plane = plane + parts_ref[4 * zh + zl]
+            done.append(plane)
+        done = jnp.concatenate(done)
+    else:
+        done = total_of(ins)
     squares = jnp.sum(jnp.sum(done * done, axis=0, keepdims=True), axis=1, keepdims=True)
-    done_ref[:, :width] = done
-    done_ref[:, width:] = jnp.broadcast_to(squares, done_ref[:, width:].shape)
-    line_ref[...] = jnp.broadcast_to(squares, line_ref.shape)
-
-
-def both_cores_body(done_ref, line_ref, out_ref):
-    width = out_ref.shape[1] - 128
-    out_ref[:, :width] = done_ref[:, :width]
-    out_ref[:, width:] = done_ref[:, width:] + line_ref[0:1, :]
-
-
-def by_column_body(cols, zh_ref, c_ref, keep_ref, got_ref, squares_ref, own_ref, give_ref):
+    wide = keep_ref.shape[1]
+    left = done[:, :wide]
+    right = pltpu.roll(done, cols, 1)[:, :wide]
+    is_first = c_ref[0] == 0
+    lane = lax.broadcasted_iota(jnp.int32, left.shape, 1)
+    keep_ref[...] = jnp.where(lane < cols, jnp.where(is_first, left, right), squares)
+    give_ref[...] = jnp.where(lane < cols, jnp.where(is_first, right, left), squares)
+
+
+def pair_body(cols, me_ref, keep_ref, got_ref, *outs):
     keep, got = keep_ref[...], got_ref[...]
-    width = keep.shape[1] - 128
-    is_first = zh_ref[0] == 0
-    rows = jnp.concatenate([jnp.where(is_first, keep, got), jnp.where(is_first, got, keep)])
-    squares_ref[...] = jnp.broadcast_to(
-        keep[0:1, width:] + got[0:1, width:], squares_ref.shape
-    )
-    wide = own_ref.shape[1]
-    left = rows[:, :wide]
-    right = pltpu.roll(rows[:, :width], cols, 1)[:, :wide]
-    is_first = c_ref[0] == 0
-    own_ref[...] = jnp.where(is_first, left, right)
-    give_ref[...] = jnp.where(is_first, right, left)
-
-
-def by_core_body(c_ref, keep_ref, got_ref, out_ref):
-    keep, got = keep_ref[...], got_ref[...]
-    is_first = c_ref[0] == 0
-    out_ref[:16] = jnp.where(is_first, keep, got)
-    out_ref[16:] = jnp.where(is_first, got, keep)
+    is_first = me_ref[0] == 0
+    half = keep.shape[0]
+    both = keep + got
+    lane = lax.broadcasted_iota(jnp.int32, keep.shape, 1)
+    outs[0][:half] = jnp.where(lane < cols, jnp.where(is_first, keep, got), both)
+    outs[0][half:] = jnp.where(lane < cols, jnp.where(is_first, got, keep), both)
+    if len(outs) == 2:
+        line = both[0:1, both.shape[1] - 1 :]
+        outs[1][...] = jnp.broadcast_to(line, outs[1].shape)
 
 
 def last_body(
@@ -191,7 +187,7 @@
     new_second_ref,
     sems,
 ):
-    for k, ref in enumerate((lines0_ref, lines1_ref, lines2_ref, lines3_ref)):
+    for k, ref in zip(ORDER, (lines0_ref, lines1_ref, lines2_ref, lines3_ref)):
         begin = pl.multiple_of((x_ref[0] ^ k) * 32, 32)
         rows_ref[pl.ds(begin, 32), :] = ref[...]
     turned_ref[...] = rows_ref[...].T
@@ -275,17 +271,22 @@
     parts = trade(parts, "y")
     parts = run(by_zl_body, [(8, width)] * 4, [SMEM] + [VMEM] * 4, (me_zl, *parts))
     parts = trade(parts, "zl")
-    done, line = run(squares_body, [(8, width + 128), (8, 128)], [VMEM] * 4, tuple(parts))
-    done = run(both_cores_body, (8, width + 128), [VMEM] * 2, (done, swap(line, "c")))
-    squares, keep, give = run(
-        functools.partial(by_column_body, cols),
-        [(64, 2, 128), (16, wide), (16, wide)],
-        [SMEM, SMEM, VMEM, VMEM],
-        (me_zh, me_c, done, swap(done, "zh")),
+    pair = functools.partial(pair_body, cols)
+    keep, give = run(
+        functools.partial(reduce_body, cols),
+        [(8, wide)] * 2,
+        [SMEM] + [VMEM] * 4,
+        (me_c, *parts),
+    )
+    keep = run(pair, (16, wide), [SMEM, VMEM, VMEM], (me_c, keep, swap(give, "c")))
+    line, squares = run(
+        pair,
+        [(32, wide), (64, 2, 128)],
+        [SMEM, VMEM, VMEM],
+        (me_zh, keep, swap(keep, "zh")),
     )
     squares = lax.all_to_all(squares, ("y", "zl", "x"), 0, 0, tiled=True)
-    lines = run(by_core_body, (32, wide), [SMEM, VMEM, VMEM], (me_c, keep, swap(give, "c")))
-    lines = trade([lines] * 4, "x")
+    lines = trade([line] * 4, "x")
 
     steps = 4
     outs = [(cols, rows), (cols, rank), (cols, rank)]

time: 72.4 us -> 71.1 us (0.982)
  waiting for transfers between devices: 26.2 us -> 25.2 us
    ppermute x12, starting transfers between devices: 17.6 us -> 16.1 us  [trade(): lax.ppermute(values[k], axis, [(i, i ^ k) for i in range(4)])]
    ppermute x5 -> x4, waiting for transfers between devices: 7.58 us -> 6.4 us  [swap(): return lax.ppermute(value, axis, [(0, 1), (1, 0)])]
    all_to_all x1, starting transfers between devices: 7.12 us -> 8.24 us  [per_device(): squares = lax.all_to_all(squares, ('y', 'zl', 'x'), 0, 0, tiled=True)]
    all_to_all x1, waiting for transfers between devices: 0.01 us -> 0.78 us  [per_device(): squares = lax.all_to_all(squares, ('y', 'zl', 'x'), 0, 0, tiled=True)]
    pallas_call x10 -> x9, Pallas kernels: 6.72 us -> 6.8 us  [run(): pl.pallas_call(body, in_specs=specs, out_shape=made[0] if single else tup...]
    ppermute x5 -> x4, starting transfers between devices: 11.9 us -> 11.9 us  [swap(): return lax.ppermute(value, axis, [(0, 1), (1, 0)])]
  transfers between devices with their start and end apart: 18 -> 17, of which waited for: 14 -> 14; matrix products, arithmetic and copies ran while one was open for 0% -> 0% of each run, Pallas kernels for 4% -> 4%
where the time goes in v4:
time: 71.1 us; the launch traced here: 70.9 us
  starting transfers between devices  36.3 us (51%)
  waiting for transfers between devices  25.2 us (35%)
  Pallas kernels  8.61 us (12%)
  between operations  0.77 us (1%)
    ppermute x12, waiting for transfers between devices, trade(): lax.ppermute(values[k], axis, [(i, i ^ k) for i in range(4)])  18 us
    ppermute x12, starting transfers between devices, trade(): lax.ppermute(values[k], axis, [(i, i ^ k) for i in range(4)])  16.1 us
    ppermute x4, starting transfers between devices, swap(): return lax.ppermute(value, axis, [(0, 1), (1, 0)])  11.9 us
    all_to_all x1, starting transfers between devices, per_device(): squares = lax.all_to_all(squares, ('y', 'zl', 'x'), 0, 0, tiled=True)  8.24 us
    pallas_call x9, Pallas kernels, run(): pl.pallas_call(body, in_specs=specs, out_shape=made[0] if single else tup...  6.8 us
    ppermute x4, waiting for transfers between devices, swap(): return lax.ppermute(value, axis, [(0, 1), (1, 0)])  6.4 us
    pallas_call x1, Pallas kernels, per_device(): pl.pallas_call(functools.partial(last_body, steps), in_specs=[SMEM] + [VM...  1.82 us
  transfers between devices with their start and end apart: 17, of which 14 were waited for; matrix products, arithmetic and copies ran while one was open for 0% of the time, Pallas kernels for 4%

profile of v4, /device:TPU:8, one launch (start us, length us, event | category | flops | bytes accessed | tf_op | source)
XLA Modules:
  0.0 70.9 jit_solution(5649436458424425338)
XLA Ops:
  0.6 1.5 %shard_map.85 = (f32[32,256]{1,0:T(8,128)S(1)}, f32[32,256]{1,0:T(8,128)S(1)}, f32[32,256]{1,0:T(8,128)S(1)}, f32[32,256]{1,0:T(8,128)S(1)}) custom-call(s32[1]{0:T(128)} %bitcast.x_ref, bf16[256,1024]{1,0:T(8,128)(2,1)} %bitcast.17, bf16[1024,128]{1,0:T(8,128)(2,1)} %proj_ref.1), custom_call_target="tpu_custom_call" | custom-call | bytes 1048576 | tf_op jit(solution)/shard_map/pallas_call | solution.py:44
  2.2 2.9 %collective-permute-start = (f32[32,256]{1,0:T(8,128)S(1)}, f32[32,256]{1,0:T(8,128)S(1)}, u32[]{:S(2)}, u32[]{:S(2)}) collective-permute-start(f32[32,256]{1,0:T(8,128)S(1)} %get-tuple-element.26), channel_id=1, source_target_pairs={{0,6},{2,4},{4,2},{6,0},{1,7},{3,5},{5,3},{7,1},{8,14},{10,12},{12... | collective-permute-start | bytes 98312 | tf_op jit(solution)/shard_map/ppermute | solution.py:30
  5.0 0.8 %collective-permute-start.1 = (f32[32,256]{1,0:T(8,128)S(1)}, f32[32,256]{1,0:T(8,128)S(1)}, u32[]{:S(2)}, u32[]{:S(2)}) collective-permute-start(f32[32,256]{1,0:T(8,128)S(1)} %get-tuple-element.27), channel_id=1, source_target_pairs={{0,4},{2,6},{4,0},{6,2},{1,5},{3,7},{5,1},{7,3},{8,12},{10,14},{12... | collective-permute-start | bytes 98312 | tf_op jit(solution)/shard_map/ppermute | solution.py:30
  5.8 0.5 collective-permute-start.2
  6.3 1.0 %collective-permute-done.refs_0_ = f32[32,256]{1,0:T(8,128)S(1)} collective-permute-done((f32[32,256]{1,0:T(8,128)S(1)}, f32[32,256]{1,0:T(8,128)S(1)}, u32[]{:S(2)}, u32[]{:S(2)}) %collective-permute-start) | collective-permute-done | bytes 32800 | tf_op jit(solution)/shard_map/ppermute | solution.py:30
  7.4 3.1 %collective-permute-done.1.refs_1_ = f32[32,256]{1,0:T(8,128)S(1)} collective-permute-done((f32[32,256]{1,0:T(8,128)S(1)}, f32[32,256]{1,0:T(8,128)S(1)}, u32[]{:S(2)}, u32[]{:S(2)}) %collective-permute-start.1) | collective-permute-done | bytes 32800 | tf_op jit(solution)/shard_map/ppermute | solution.py:30
  10.4 0.0 collective-permute-done.2.refs_2_
  10.4 7.3 %collective-permute-start.3 = (f32[16,256]{1,0:T(8,128)S(1)}, f32[16,256]{1,0:T(8,128)S(1)}, u32[]{:S(2)}, u32[]{:S(2)}) collective-permute-start(f32[16,256]{1,0:T(8,128)S(1)} %get-tuple-element.31), channel_id=1, source_target_pairs={{0,1},{1,0},{2,3},{3,2},{4,5},{5,4},{6,7},{7,6},{8,9},{9,8},{10,11... | collective-permute-start | bytes 49160 | tf_op jit(solution)/shard_map/ppermute | solution.py:26
  17.7 3.2 %shard_map.87.og_ref = bf16[256,14336]{1,0:T(8,128)(2,1)S(1)} custom-call(bf16[256,14336]{1,0:T(8,128)(2,1)} %bitcast.16, f32[16,256]{1,0:T(8,128)S(1)} %get-tuple-element.30.after_ref.one_ref), custom_call_target="tpu_custom_call" | custom-call | bytes 16777216 | tf_op jit(solution)/shard_map/pallas_call | solution.py:44
  20.9 0.0 copy-start
  20.9 0.0 copy-start.1
  20.9 0.0 copy-start.2
  20.9 0.0 copy-start.3
  21.0 0.0 collective-permute-done.3.two_ref
  21.0 1.2 %shard_map.88 = (f32[16,8,896]{2,1,0:T(8,128)S(1)}, f32[16,8,896]{2,1,0:T(8,128)S(1)}) custom-call(s32[1]{0:T(128)} %bitcast.2.c_ref.me_ref, f32[16,256]{1,0:T(8,128)S(1)} %get-tuple-element.30.after_ref.one_ref, f32[16,256]{1,0:T(8,128)S(1)} %collective-permute-done.3.two_ref, bf16[256,14336]{1,0:T(8,128)(2,1)S(1)} %shard_map.87.og_ref), custom_call_target="tpu_custom_call" | custom-call | flops 234881024 | bytes 8388608 | tf_op jit(solution)/shard_map/pallas_call | solution.py:44
  22.2 0.1 collective-permute-start.4
  22.3 1.8 %collective-permute-done.4.b_ref = f32[16,8,896]{2,1,0:T(8,128)S(1)} collective-permute-done((f32[16,8,896]{2,1,0:T(8,128)S(1)}, f32[16,8,896]{2,1,0:T(8,128)S(1)}, u32[]{:S(2)}, u32[]{:S(2)}) %collective-permute-start.4) | collective-permute-done | bytes 458784 | tf_op jit(solution)/shard_map/ppermute | solution.py:26
  24.1 1.7 %collective-permute-start.5 = (f32[4,8,896]{2,1,0:T(8,128)S(1)}, f32[4,8,896]{2,1,0:T(8,128)S(1)}, u32[]{:S(2)}, u32[]{:S(2)}) collective-permute-start(f32[4,8,896]{2,1,0:T(8,128)S(1)} %get-tuple-element.34), channel_id=1, source_target_pairs={{0,192},{64,128},{128,64},{192,0},{1,193},{65,129},{129,65},{193,1... | collective-permute-start | bytes 344072 | tf_op jit(solution)/shard_map/ppermute | solution.py:30
  25.8 0.9 %collective-permute-start.6 = (f32[4,8,896]{2,1,0:T(8,128)S(1)}, f32[4,8,896]{2,1,0:T(8,128)S(1)}, u32[]{:S(2)}, u32[]{:S(2)}) collective-permute-start(f32[4,8,896]{2,1,0:T(8,128)S(1)} %get-tuple-element.35), channel_id=1, source_target_pairs={{0,128},{64,192},{128,0},{192,64},{1,129},{65,193},{129,1},{193,65... | collective-permute-start | bytes 344072 | tf_op jit(solution)/shard_map/ppermute | solution.py:30
  26.7 1.6 %collective-permute-start.7 = (f32[4,8,896]{2,1,0:T(8,128)S(1)}, f32[4,8,896]{2,1,0:T(8,128)S(1)}, u32[]{:S(2)}, u32[]{:S(2)}) collective-permute-start(f32[4,8,896]{2,1,0:T(8,128)S(1)} %get-tuple-element.36), channel_id=1, source_target_pairs={{0,64},{64,0},{128,192},{192,128},{1,65},{65,1},{129,193},{193,129... | collective-permute-start | bytes 344072 | tf_op jit(solution)/shard_map/ppermute | solution.py:30
  28.3 2.2 %collective-permute-done.5.refs_0_ = f32[4,8,896]{2,1,0:T(8,128)S(1)} collective-permute-done((f32[4,8,896]{2,1,0:T(8,128)S(1)}, f32[4,8,896]{2,1,0:T(8,128)S(1)}, u32[]{:S(2)}, u32[]{:S(2)}) %collective-permute-start.5) | collective-permute-done | bytes 114720 | tf_op jit(solution)/shard_map/ppermute | solution.py:30
  30.4 2.9 %collective-permute-done.6.refs_1_ = f32[4,8,896]{2,1,0:T(8,128)S(1)} collective-permute-done((f32[4,8,896]{2,1,0:T(8,128)S(1)}, f32[4,8,896]{2,1,0:T(8,128)S(1)}, u32[]{:S(2)}, u32[]{:S(2)}) %collective-permute-start.6) | collective-permute-done | bytes 114720 | tf_op jit(solution)/shard_map/ppermute | solution.py:30
  33.3 0.4 collective-permute-done.7.refs_2_
  33.7 1.1 %collective-permute-start.10 = (f32[8,896]{1,0:T(8,128)S(1)}, f32[8,896]{1,0:T(8,128)S(1)}, u32[]{:S(2)}, u32[]{:S(2)}) collective-permute-start(f32[8,896]{1,0:T(8,128)S(1)} %get-tuple-element.40), channel_id=1, source_target_pairs={{0,16},{16,0},{32,48},{48,32},{1,17},{17,1},{33,49},{49,33},{2,18}... | collective-permute-start | bytes 86024 | tf_op jit(solution)/shard_map/ppermute | solution.py:30
  34.8 1.9 %collective-permute-start.8 = (f32[8,896]{1,0:T(8,128)S(1)}, f32[8,896]{1,0:T(8,128)S(1)}, u32[]{:S(2)}, u32[]{:S(2)}) collective-permute-start(f32[8,896]{1,0:T(8,128)S(1)} %get-tuple-element.38), channel_id=1, source_target_pairs={{0,48},{16,32},{32,16},{48,0},{1,49},{17,33},{33,17},{49,1},{2,50}... | collective-permute-start | bytes 86024 | tf_op jit(solution)/shard_map/ppermute | solution.py:30
  36.7 0.6 collective-permute-start.9
  37.3 0.4 collective-permute-done.10.refs_2_
  37.7 2.8 %collective-permute-done.8.refs_0_ = f32[8,896]{1,0:T(8,128)S(1)} collective-permute-done((f32[8,896]{1,0:T(8,128)S(1)}, f32[8,896]{1,0:T(8,128)S(1)}, u32[]{:S(2)}, u32[]{:S(2)}) %collective-permute-start.8) | collective-permute-done | bytes 28704 | tf_op jit(solution)/shard_map/ppermute | solution.py:30
  40.5 1.0 %collective-permute-done.9.refs_1_ = f32[8,896]{1,0:T(8,128)S(1)} collective-permute-done((f32[8,896]{1,0:T(8,128)S(1)}, f32[8,896]{1,0:T(8,128)S(1)}, u32[]{:S(2)}, u32[]{:S(2)}) %collective-permute-start.9) | collective-permute-done | bytes 28704 | tf_op jit(solution)/shard_map/ppermute | solution.py:30
  41.5 0.1 shard_map.91
  41.6 0.1 collective-permute-start.11
  41.7 1.2 %collective-permute-done.11.got_ref = f32[8,512]{1,0:T(8,128)S(1)} collective-permute-done((f32[8,512]{1,0:T(8,128)S(1)}, f32[8,512]{1,0:T(8,128)S(1)}, u32[]{:S(2)}, u32[]{:S(2)}) %collective-permute-start.11) | collective-permute-done | bytes 16416 | tf_op jit(solution)/shard_map/ppermute | solution.py:26
  42.9 4.5 %collective-permute-start.12 = (f32[16,512]{1,0:T(8,128)S(1)}, f32[16,512]{1,0:T(8,128)S(1)}, u32[]{:S(2)}, u32[]{:S(2)}) collective-permute-start(f32[16,512]{1,0:T(8,128)S(1)} %shard_map.92.keep_ref), channel_id=1, source_target_pairs={{0,1},{1,0},{2,3},{3,2},{4,5},{5,4},{6,7},{7,6},{8,9},{9,8},{10,11... | collective-permute-start | bytes 98312 | tf_op jit(solution)/shard_map/ppermute | solution.py:26
  47.3 3.4 %collective-permute-done.12.got_ref = f32[16,512]{1,0:T(8,128)S(1)} collective-permute-done((f32[16,512]{1,0:T(8,128)S(1)}, f32[16,512]{1,0:T(8,128)S(1)}, u32[]{:S(2)}, u32[]{:S(2)}) %collective-permute-start.12) | collective-permute-done | bytes 32800 | tf_op jit(solution)/shard_map/ppermute | solution.py:26
  50.8 0.8 %shard_map.93 = (f32[32,512]{1,0:T(8,128)S(1)}, f32[64,2,128]{2,1,0:T(2,128)}) custom-call(s32[1]{0:T(128)} %bitcast.1.zh_ref.me_ref, f32[16,512]{1,0:T(8,128)S(1)} %shard_map.92.keep_ref, f32[16,512]{1,0:T(8,128)S(1)} %collective-permute-done.12.got_ref), custom_call_target="tpu_custom_call" | custom-call | bytes 1048576 | tf_op jit(solution)/shard_map/pallas_call | solution.py:44
  51.5 8.2 %all-to-all-start = ((f32[64,2,128]{2,1,0:T(2,128)}), f32[64,2,128]{2,1,0:T(2,128)S(1)}, u32[]{:S(2)}, u32[]{:S(2)}) async-start(f32[64,2,128]{2,1,0:T(2,128)} %get-tuple-element.44), calls=%async_computation | async-start | bytes 131072 | tf_op jit(solution)/shard_map/all_to_all | solution.py:288
  59.8 2.8 %collective-permute-start.13 = (f32[32,512]{1,0:T(8,128)S(1)}, f32[32,512]{1,0:T(8,128)S(1)}, u32[]{:S(2)}, u32[]{:S(2)}) collective-permute-start(f32[32,512]{1,0:T(8,128)S(1)} %get-tuple-element.45.lines3_ref), channel_id=1, source_target_pairs={{0,6},{2,4},{4,2},{6,0},{1,7},{3,5},{5,3},{7,1},{8,14},{10,12},{12... | collective-permute-start | bytes 196616 | tf_op jit(solution)/shard_map/ppermute | solution.py:30
  62.5 0.9 %collective-permute-start.14 = (f32[32,512]{1,0:T(8,128)S(1)}, f32[32,512]{1,0:T(8,128)S(1)}, u32[]{:S(2)}, u32[]{:S(2)}) collective-permute-start(f32[32,512]{1,0:T(8,128)S(1)} %get-tuple-element.45.lines3_ref), channel_id=1, source_target_pairs={{0,4},{2,6},{4,0},{6,2},{1,5},{3,7},{5,1},{7,3},{8,12},{10,14},{12... | collective-permute-start | bytes 196616 | tf_op jit(solution)/shard_map/ppermute | solution.py:30
  63.4 0.6 collective-permute-start.15
  64.0 2.3 %collective-permute-done.13.lines0_ref = f32[32,512]{1,0:T(8,128)S(1)} collective-permute-done((f32[32,512]{1,0:T(8,128)S(1)}, f32[32,512]{1,0:T(8,128)S(1)}, u32[]{:S(2)}, u32[]{:S(2)}) %collective-permute-start.13) | collective-permute-done | bytes 65568 | tf_op jit(solution)/shard_map/ppermute | solution.py:30
  66.3 2.0 %collective-permute-done.14.lines1_ref = f32[32,512]{1,0:T(8,128)S(1)} collective-permute-done((f32[32,512]{1,0:T(8,128)S(1)}, f32[32,512]{1,0:T(8,128)S(1)}, u32[]{:S(2)}, u32[]{:S(2)}) %collective-permute-start.14) | collective-permute-done | bytes 65568 | tf_op jit(solution)/shard_map/ppermute | solution.py:30
  68.3 0.0 collective-permute-done.15.lines2_ref
  68.3 0.8 %all-to-all-done.squares_ref = f32[64,2,128]{2,1,0:T(2,128)S(1)} async-done(((f32[64,2,128]{2,1,0:T(2,128)}), f32[64,2,128]{2,1,0:T(2,128)S(1)}, u32[]{:S(2)}, u32[]{:S(2)}) %all-to-all-start) | async-done | bytes 65568 | tf_op jit(solution)/shard_map/all_to_all | solution.py:288
  69.1 0.0 copy-done
  69.1 0.0 copy-done.1
  69.1 0.0 copy-done.2
  69.1 0.0 copy-done.3
  69.1 1.8 %shard_map.94 = (f32[448,1024]{1,0:T(8,128)}, f32[448,128]{1,0:T(8,128)}, f32[448,128]{1,0:T(8,128)}) custom-call(s32[1]{0:T(128)} %bitcast.x_ref, f32[64,2,128]{2,1,0:T(2,128)S(1)} %all-to-all-done.squares_ref, f32[32,512]{1,0:T(8,128)S(1)} %collective-permute-done.13.lines0_ref, f32[32,512]{1,0:T(8,128)S(1)} %collective-permute-done.14.lines1_ref, ...), custom_call_target="tpu_custom_call" | custom-call | flops 117440512 | bytes 4194304 | tf_op jit(solution)/shard_map/pallas_call | solution.py:293
  (4 shorter events, 0.1 us)
Async XLA Ops:
  2.2 5.2 %collective-permute-start = (f32[32,256]{1,0:T(8,128)S(1)}, f32[32,256]{1,0:T(8,128)S(1)}, u32[]{:S(2)}, u32[]{:S(2)}) collective-permute-start(f32[32,256]{1,0:T(8,128)S(1)} %get-tuple-element.26), channel_id=1, source_target_pairs={{0,6},{2,4},{4,2},{6,0},{1,7},{3,5},{5,3},{7,1},{8,14},{10,12},{12... | collective-permute-start | bytes 98312 | tf_op jit(solution)/shard_map/ppermute | solution.py:30
  5.0 5.4 %collective-permute-start.1 = (f32[32,256]{1,0:T(8,128)S(1)}, f32[32,256]{1,0:T(8,128)S(1)}, u32[]{:S(2)}, u32[]{:S(2)}) collective-permute-start(f32[32,256]{1,0:T(8,128)S(1)} %get-tuple-element.27), channel_id=1, source_target_pairs={{0,4},{2,6},{4,0},{6,2},{1,5},{3,7},{5,1},{7,3},{8,12},{10,14},{12... | collective-permute-start | bytes 98312 | tf_op jit(solution)/shard_map/ppermute | solution.py:30
  5.8 4.6 %collective-permute-start.2 = (f32[32,256]{1,0:T(8,128)S(1)}, f32[32,256]{1,0:T(8,128)S(1)}, u32[]{:S(2)}, u32[]{:S(2)}) collective-permute-start(f32[32,256]{1,0:T(8,128)S(1)} %get-tuple-element.28), channel_id=1, source_target_pairs={{0,2},{2,0},{4,6},{6,4},{1,3},{3,1},{5,7},{7,5},{8,10},{10,8},{12,... | collective-permute-start | bytes 98312 | tf_op jit(solution)/shard_map/ppermute | solution.py:30
  10.4 10.5 %collective-permute-start.3 = (f32[16,256]{1,0:T(8,128)S(1)}, f32[16,256]{1,0:T(8,128)S(1)}, u32[]{:S(2)}, u32[]{:S(2)}) collective-permute-start(f32[16,256]{1,0:T(8,128)S(1)} %get-tuple-element.31), channel_id=1, source_target_pairs={{0,1},{1,0},{2,3},{3,2},{4,5},{5,4},{6,7},{7,6},{8,9},{9,8},{10,11... | collective-permute-start | bytes 49160 | tf_op jit(solution)/shard_map/ppermute | solution.py:26
  20.9 48.2 %copy-start = (bf16[1024,128]{1,0:T(8,128)(2,1)S(1)}, bf16[1024,128]{1,0:T(8,128)(2,1)}, u32[]{:S(2)}) copy-start(bf16[1024,128]{1,0:T(8,128)(2,1)} %proj_ref.1) | copy-start | bytes 786436
  20.9 48.2 %copy-start.1 = (bf16[1024,448]{0,1:T(8,128)(2,1)S(1)}, bf16[1024,448]{0,1:T(8,128)(2,1)}, u32[]{:S(2)}) copy-start(bf16[1024,448]{0,1:T(8,128)(2,1)} %param.9) | copy-start | bytes 2752516
  20.9 48.2 %copy-start.2 = (f32[128,448]{0,1:T(8,128)S(1)}, f32[128,448]{0,1:T(8,128)}, u32[]{:S(2)}) copy-start(f32[128,448]{0,1:T(8,128)} %param.10) | copy-start | bytes 688132
  20.9 48.2 %copy-start.3 = (f32[128,448]{0,1:T(8,128)S(1)}, f32[128,448]{0,1:T(8,128)}, u32[]{:S(2)}) copy-start(f32[128,448]{0,1:T(8,128)} %param.11) | copy-start | bytes 688132
  22.2 1.9 %collective-permute-start.4 = (f32[16,8,896]{2,1,0:T(8,128)S(1)}, f32[16,8,896]{2,1,0:T(8,128)S(1)}, u32[]{:S(2)}, u32[]{:S(2)}) collective-permute-start(f32[16,8,896]{2,1,0:T(8,128)S(1)} %get-tuple-element.33), channel_id=1, source_target_pairs={{0,8},{8,0},{1,9},{9,1},{2,10},{10,2},{3,11},{11,3},{4,12},{12,4},... | collective-permute-start | bytes 1376264 | tf_op jit(solution)/shard_map/ppermute | solution.py:26
  24.1 6.3 %collective-permute-start.5 = (f32[4,8,896]{2,1,0:T(8,128)S(1)}, f32[4,8,896]{2,1,0:T(8,128)S(1)}, u32[]{:S(2)}, u32[]{:S(2)}) collective-permute-start(f32[4,8,896]{2,1,0:T(8,128)S(1)} %get-tuple-element.34), channel_id=1, source_target_pairs={{0,192},{64,128},{128,64},{192,0},{1,193},{65,129},{129,65},{193,1... | collective-permute-start | bytes 344072 | tf_op jit(solution)/shard_map/ppermute | solution.py:30
  25.8 7.5 %collective-permute-start.6 = (f32[4,8,896]{2,1,0:T(8,128)S(1)}, f32[4,8,896]{2,1,0:T(8,128)S(1)}, u32[]{:S(2)}, u32[]{:S(2)}) collective-permute-start(f32[4,8,896]{2,1,0:T(8,128)S(1)} %get-tuple-element.35), channel_id=1, source_target_pairs={{0,128},{64,192},{128,0},{192,64},{1,129},{65,193},{129,1},{193,65... | collective-permute-start | bytes 344072 | tf_op jit(solution)/shard_map/ppermute | solution.py:30
  26.7 7.0 %collective-permute-start.7 = (f32[4,8,896]{2,1,0:T(8,128)S(1)}, f32[4,8,896]{2,1,0:T(8,128)S(1)}, u32[]{:S(2)}, u32[]{:S(2)}) collective-permute-start(f32[4,8,896]{2,1,0:T(8,128)S(1)} %get-tuple-element.36), channel_id=1, source_target_pairs={{0,64},{64,0},{128,192},{192,128},{1,65},{65,1},{129,193},{193,129... | collective-permute-start | bytes 344072 | tf_op jit(solution)/shard_map/ppermute | solution.py:30
  33.7 4.0 %collective-permute-start.10 = (f32[8,896]{1,0:T(8,128)S(1)}, f32[8,896]{1,0:T(8,128)S(1)}, u32[]{:S(2)}, u32[]{:S(2)}) collective-permute-start(f32[8,896]{1,0:T(8,128)S(1)} %get-tuple-element.40), channel_id=1, source_target_pairs={{0,16},{16,0},{32,48},{48,32},{1,17},{17,1},{33,49},{49,33},{2,18}... | collective-permute-start | bytes 86024 | tf_op jit(solution)/shard_map/ppermute | solution.py:30
  34.8 5.7 %collective-permute-start.8 = (f32[8,896]{1,0:T(8,128)S(1)}, f32[8,896]{1,0:T(8,128)S(1)}, u32[]{:S(2)}, u32[]{:S(2)}) collective-permute-start(f32[8,896]{1,0:T(8,128)S(1)} %get-tuple-element.38), channel_id=1, source_target_pairs={{0,48},{16,32},{32,16},{48,0},{1,49},{17,33},{33,17},{49,1},{2,50}... | collective-permute-start | bytes 86024 | tf_op jit(solution)/shard_map/ppermute | solution.py:30
  36.7 4.8 %collective-permute-start.9 = (f32[8,896]{1,0:T(8,128)S(1)}, f32[8,896]{1,0:T(8,128)S(1)}, u32[]{:S(2)}, u32[]{:S(2)}) collective-permute-start(f32[8,896]{1,0:T(8,128)S(1)} %get-tuple-element.39), channel_id=1, source_target_pairs={{0,32},{16,48},{32,0},{48,16},{1,33},{17,49},{33,1},{49,17},{2,34}... | collective-permute-start | bytes 86024 | tf_op jit(solution)/shard_map/ppermute | solution.py:30
  41.6 1.3 %collective-permute-start.11 = (f32[8,512]{1,0:T(8,128)S(1)}, f32[8,512]{1,0:T(8,128)S(1)}, u32[]{:S(2)}, u32[]{:S(2)}) collective-permute-start(f32[8,512]{1,0:T(8,128)S(1)} %get-tuple-element.43), channel_id=1, source_target_pairs={{0,8},{8,0},{1,9},{9,1},{2,10},{10,2},{3,11},{11,3},{4,12},{12,4},... | collective-permute-start | bytes 49160 | tf_op jit(solution)/shard_map/ppermute | solution.py:26
  42.9 7.9 %collective-permute-start.12 = (f32[16,512]{1,0:T(8,128)S(1)}, f32[16,512]{1,0:T(8,128)S(1)}, u32[]{:S(2)}, u32[]{:S(2)}) collective-permute-start(f32[16,512]{1,0:T(8,128)S(1)} %shard_map.92.keep_ref), channel_id=1, source_target_pairs={{0,1},{1,0},{2,3},{3,2},{4,5},{5,4},{6,7},{7,6},{8,9},{9,8},{10,11... | collective-permute-start | bytes 98312 | tf_op jit(solution)/shard_map/ppermute | solution.py:26
  51.5 17.6 %all-to-all-start = ((f32[64,2,128]{2,1,0:T(2,128)}), f32[64,2,128]{2,1,0:T(2,128)S(1)}, u32[]{:S(2)}, u32[]{:S(2)}) async-start(f32[64,2,128]{2,1,0:T(2,128)} %get-tuple-element.44), calls=%async_computation | async-start | bytes 131072 | tf_op jit(solution)/shard_map/all_to_all | solution.py:288
  59.8 6.5 %collective-permute-start.13 = (f32[32,512]{1,0:T(8,128)S(1)}, f32[32,512]{1,0:T(8,128)S(1)}, u32[]{:S(2)}, u32[]{:S(2)}) collective-permute-start(f32[32,512]{1,0:T(8,128)S(1)} %get-tuple-element.45.lines3_ref), channel_id=1, source_target_pairs={{0,6},{2,4},{4,2},{6,0},{1,7},{3,5},{5,3},{7,1},{8,14},{10,12},{12... | collective-permute-start | bytes 196616 | tf_op jit(solution)/shard_map/ppermute | solution.py:30
  62.5 5.8 %collective-permute-start.14 = (f32[32,512]{1,0:T(8,128)S(1)}, f32[32,512]{1,0:T(8,128)S(1)}, u32[]{:S(2)}, u32[]{:S(2)}) collective-permute-start(f32[32,512]{1,0:T(8,128)S(1)} %get-tuple-element.45.lines3_ref), channel_id=1, source_target_pairs={{0,4},{2,6},{4,0},{6,2},{1,5},{3,7},{5,1},{7,3},{8,12},{10,14},{12... | collective-permute-start | bytes 196616 | tf_op jit(solution)/shard_map/ppermute | solution.py:30
  63.4 4.9 %collective-permute-start.15 = (f32[32,512]{1,0:T(8,128)S(1)}, f32[32,512]{1,0:T(8,128)S(1)}, u32[]{:S(2)}, u32[]{:S(2)}) collective-permute-start(f32[32,512]{1,0:T(8,128)S(1)} %get-tuple-element.45.lines3_ref), channel_id=1, source_target_pairs={{0,2},{2,0},{4,6},{6,4},{1,3},{3,1},{5,7},{7,5},{8,10},{10,8},{12,... | collective-permute-start | bytes 196616 | tf_op jit(solution)/shard_map/ppermute | solution.py:30

commit v5 on v4

--- a/solution.py
+++ b/solution.py
@@ -26,8 +26,8 @@
     return lax.ppermute(value, axis, [(0, 1), (1, 0)])
 
 
-def trade(values, axis):
-    return [lax.ppermute(values[k], axis, [(i, i ^ k) for i in range(4)]) for k in ORDER[:3]] + [
+def trade(values, axis, order=(3, 2, 1)):
+    return [lax.ppermute(values[k], axis, [(i, i ^ k) for i in range(4)]) for k in order] + [
         values[0]
     ]
 
@@ -61,14 +61,21 @@
 
 def first_body(x_ref, acts_hbm, proj_hbm, *rest):
     outs, (acts_ref, proj_ref, turned_ref, sems) = rest[:-4], rest[-4:]
-    one = pltpu.make_async_copy(acts_hbm, acts_ref, sems.at[0])
-    two = pltpu.make_async_copy(proj_hbm, proj_ref, sems.at[1])
-    two.start()
-    one.start()
-    two.wait()
-    one.wait()
-    y = jnp.dot(acts_ref[...], proj_ref[...], preferred_element_type=F32)
-    turned_ref[...] = y.T
+    half = acts_ref.shape[0] // 2
+    whole = pltpu.make_async_copy(proj_hbm, proj_ref, sems.at[2])
+    whole.start()
+    copies = []
+    for n in range(2):
+        here = pl.ds(n * half, half)
+        copies.append(pltpu.make_async_copy(acts_hbm.at[here], acts_ref.at[here], sems.at[n]))
+        copies[-1].start()
+    whole.wait()
+    for n in range(2):
+        copies[n].wait()
+        y = jnp.dot(
+            acts_ref[n * half : (n + 1) * half, :], proj_ref[...], preferred_element_type=F32
+        )
+        turned_ref[:, n * half : (n + 1) * half] = y.T
     for k in range(4):
         begin = pl.multiple_of((x_ref[0] ^ k) * 32, 32)
         outs[k][...] = turned_ref[pl.ds(begin, 32), :]
@@ -245,7 +252,7 @@
             pltpu.VMEM((tokens, rows), BF16),
             pltpu.VMEM((rows, rank), BF16),
             pltpu.VMEM((rank, tokens), F32),
-            pltpu.SemaphoreType.DMA((2,)),
+            pltpu.SemaphoreType.DMA((3,)),
         ],
     )
     y = trade(y, "x")
@@ -270,7 +277,7 @@
     parts = run(by_y_body, [(4, 8, width)] * 4, [SMEM, VMEM, VMEM], (me_y, keep, swap(give, "c")))
     parts = trade(parts, "y")
     parts = run(by_zl_body, [(8, width)] * 4, [SMEM] + [VMEM] * 4, (me_zl, *parts))
-    parts = trade(parts, "zl")
+    parts = trade(parts, "zl", (2, 1, 3))
     pair = functools.partial(pair_body, cols)
     keep, give = run(
         functools.partial(reduce_body, cols),

time: 71.1 us -> 70.3 us (0.989)
  waiting for transfers between devices: 25.2 us -> 23.3 us
  starting transfers between devices: 36.3 us -> 37.3 us
    ppermute x12, waiting for transfers between devices: 18 us -> 16.1 us  [trade(): lax.ppermute(values[k], axis, [(i, i ^ k) for i in range(4)])]
    ppermute x12, starting transfers between devices: 16.1 us -> 17 us  [trade(): lax.ppermute(values[k], axis, [(i, i ^ k) for i in range(4)])]
  transfers between devices with their start and end apart: 17 -> 17, of which waited for: 14 -> 13; matrix products, arithmetic and copies ran while one was open for 0% -> 0% of each run, Pallas kernels for 4% -> 5%
where the time goes in v5:
time: 70.3 us; the launch traced here: 70.2 us
  starting transfers between devices  37.3 us (53%)
  waiting for transfers between devices  23.3 us (33%)
  Pallas kernels  8.75 us (12%)
  between operations  0.77 us (1%)
    ppermute x12, starting transfers between devices, trade(): lax.ppermute(values[k], axis, [(i, i ^ k) for i in range(4)])  17 us
    ppermute x12, waiting for transfers between devices, trade(): lax.ppermute(values[k], axis, [(i, i ^ k) for i in range(4)])  16.1 us
    ppermute x4, starting transfers between devices, swap(): return lax.ppermute(value, axis, [(0, 1), (1, 0)])  11.9 us
    all_to_all x1, starting transfers between devices, per_device(): squares = lax.all_to_all(squares, ('y', 'zl', 'x'), 0, 0, tiled=True)  8.35 us
    pallas_call x9, Pallas kernels, run(): pl.pallas_call(body, in_specs=specs, out_shape=made[0] if single else tup...  6.93 us
    ppermute x4, waiting for transfers between devices, swap(): return lax.ppermute(value, axis, [(0, 1), (1, 0)])  6.41 us
    pallas_call x1, Pallas kernels, per_device(): pl.pallas_call(functools.partial(last_body, steps), in_specs=[SMEM] + [VM...  1.82 us
  transfers between devices with their start and end apart: 17, of which 13 were waited for; matrix products, arithmetic and copies ran while one was open for 0% of the time, Pallas kernels for 5%

profile of v5, /device:TPU:8, one launch (start us, length us, event | category | flops | bytes accessed | tf_op | source)
XLA Modules:
  0.0 70.2 jit_solution(10792149396863620165)
XLA Ops:
  0.6 1.6 %shard_map.85 = (f32[32,256]{1,0:T(8,128)S(1)}, f32[32,256]{1,0:T(8,128)S(1)}, f32[32,256]{1,0:T(8,128)S(1)}, f32[32,256]{1,0:T(8,128)S(1)}) custom-call(s32[1]{0:T(128)} %bitcast.x_ref, bf16[256,1024]{1,0:T(8,128)(2,1)} %bitcast.17, bf16[1024,128]{1,0:T(8,128)(2,1)} %proj_ref.1), custom_call_target="tpu_custom_call" | custom-call | bytes 1048576 | tf_op jit(solution)/shard_map/pallas_call | solution.py:44
  2.3 2.8 %collective-permute-start = (f32[32,256]{1,0:T(8,128)S(1)}, f32[32,256]{1,0:T(8,128)S(1)}, u32[]{:S(2)}, u32[]{:S(2)}) collective-permute-start(f32[32,256]{1,0:T(8,128)S(1)} %get-tuple-element.26), channel_id=1, source_target_pairs={{0,6},{2,4},{4,2},{6,0},{1,7},{3,5},{5,3},{7,1},{8,14},{10,12},{12... | collective-permute-start | bytes 98312 | tf_op jit(solution)/shard_map/ppermute | solution.py:30
  5.1 0.8 %collective-permute-start.1 = (f32[32,256]{1,0:T(8,128)S(1)}, f32[32,256]{1,0:T(8,128)S(1)}, u32[]{:S(2)}, u32[]{:S(2)}) collective-permute-start(f32[32,256]{1,0:T(8,128)S(1)} %get-tuple-element.27), channel_id=1, source_target_pairs={{0,4},{2,6},{4,0},{6,2},{1,5},{3,7},{5,1},{7,3},{8,12},{10,14},{12... | collective-permute-start | bytes 98312 | tf_op jit(solution)/shard_map/ppermute | solution.py:30
  5.9 0.5 collective-permute-start.2
  6.5 1.0 %collective-permute-done.refs_0_ = f32[32,256]{1,0:T(8,128)S(1)} collective-permute-done((f32[32,256]{1,0:T(8,128)S(1)}, f32[32,256]{1,0:T(8,128)S(1)}, u32[]{:S(2)}, u32[]{:S(2)}) %collective-permute-start) | collective-permute-done | bytes 32800 | tf_op jit(solution)/shard_map/ppermute | solution.py:30
  7.5 3.1 %collective-permute-done.1.refs_1_ = f32[32,256]{1,0:T(8,128)S(1)} collective-permute-done((f32[32,256]{1,0:T(8,128)S(1)}, f32[32,256]{1,0:T(8,128)S(1)}, u32[]{:S(2)}, u32[]{:S(2)}) %collective-permute-start.1) | collective-permute-done | bytes 32800 | tf_op jit(solution)/shard_map/ppermute | solution.py:30
  10.6 0.0 collective-permute-done.2.refs_2_
  10.6 7.3 %collective-permute-start.3 = (f32[16,256]{1,0:T(8,128)S(1)}, f32[16,256]{1,0:T(8,128)S(1)}, u32[]{:S(2)}, u32[]{:S(2)}) collective-permute-start(f32[16,256]{1,0:T(8,128)S(1)} %get-tuple-element.31), channel_id=1, source_target_pairs={{0,1},{1,0},{2,3},{3,2},{4,5},{5,4},{6,7},{7,6},{8,9},{9,8},{10,11... | collective-permute-start | bytes 49160 | tf_op jit(solution)/shard_map/ppermute | solution.py:26
  17.8 3.2 %shard_map.87.og_ref = bf16[256,14336]{1,0:T(8,128)(2,1)S(1)} custom-call(bf16[256,14336]{1,0:T(8,128)(2,1)} %bitcast.16, f32[16,256]{1,0:T(8,128)S(1)} %get-tuple-element.30.after_ref.one_ref), custom_call_target="tpu_custom_call" | custom-call | bytes 16777216 | tf_op jit(solution)/shard_map/pallas_call | solution.py:44
  21.0 0.0 copy-start
  21.1 0.0 copy-start.1
  21.1 0.0 copy-start.2
  21.1 0.0 copy-start.3
  21.1 0.0 collective-permute-done.3.two_ref
  21.1 1.2 %shard_map.88 = (f32[16,8,896]{2,1,0:T(8,128)S(1)}, f32[16,8,896]{2,1,0:T(8,128)S(1)}) custom-call(s32[1]{0:T(128)} %bitcast.2.c_ref.me_ref, f32[16,256]{1,0:T(8,128)S(1)} %get-tuple-element.30.after_ref.one_ref, f32[16,256]{1,0:T(8,128)S(1)} %collective-permute-done.3.two_ref, bf16[256,14336]{1,0:T(8,128)(2,1)S(1)} %shard_map.87.og_ref), custom_call_target="tpu_custom_call" | custom-call | flops 234881024 | bytes 8388608 | tf_op jit(solution)/shard_map/pallas_call | solution.py:44
  22.3 0.1 collective-permute-start.4
  22.4 1.8 %collective-permute-done.4.b_ref = f32[16,8,896]{2,1,0:T(8,128)S(1)} collective-permute-done((f32[16,8,896]{2,1,0:T(8,128)S(1)}, f32[16,8,896]{2,1,0:T(8,128)S(1)}, u32[]{:S(2)}, u32[]{:S(2)}) %collective-permute-start.4) | collective-permute-done | bytes 458784 | tf_op jit(solution)/shard_map/ppermute | solution.py:26
  24.2 1.7 %collective-permute-start.5 = (f32[4,8,896]{2,1,0:T(8,128)S(1)}, f32[4,8,896]{2,1,0:T(8,128)S(1)}, u32[]{:S(2)}, u32[]{:S(2)}) collective-permute-start(f32[4,8,896]{2,1,0:T(8,128)S(1)} %get-tuple-element.34), channel_id=1, source_target_pairs={{0,192},{64,128},{128,64},{192,0},{1,193},{65,129},{129,65},{193,1... | collective-permute-start | bytes 344072 | tf_op jit(solution)/shard_map/ppermute | solution.py:30
  25.9 0.9 %collective-permute-start.6 = (f32[4,8,896]{2,1,0:T(8,128)S(1)}, f32[4,8,896]{2,1,0:T(8,128)S(1)}, u32[]{:S(2)}, u32[]{:S(2)}) collective-permute-start(f32[4,8,896]{2,1,0:T(8,128)S(1)} %get-tuple-element.35), channel_id=1, source_target_pairs={{0,128},{64,192},{128,0},{192,64},{1,129},{65,193},{129,1},{193,65... | collective-permute-start | bytes 344072 | tf_op jit(solution)/shard_map/ppermute | solution.py:30
  26.8 1.6 %collective-permute-start.7 = (f32[4,8,896]{2,1,0:T(8,128)S(1)}, f32[4,8,896]{2,1,0:T(8,128)S(1)}, u32[]{:S(2)}, u32[]{:S(2)}) collective-permute-start(f32[4,8,896]{2,1,0:T(8,128)S(1)} %get-tuple-element.36), channel_id=1, source_target_pairs={{0,64},{64,0},{128,192},{192,128},{1,65},{65,1},{129,193},{193,129... | collective-permute-start | bytes 344072 | tf_op jit(solution)/shard_map/ppermute | solution.py:30
  28.4 2.2 %collective-permute-done.5.refs_0_ = f32[4,8,896]{2,1,0:T(8,128)S(1)} collective-permute-done((f32[4,8,896]{2,1,0:T(8,128)S(1)}, f32[4,8,896]{2,1,0:T(8,128)S(1)}, u32[]{:S(2)}, u32[]{:S(2)}) %collective-permute-start.5) | collective-permute-done | bytes 114720 | tf_op jit(solution)/shard_map/ppermute | solution.py:30
  30.6 2.9 %collective-permute-done.6.refs_1_ = f32[4,8,896]{2,1,0:T(8,128)S(1)} collective-permute-done((f32[4,8,896]{2,1,0:T(8,128)S(1)}, f32[4,8,896]{2,1,0:T(8,128)S(1)}, u32[]{:S(2)}, u32[]{:S(2)}) %collective-permute-start.6) | collective-permute-done | bytes 114720 | tf_op jit(solution)/shard_map/ppermute | solution.py:30
  33.4 0.4 collective-permute-done.7.refs_2_
  33.8 2.0 %collective-permute-start.10 = (f32[8,896]{1,0:T(8,128)S(1)}, f32[8,896]{1,0:T(8,128)S(1)}, u32[]{:S(2)}, u32[]{:S(2)}) collective-permute-start(f32[8,896]{1,0:T(8,128)S(1)} %get-tuple-element.40), channel_id=1, source_target_pairs={{0,48},{16,32},{32,16},{48,0},{1,49},{17,33},{33,17},{49,1},{2,50}... | collective-permute-start | bytes 86024 | tf_op jit(solution)/shard_map/ppermute | solution.py:30
  35.9 0.6 collective-permute-start.8
  36.4 1.9 %collective-permute-start.9 = (f32[8,896]{1,0:T(8,128)S(1)}, f32[8,896]{1,0:T(8,128)S(1)}, u32[]{:S(2)}, u32[]{:S(2)}) collective-permute-start(f32[8,896]{1,0:T(8,128)S(1)} %get-tuple-element.39), channel_id=1, source_target_pairs={{0,16},{16,0},{32,48},{48,32},{1,17},{17,1},{33,49},{49,33},{2,18}... | collective-permute-start | bytes 86024 | tf_op jit(solution)/shard_map/ppermute | solution.py:30
  38.3 1.6 %collective-permute-done.10.refs_2_ = f32[8,896]{1,0:T(8,128)S(1)} collective-permute-done((f32[8,896]{1,0:T(8,128)S(1)}, f32[8,896]{1,0:T(8,128)S(1)}, u32[]{:S(2)}, u32[]{:S(2)}) %collective-permute-start.10) | collective-permute-done | bytes 28704 | tf_op jit(solution)/shard_map/ppermute | solution.py:30
  39.9 0.7 %collective-permute-done.8.refs_0_ = f32[8,896]{1,0:T(8,128)S(1)} collective-permute-done((f32[8,896]{1,0:T(8,128)S(1)}, f32[8,896]{1,0:T(8,128)S(1)}, u32[]{:S(2)}, u32[]{:S(2)}) %collective-permute-start.8) | collective-permute-done | bytes 28704 | tf_op jit(solution)/shard_map/ppermute | solution.py:30
  40.6 0.0 collective-permute-done.9.refs_1_
  40.6 0.1 shard_map.91
  40.7 0.1 collective-permute-start.11
  40.8 1.2 %collective-permute-done.11.got_ref = f32[8,512]{1,0:T(8,128)S(1)} collective-permute-done((f32[8,512]{1,0:T(8,128)S(1)}, f32[8,512]{1,0:T(8,128)S(1)}, u32[]{:S(2)}, u32[]{:S(2)}) %collective-permute-start.11) | collective-permute-done | bytes 16416 | tf_op jit(solution)/shard_map/ppermute | solution.py:26
  42.0 4.5 %collective-permute-start.12 = (f32[16,512]{1,0:T(8,128)S(1)}, f32[16,512]{1,0:T(8,128)S(1)}, u32[]{:S(2)}, u32[]{:S(2)}) collective-permute-start(f32[16,512]{1,0:T(8,128)S(1)} %shard_map.92.keep_ref), channel_id=1, source_target_pairs={{0,1},{1,0},{2,3},{3,2},{4,5},{5,4},{6,7},{7,6},{8,9},{9,8},{10,11... | collective-permute-start | bytes 98312 | tf_op jit(solution)/shard_map/ppermute | solution.py:26
  46.5 3.4 %collective-permute-done.12.got_ref = f32[16,512]{1,0:T(8,128)S(1)} collective-permute-done((f32[16,512]{1,0:T(8,128)S(1)}, f32[16,512]{1,0:T(8,128)S(1)}, u32[]{:S(2)}, u32[]{:S(2)}) %collective-permute-start.12) | collective-permute-done | bytes 32800 | tf_op jit(solution)/shard_map/ppermute | solution.py:26
  49.9 0.8 %shard_map.93 = (f32[32,512]{1,0:T(8,128)S(1)}, f32[64,2,128]{2,1,0:T(2,128)}) custom-call(s32[1]{0:T(128)} %bitcast.1.zh_ref.me_ref, f32[16,512]{1,0:T(8,128)S(1)} %shard_map.92.keep_ref, f32[16,512]{1,0:T(8,128)S(1)} %collective-permute-done.12.got_ref), custom_call_target="tpu_custom_call" | custom-call | bytes 1048576 | tf_op jit(solution)/shard_map/pallas_call | solution.py:44
  50.7 8.4 %all-to-all-start = ((f32[64,2,128]{2,1,0:T(2,128)}), f32[64,2,128]{2,1,0:T(2,128)S(1)}, u32[]{:S(2)}, u32[]{:S(2)}) async-start(f32[64,2,128]{2,1,0:T(2,128)} %get-tuple-element.44), calls=%async_computation | async-start | bytes 131072 | tf_op jit(solution)/shard_map/all_to_all | solution.py:295
  59.0 2.8 %collective-permute-start.13 = (f32[32,512]{1,0:T(8,128)S(1)}, f32[32,512]{1,0:T(8,128)S(1)}, u32[]{:S(2)}, u32[]{:S(2)}) collective-permute-start(f32[32,512]{1,0:T(8,128)S(1)} %get-tuple-element.45.lines3_ref), channel_id=1, source_target_pairs={{0,6},{2,4},{4,2},{6,0},{1,7},{3,5},{5,3},{7,1},{8,14},{10,12},{12... | collective-permute-start | bytes 196616 | tf_op jit(solution)/shard_map/ppermute | solution.py:30
  61.8 0.9 %collective-permute-start.14 = (f32[32,512]{1,0:T(8,128)S(1)}, f32[32,512]{1,0:T(8,128)S(1)}, u32[]{:S(2)}, u32[]{:S(2)}) collective-permute-start(f32[32,512]{1,0:T(8,128)S(1)} %get-tuple-element.45.lines3_ref), channel_id=1, source_target_pairs={{0,4},{2,6},{4,0},{6,2},{1,5},{3,7},{5,1},{7,3},{8,12},{10,14},{12... | collective-permute-start | bytes 196616 | tf_op jit(solution)/shard_map/ppermute | solution.py:30
  62.6 0.6 collective-permute-start.15
  63.2 2.3 %collective-permute-done.13.lines0_ref = f32[32,512]{1,0:T(8,128)S(1)} collective-permute-done((f32[32,512]{1,0:T(8,128)S(1)}, f32[32,512]{1,0:T(8,128)S(1)}, u32[]{:S(2)}, u32[]{:S(2)}) %collective-permute-start.13) | collective-permute-done | bytes 65568 | tf_op jit(solution)/shard_map/ppermute | solution.py:30
  65.5 2.0 %collective-permute-done.14.lines1_ref = f32[32,512]{1,0:T(8,128)S(1)} collective-permute-done((f32[32,512]{1,0:T(8,128)S(1)}, f32[32,512]{1,0:T(8,128)S(1)}, u32[]{:S(2)}, u32[]{:S(2)}) %collective-permute-start.14) | collective-permute-done | bytes 65568 | tf_op jit(solution)/shard_map/ppermute | solution.py:30
  67.6 0.0 collective-permute-done.15.lines2_ref
  67.6 0.8 %all-to-all-done.squares_ref = f32[64,2,128]{2,1,0:T(2,128)S(1)} async-done(((f32[64,2,128]{2,1,0:T(2,128)}), f32[64,2,128]{2,1,0:T(2,128)S(1)}, u32[]{:S(2)}, u32[]{:S(2)}) %all-to-all-start) | async-done | bytes 65568 | tf_op jit(solution)/shard_map/all_to_all | solution.py:295
  68.3 0.0 copy-done
  68.3 0.0 copy-done.1
  68.3 0.0 copy-done.2
  68.4 0.0 copy-done.3
  68.4 1.8 %shard_map.94 = (f32[448,1024]{1,0:T(8,128)}, f32[448,128]{1,0:T(8,128)}, f32[448,128]{1,0:T(8,128)}) custom-call(s32[1]{0:T(128)} %bitcast.x_ref, f32[64,2,128]{2,1,0:T(2,128)S(1)} %all-to-all-done.squares_ref, f32[32,512]{1,0:T(8,128)S(1)} %collective-permute-done.13.lines0_ref, f32[32,512]{1,0:T(8,128)S(1)} %collective-permute-done.14.lines1_ref, ...), custom_call_target="tpu_custom_call" | custom-call | flops 117440512 | bytes 4194304 | tf_op jit(solution)/shard_map/pallas_call | solution.py:300
  (4 shorter events, 0.1 us)
Async XLA Ops:
  2.3 5.2 %collective-permute-start = (f32[32,256]{1,0:T(8,128)S(1)}, f32[32,256]{1,0:T(8,128)S(1)}, u32[]{:S(2)}, u32[]{:S(2)}) collective-permute-start(f32[32,256]{1,0:T(8,128)S(1)} %get-tuple-element.26), channel_id=1, source_target_pairs={{0,6},{2,4},{4,2},{6,0},{1,7},{3,5},{5,3},{7,1},{8,14},{10,12},{12... | collective-permute-start | bytes 98312 | tf_op jit(solution)/shard_map/ppermute | solution.py:30
  5.1 5.4 %collective-permute-start.1 = (f32[32,256]{1,0:T(8,128)S(1)}, f32[32,256]{1,0:T(8,128)S(1)}, u32[]{:S(2)}, u32[]{:S(2)}) collective-permute-start(f32[32,256]{1,0:T(8,128)S(1)} %get-tuple-element.27), channel_id=1, source_target_pairs={{0,4},{2,6},{4,0},{6,2},{1,5},{3,7},{5,1},{7,3},{8,12},{10,14},{12... | collective-permute-start | bytes 98312 | tf_op jit(solution)/shard_map/ppermute | solution.py:30
  5.9 4.6 %collective-permute-start.2 = (f32[32,256]{1,0:T(8,128)S(1)}, f32[32,256]{1,0:T(8,128)S(1)}, u32[]{:S(2)}, u32[]{:S(2)}) collective-permute-start(f32[32,256]{1,0:T(8,128)S(1)} %get-tuple-element.28), channel_id=1, source_target_pairs={{0,2},{2,0},{4,6},{6,4},{1,3},{3,1},{5,7},{7,5},{8,10},{10,8},{12,... | collective-permute-start | bytes 98312 | tf_op jit(solution)/shard_map/ppermute | solution.py:30
  10.6 10.5 %collective-permute-start.3 = (f32[16,256]{1,0:T(8,128)S(1)}, f32[16,256]{1,0:T(8,128)S(1)}, u32[]{:S(2)}, u32[]{:S(2)}) collective-permute-start(f32[16,256]{1,0:T(8,128)S(1)} %get-tuple-element.31), channel_id=1, source_target_pairs={{0,1},{1,0},{2,3},{3,2},{4,5},{5,4},{6,7},{7,6},{8,9},{9,8},{10,11... | collective-permute-start | bytes 49160 | tf_op jit(solution)/shard_map/ppermute | solution.py:26
  21.0 47.3 %copy-start = (bf16[1024,128]{1,0:T(8,128)(2,1)S(1)}, bf16[1024,128]{1,0:T(8,128)(2,1)}, u32[]{:S(2)}) copy-start(bf16[1024,128]{1,0:T(8,128)(2,1)} %proj_ref.1) | copy-start | bytes 786436
  21.1 47.3 %copy-start.1 = (bf16[1024,448]{0,1:T(8,128)(2,1)S(1)}, bf16[1024,448]{0,1:T(8,128)(2,1)}, u32[]{:S(2)}) copy-start(bf16[1024,448]{0,1:T(8,128)(2,1)} %param.9) | copy-start | bytes 2752516
  21.1 47.3 %copy-start.2 = (f32[128,448]{0,1:T(8,128)S(1)}, f32[128,448]{0,1:T(8,128)}, u32[]{:S(2)}) copy-start(f32[128,448]{0,1:T(8,128)} %param.10) | copy-start | bytes 688132
  21.1 47.3 %copy-start.3 = (f32[128,448]{0,1:T(8,128)S(1)}, f32[128,448]{0,1:T(8,128)}, u32[]{:S(2)}) copy-start(f32[128,448]{0,1:T(8,128)} %param.11) | copy-start | bytes 688132
  22.3 1.9 %collective-permute-start.4 = (f32[16,8,896]{2,1,0:T(8,128)S(1)}, f32[16,8,896]{2,1,0:T(8,128)S(1)}, u32[]{:S(2)}, u32[]{:S(2)}) collective-permute-start(f32[16,8,896]{2,1,0:T(8,128)S(1)} %get-tuple-element.33), channel_id=1, source_target_pairs={{0,8},{8,0},{1,9},{9,1},{2,10},{10,2},{3,11},{11,3},{4,12},{12,4},... | collective-permute-start | bytes 1376264 | tf_op jit(solution)/shard_map/ppermute | solution.py:26
  24.2 6.3 %collective-permute-start.5 = (f32[4,8,896]{2,1,0:T(8,128)S(1)}, f32[4,8,896]{2,1,0:T(8,128)S(1)}, u32[]{:S(2)}, u32[]{:S(2)}) collective-permute-start(f32[4,8,896]{2,1,0:T(8,128)S(1)} %get-tuple-element.34), channel_id=1, source_target_pairs={{0,192},{64,128},{128,64},{192,0},{1,193},{65,129},{129,65},{193,1... | collective-permute-start | bytes 344072 | tf_op jit(solution)/shard_map/ppermute | solution.py:30
  25.9 7.5 %collective-permute-start.6 = (f32[4,8,896]{2,1,0:T(8,128)S(1)}, f32[4,8,896]{2,1,0:T(8,128)S(1)}, u32[]{:S(2)}, u32[]{:S(2)}) collective-permute-start(f32[4,8,896]{2,1,0:T(8,128)S(1)} %get-tuple-element.35), channel_id=1, source_target_pairs={{0,128},{64,192},{128,0},{192,64},{1,129},{65,193},{129,1},{193,65... | collective-permute-start | bytes 344072 | tf_op jit(solution)/shard_map/ppermute | solution.py:30
  26.8 7.0 %collective-permute-start.7 = (f32[4,8,896]{2,1,0:T(8,128)S(1)}, f32[4,8,896]{2,1,0:T(8,128)S(1)}, u32[]{:S(2)}, u32[]{:S(2)}) collective-permute-start(f32[4,8,896]{2,1,0:T(8,128)S(1)} %get-tuple-element.36), channel_id=1, source_target_pairs={{0,64},{64,0},{128,192},{192,128},{1,65},{65,1},{129,193},{193,129... | collective-permute-start | bytes 344072 | tf_op jit(solution)/shard_map/ppermute | solution.py:30
  33.8 6.1 %collective-permute-start.10 = (f32[8,896]{1,0:T(8,128)S(1)}, f32[8,896]{1,0:T(8,128)S(1)}, u32[]{:S(2)}, u32[]{:S(2)}) collective-permute-start(f32[8,896]{1,0:T(8,128)S(1)} %get-tuple-element.40), channel_id=1, source_target_pairs={{0,48},{16,32},{32,16},{48,0},{1,49},{17,33},{33,17},{49,1},{2,50}... | collective-permute-start | bytes 86024 | tf_op jit(solution)/shard_map/ppermute | solution.py:30
  35.9 4.8 %collective-permute-start.8 = (f32[8,896]{1,0:T(8,128)S(1)}, f32[8,896]{1,0:T(8,128)S(1)}, u32[]{:S(2)}, u32[]{:S(2)}) collective-permute-start(f32[8,896]{1,0:T(8,128)S(1)} %get-tuple-element.38), channel_id=1, source_target_pairs={{0,32},{16,48},{32,0},{48,16},{1,33},{17,49},{33,1},{49,17},{2,34}... | collective-permute-start | bytes 86024 | tf_op jit(solution)/shard_map/ppermute | solution.py:30
  36.4 4.2 %collective-permute-start.9 = (f32[8,896]{1,0:T(8,128)S(1)}, f32[8,896]{1,0:T(8,128)S(1)}, u32[]{:S(2)}, u32[]{:S(2)}) collective-permute-start(f32[8,896]{1,0:T(8,128)S(1)} %get-tuple-element.39), channel_id=1, source_target_pairs={{0,16},{16,0},{32,48},{48,32},{1,17},{17,1},{33,49},{49,33},{2,18}... | collective-permute-start | bytes 86024 | tf_op jit(solution)/shard_map/ppermute | solution.py:30
  40.7 1.3 %collective-permute-start.11 = (f32[8,512]{1,0:T(8,128)S(1)}, f32[8,512]{1,0:T(8,128)S(1)}, u32[]{:S(2)}, u32[]{:S(2)}) collective-permute-start(f32[8,512]{1,0:T(8,128)S(1)} %get-tuple-element.43), channel_id=1, source_target_pairs={{0,8},{8,0},{1,9},{9,1},{2,10},{10,2},{3,11},{11,3},{4,12},{12,4},... | collective-permute-start | bytes 49160 | tf_op jit(solution)/shard_map/ppermute | solution.py:26
  42.0 7.9 %collective-permute-start.12 = (f32[16,512]{1,0:T(8,128)S(1)}, f32[16,512]{1,0:T(8,128)S(1)}, u32[]{:S(2)}, u32[]{:S(2)}) collective-permute-start(f32[16,512]{1,0:T(8,128)S(1)} %shard_map.92.keep_ref), channel_id=1, source_target_pairs={{0,1},{1,0},{2,3},{3,2},{4,5},{5,4},{6,7},{7,6},{8,9},{9,8},{10,11... | collective-permute-start | bytes 98312 | tf_op jit(solution)/shard_map/ppermute | solution.py:26
  50.7 17.7 %all-to-all-start = ((f32[64,2,128]{2,1,0:T(2,128)}), f32[64,2,128]{2,1,0:T(2,128)S(1)}, u32[]{:S(2)}, u32[]{:S(2)}) async-start(f32[64,2,128]{2,1,0:T(2,128)} %get-tuple-element.44), calls=%async_computation | async-start | bytes 131072 | tf_op jit(solution)/shard_map/all_to_all | solution.py:295
  59.0 6.5 %collective-permute-start.13 = (f32[32,512]{1,0:T(8,128)S(1)}, f32[32,512]{1,0:T(8,128)S(1)}, u32[]{:S(2)}, u32[]{:S(2)}) collective-permute-start(f32[32,512]{1,0:T(8,128)S(1)} %get-tuple-element.45.lines3_ref), channel_id=1, source_target_pairs={{0,6},{2,4},{4,2},{6,0},{1,7},{3,5},{5,3},{7,1},{8,14},{10,12},{12... | collective-permute-start | bytes 196616 | tf_op jit(solution)/shard_map/ppermute | solution.py:30
  61.8 5.8 %collective-permute-start.14 = (f32[32,512]{1,0:T(8,128)S(1)}, f32[32,512]{1,0:T(8,128)S(1)}, u32[]{:S(2)}, u32[]{:S(2)}) collective-permute-start(f32[32,512]{1,0:T(8,128)S(1)} %get-tuple-element.45.lines3_ref), channel_id=1, source_target_pairs={{0,4},{2,6},{4,0},{6,2},{1,5},{3,7},{5,1},{7,3},{8,12},{10,14},{12... | collective-permute-start | bytes 196616 | tf_op jit(solution)/shard_map/ppermute | solution.py:30
  62.6 4.9 %collective-permute-start.15 = (f32[32,512]{1,0:T(8,128)S(1)}, f32[32,512]{1,0:T(8,128)S(1)}, u32[]{:S(2)}, u32[]{:S(2)}) collective-permute-start(f32[32,512]{1,0:T(8,128)S(1)} %get-tuple-element.45.lines3_ref), channel_id=1, source_target_pairs={{0,2},{2,0},{4,6},{6,4},{1,3},{3,1},{5,7},{7,5},{8,10},{10,8},{12,... | collective-permute-start | bytes 196616 | tf_op jit(solution)/shard_map/ppermute | solution.py:30

commit v6 on v4

--- a/solution.py
+++ b/solution.py
@@ -26,8 +26,8 @@
     return lax.ppermute(value, axis, [(0, 1), (1, 0)])
 
 
-def trade(values, axis):
-    return [lax.ppermute(values[k], axis, [(i, i ^ k) for i in range(4)]) for k in ORDER[:3]] + [
+def trade(values, axis, order=(3, 2, 1)):
+    return [lax.ppermute(values[k], axis, [(i, i ^ k) for i in range(4)]) for k in order] + [
         values[0]
     ]
 
@@ -270,7 +270,7 @@
     parts = run(by_y_body, [(4, 8, width)] * 4, [SMEM, VMEM, VMEM], (me_y, keep, swap(give, "c")))
     parts = trade(parts, "y")
     parts = run(by_zl_body, [(8, width)] * 4, [SMEM] + [VMEM] * 4, (me_zl, *parts))
-    parts = trade(parts, "zl")
+    parts = trade(parts, "zl", (2, 1, 3))
     pair = functools.partial(pair_body, cols)
     keep, give = run(
         functools.partial(reduce_body, cols),

time: 71.1 us -> 70.2 us (0.987)
  waiting for transfers between devices: 25.2 us -> 23.3 us
  starting transfers between devices: 36.3 us -> 37.3 us
    ppermute x12, waiting for transfers between devices: 18 us -> 16.1 us  [trade(): lax.ppermute(values[k], axis, [(i, i ^ k) for i in range(4)])]
    ppermute x12, starting transfers between devices: 16.1 us -> 17 us  [trade(): lax.ppermute(values[k], axis, [(i, i ^ k) for i in range(4)])]
  transfers between devices with their start and end apart: 17 -> 17, of which waited for: 14 -> 13; matrix products, arithmetic and copies ran while one was open for 0% -> 0% of each run, Pallas kernels for 4% -> 5%
where the time goes in v6:
time: 70.2 us; the launch traced here: 70.1 us
  starting transfers between devices  37.3 us (53%)
  waiting for transfers between devices  23.3 us (33%)
  Pallas kernels  8.62 us (12%)
  between operations  0.77 us (1%)
    ppermute x12, starting transfers between devices, trade(): lax.ppermute(values[k], axis, [(i, i ^ k) for i in range(4)])  17 us
    ppermute x12, waiting for transfers between devices, trade(): lax.ppermute(values[k], axis, [(i, i ^ k) for i in range(4)])  16.1 us
    ppermute x4, starting transfers between devices, swap(): return lax.ppermute(value, axis, [(0, 1), (1, 0)])  11.9 us
    all_to_all x1, starting transfers between devices, per_device(): squares = lax.all_to_all(squares, ('y', 'zl', 'x'), 0, 0, tiled=True)  8.36 us
    pallas_call x9, Pallas kernels, run(): pl.pallas_call(body, in_specs=specs, out_shape=made[0] if single else tup...  6.8 us
    ppermute x4, waiting for transfers between devices, swap(): return lax.ppermute(value, axis, [(0, 1), (1, 0)])  6.41 us
    pallas_call x1, Pallas kernels, per_device(): pl.pallas_call(functools.partial(last_body, steps), in_specs=[SMEM] + [VM...  1.82 us
  transfers between devices with their start and end apart: 17, of which 13 were waited for; matrix products, arithmetic and copies ran while one was open for 0% of the time, Pallas kernels for 5%

profile of v6, /device:TPU:8, one launch (start us, length us, event | category | flops | bytes accessed | tf_op | source)
XLA Modules:
  0.0 70.1 jit_solution(13283547521640740981)
XLA Ops:
  0.6 1.5 %shard_map.85 = (f32[32,256]{1,0:T(8,128)S(1)}, f32[32,256]{1,0:T(8,128)S(1)}, f32[32,256]{1,0:T(8,128)S(1)}, f32[32,256]{1,0:T(8,128)S(1)}) custom-call(s32[1]{0:T(128)} %bitcast.x_ref, bf16[256,1024]{1,0:T(8,128)(2,1)} %bitcast.17, bf16[1024,128]{1,0:T(8,128)(2,1)} %proj_ref.1), custom_call_target="tpu_custom_call" | custom-call | bytes 1048576 | tf_op jit(solution)/shard_map/pallas_call | solution.py:44
  2.2 2.9 %collective-permute-start = (f32[32,256]{1,0:T(8,128)S(1)}, f32[32,256]{1,0:T(8,128)S(1)}, u32[]{:S(2)}, u32[]{:S(2)}) collective-permute-start(f32[32,256]{1,0:T(8,128)S(1)} %get-tuple-element.26), channel_id=1, source_target_pairs={{0,6},{2,4},{4,2},{6,0},{1,7},{3,5},{5,3},{7,1},{8,14},{10,12},{12... | collective-permute-start | bytes 98312 | tf_op jit(solution)/shard_map/ppermute | solution.py:30
  5.0 0.8 %collective-permute-start.1 = (f32[32,256]{1,0:T(8,128)S(1)}, f32[32,256]{1,0:T(8,128)S(1)}, u32[]{:S(2)}, u32[]{:S(2)}) collective-permute-start(f32[32,256]{1,0:T(8,128)S(1)} %get-tuple-element.27), channel_id=1, source_target_pairs={{0,4},{2,6},{4,0},{6,2},{1,5},{3,7},{5,1},{7,3},{8,12},{10,14},{12... | collective-permute-start | bytes 98312 | tf_op jit(solution)/shard_map/ppermute | solution.py:30
  5.8 0.5 collective-permute-start.2
  6.3 1.0 %collective-permute-done.refs_0_ = f32[32,256]{1,0:T(8,128)S(1)} collective-permute-done((f32[32,256]{1,0:T(8,128)S(1)}, f32[32,256]{1,0:T(8,128)S(1)}, u32[]{:S(2)}, u32[]{:S(2)}) %collective-permute-start) | collective-permute-done | bytes 32800 | tf_op jit(solution)/shard_map/ppermute | solution.py:30
  7.4 3.1 %collective-permute-done.1.refs_1_ = f32[32,256]{1,0:T(8,128)S(1)} collective-permute-done((f32[32,256]{1,0:T(8,128)S(1)}, f32[32,256]{1,0:T(8,128)S(1)}, u32[]{:S(2)}, u32[]{:S(2)}) %collective-permute-start.1) | collective-permute-done | bytes 32800 | tf_op jit(solution)/shard_map/ppermute | solution.py:30
  10.4 0.0 collective-permute-done.2.refs_2_
  10.4 7.3 %collective-permute-start.3 = (f32[16,256]{1,0:T(8,128)S(1)}, f32[16,256]{1,0:T(8,128)S(1)}, u32[]{:S(2)}, u32[]{:S(2)}) collective-permute-start(f32[16,256]{1,0:T(8,128)S(1)} %get-tuple-element.31), channel_id=1, source_target_pairs={{0,1},{1,0},{2,3},{3,2},{4,5},{5,4},{6,7},{7,6},{8,9},{9,8},{10,11... | collective-permute-start | bytes 49160 | tf_op jit(solution)/shard_map/ppermute | solution.py:26
  17.7 3.2 %shard_map.87.og_ref = bf16[256,14336]{1,0:T(8,128)(2,1)S(1)} custom-call(bf16[256,14336]{1,0:T(8,128)(2,1)} %bitcast.16, f32[16,256]{1,0:T(8,128)S(1)} %get-tuple-element.30.after_ref.one_ref), custom_call_target="tpu_custom_call" | custom-call | bytes 16777216 | tf_op jit(solution)/shard_map/pallas_call | solution.py:44
  20.9 0.0 copy-start
  20.9 0.0 copy-start.1
  20.9 0.0 copy-start.2
  20.9 0.0 copy-start.3
  21.0 0.0 collective-permute-done.3.two_ref
  21.0 1.2 %shard_map.88 = (f32[16,8,896]{2,1,0:T(8,128)S(1)}, f32[16,8,896]{2,1,0:T(8,128)S(1)}) custom-call(s32[1]{0:T(128)} %bitcast.2.c_ref.me_ref, f32[16,256]{1,0:T(8,128)S(1)} %get-tuple-element.30.after_ref.one_ref, f32[16,256]{1,0:T(8,128)S(1)} %collective-permute-done.3.two_ref, bf16[256,14336]{1,0:T(8,128)(2,1)S(1)} %shard_map.87.og_ref), custom_call_target="tpu_custom_call" | custom-call | flops 234881024 | bytes 8388608 | tf_op jit(solution)/shard_map/pallas_call | solution.py:44
  22.2 0.1 collective-permute-start.4
  22.3 1.8 %collective-permute-done.4.b_ref = f32[16,8,896]{2,1,0:T(8,128)S(1)} collective-permute-done((f32[16,8,896]{2,1,0:T(8,128)S(1)}, f32[16,8,896]{2,1,0:T(8,128)S(1)}, u32[]{:S(2)}, u32[]{:S(2)}) %collective-permute-start.4) | collective-permute-done | bytes 458784 | tf_op jit(solution)/shard_map/ppermute | solution.py:26
  24.1 1.7 %collective-permute-start.5 = (f32[4,8,896]{2,1,0:T(8,128)S(1)}, f32[4,8,896]{2,1,0:T(8,128)S(1)}, u32[]{:S(2)}, u32[]{:S(2)}) collective-permute-start(f32[4,8,896]{2,1,0:T(8,128)S(1)} %get-tuple-element.34), channel_id=1, source_target_pairs={{0,192},{64,128},{128,64},{192,0},{1,193},{65,129},{129,65},{193,1... | collective-permute-start | bytes 344072 | tf_op jit(solution)/shard_map/ppermute | solution.py:30
  25.8 0.9 %collective-permute-start.6 = (f32[4,8,896]{2,1,0:T(8,128)S(1)}, f32[4,8,896]{2,1,0:T(8,128)S(1)}, u32[]{:S(2)}, u32[]{:S(2)}) collective-permute-start(f32[4,8,896]{2,1,0:T(8,128)S(1)} %get-tuple-element.35), channel_id=1, source_target_pairs={{0,128},{64,192},{128,0},{192,64},{1,129},{65,193},{129,1},{193,65... | collective-permute-start | bytes 344072 | tf_op jit(solution)/shard_map/ppermute | solution.py:30
  26.7 1.6 %collective-permute-start.7 = (f32[4,8,896]{2,1,0:T(8,128)S(1)}, f32[4,8,896]{2,1,0:T(8,128)S(1)}, u32[]{:S(2)}, u32[]{:S(2)}) collective-permute-start(f32[4,8,896]{2,1,0:T(8,128)S(1)} %get-tuple-element.36), channel_id=1, source_target_pairs={{0,64},{64,0},{128,192},{192,128},{1,65},{65,1},{129,193},{193,129... | collective-permute-start | bytes 344072 | tf_op jit(solution)/shard_map/ppermute | solution.py:30
  28.3 2.2 %collective-permute-done.5.refs_0_ = f32[4,8,896]{2,1,0:T(8,128)S(1)} collective-permute-done((f32[4,8,896]{2,1,0:T(8,128)S(1)}, f32[4,8,896]{2,1,0:T(8,128)S(1)}, u32[]{:S(2)}, u32[]{:S(2)}) %collective-permute-start.5) | collective-permute-done | bytes 114720 | tf_op jit(solution)/shard_map/ppermute | solution.py:30
  30.4 2.9 %collective-permute-done.6.refs_1_ = f32[4,8,896]{2,1,0:T(8,128)S(1)} collective-permute-done((f32[4,8,896]{2,1,0:T(8,128)S(1)}, f32[4,8,896]{2,1,0:T(8,128)S(1)}, u32[]{:S(2)}, u32[]{:S(2)}) %collective-permute-start.6) | collective-permute-done | bytes 114720 | tf_op jit(solution)/shard_map/ppermute | solution.py:30
  33.3 0.4 collective-permute-done.7.refs_2_
  33.7 2.0 %collective-permute-start.10 = (f32[8,896]{1,0:T(8,128)S(1)}, f32[8,896]{1,0:T(8,128)S(1)}, u32[]{:S(2)}, u32[]{:S(2)}) collective-permute-start(f32[8,896]{1,0:T(8,128)S(1)} %get-tuple-element.40), channel_id=1, source_target_pairs={{0,48},{16,32},{32,16},{48,0},{1,49},{17,33},{33,17},{49,1},{2,50}... | collective-permute-start | bytes 86024 | tf_op jit(solution)/shard_map/ppermute | solution.py:30
  35.7 0.6 collective-permute-start.8
  36.3 1.9 %collective-permute-start.9 = (f32[8,896]{1,0:T(8,128)S(1)}, f32[8,896]{1,0:T(8,128)S(1)}, u32[]{:S(2)}, u32[]{:S(2)}) collective-permute-start(f32[8,896]{1,0:T(8,128)S(1)} %get-tuple-element.39), channel_id=1, source_target_pairs={{0,16},{16,0},{32,48},{48,32},{1,17},{17,1},{33,49},{49,33},{2,18}... | collective-permute-start | bytes 86024 | tf_op jit(solution)/shard_map/ppermute | solution.py:30
  38.2 1.6 %collective-permute-done.10.refs_2_ = f32[8,896]{1,0:T(8,128)S(1)} collective-permute-done((f32[8,896]{1,0:T(8,128)S(1)}, f32[8,896]{1,0:T(8,128)S(1)}, u32[]{:S(2)}, u32[]{:S(2)}) %collective-permute-start.10) | collective-permute-done | bytes 28704 | tf_op jit(solution)/shard_map/ppermute | solution.py:30
  39.8 0.7 %collective-permute-done.8.refs_0_ = f32[8,896]{1,0:T(8,128)S(1)} collective-permute-done((f32[8,896]{1,0:T(8,128)S(1)}, f32[8,896]{1,0:T(8,128)S(1)}, u32[]{:S(2)}, u32[]{:S(2)}) %collective-permute-start.8) | collective-permute-done | bytes 28704 | tf_op jit(solution)/shard_map/ppermute | solution.py:30
  40.5 0.0 collective-permute-done.9.refs_1_
  40.5 0.1 shard_map.91
  40.6 0.1 collective-permute-start.11
  40.7 1.2 %collective-permute-done.11.got_ref = f32[8,512]{1,0:T(8,128)S(1)} collective-permute-done((f32[8,512]{1,0:T(8,128)S(1)}, f32[8,512]{1,0:T(8,128)S(1)}, u32[]{:S(2)}, u32[]{:S(2)}) %collective-permute-start.11) | collective-permute-done | bytes 16416 | tf_op jit(solution)/shard_map/ppermute | solution.py:26
  41.9 4.5 %collective-permute-start.12 = (f32[16,512]{1,0:T(8,128)S(1)}, f32[16,512]{1,0:T(8,128)S(1)}, u32[]{:S(2)}, u32[]{:S(2)}) collective-permute-start(f32[16,512]{1,0:T(8,128)S(1)} %shard_map.92.keep_ref), channel_id=1, source_target_pairs={{0,1},{1,0},{2,3},{3,2},{4,5},{5,4},{6,7},{7,6},{8,9},{9,8},{10,11... | collective-permute-start | bytes 98312 | tf_op jit(solution)/shard_map/ppermute | solution.py:26
  46.3 3.4 %collective-permute-done.12.got_ref = f32[16,512]{1,0:T(8,128)S(1)} collective-permute-done((f32[16,512]{1,0:T(8,128)S(1)}, f32[16,512]{1,0:T(8,128)S(1)}, u32[]{:S(2)}, u32[]{:S(2)}) %collective-permute-start.12) | collective-permute-done | bytes 32800 | tf_op jit(solution)/shard_map/ppermute | solution.py:26
  49.8 0.8 %shard_map.93 = (f32[32,512]{1,0:T(8,128)S(1)}, f32[64,2,128]{2,1,0:T(2,128)}) custom-call(s32[1]{0:T(128)} %bitcast.1.zh_ref.me_ref, f32[16,512]{1,0:T(8,128)S(1)} %shard_map.92.keep_ref, f32[16,512]{1,0:T(8,128)S(1)} %collective-permute-done.12.got_ref), custom_call_target="tpu_custom_call" | custom-call | bytes 1048576 | tf_op jit(solution)/shard_map/pallas_call | solution.py:44
  50.5 8.4 %all-to-all-start = ((f32[64,2,128]{2,1,0:T(2,128)}), f32[64,2,128]{2,1,0:T(2,128)S(1)}, u32[]{:S(2)}, u32[]{:S(2)}) async-start(f32[64,2,128]{2,1,0:T(2,128)} %get-tuple-element.44), calls=%async_computation | async-start | bytes 131072 | tf_op jit(solution)/shard_map/all_to_all | solution.py:288
  58.9 2.8 %collective-permute-start.13 = (f32[32,512]{1,0:T(8,128)S(1)}, f32[32,512]{1,0:T(8,128)S(1)}, u32[]{:S(2)}, u32[]{:S(2)}) collective-permute-start(f32[32,512]{1,0:T(8,128)S(1)} %get-tuple-element.45.lines3_ref), channel_id=1, source_target_pairs={{0,6},{2,4},{4,2},{6,0},{1,7},{3,5},{5,3},{7,1},{8,14},{10,12},{12... | collective-permute-start | bytes 196616 | tf_op jit(solution)/shard_map/ppermute | solution.py:30
  61.7 0.9 %collective-permute-start.14 = (f32[32,512]{1,0:T(8,128)S(1)}, f32[32,512]{1,0:T(8,128)S(1)}, u32[]{:S(2)}, u32[]{:S(2)}) collective-permute-start(f32[32,512]{1,0:T(8,128)S(1)} %get-tuple-element.45.lines3_ref), channel_id=1, source_target_pairs={{0,4},{2,6},{4,0},{6,2},{1,5},{3,7},{5,1},{7,3},{8,12},{10,14},{12... | collective-permute-start | bytes 196616 | tf_op jit(solution)/shard_map/ppermute | solution.py:30
  62.5 0.6 collective-permute-start.15
  63.1 2.3 %collective-permute-done.13.lines0_ref = f32[32,512]{1,0:T(8,128)S(1)} collective-permute-done((f32[32,512]{1,0:T(8,128)S(1)}, f32[32,512]{1,0:T(8,128)S(1)}, u32[]{:S(2)}, u32[]{:S(2)}) %collective-permute-start.13) | collective-permute-done | bytes 65568 | tf_op jit(solution)/shard_map/ppermute | solution.py:30
  65.4 2.0 %collective-permute-done.14.lines1_ref = f32[32,512]{1,0:T(8,128)S(1)} collective-permute-done((f32[32,512]{1,0:T(8,128)S(1)}, f32[32,512]{1,0:T(8,128)S(1)}, u32[]{:S(2)}, u32[]{:S(2)}) %collective-permute-start.14) | collective-permute-done | bytes 65568 | tf_op jit(solution)/shard_map/ppermute | solution.py:30
  67.4 0.0 collective-permute-done.15.lines2_ref
  67.4 0.8 %all-to-all-done.squares_ref = f32[64,2,128]{2,1,0:T(2,128)S(1)} async-done(((f32[64,2,128]{2,1,0:T(2,128)}), f32[64,2,128]{2,1,0:T(2,128)S(1)}, u32[]{:S(2)}, u32[]{:S(2)}) %all-to-all-start) | async-done | bytes 65568 | tf_op jit(solution)/shard_map/all_to_all | solution.py:288
  68.2 0.0 copy-done
  68.2 0.0 copy-done.1
  68.2 0.0 copy-done.2
  68.2 0.0 copy-done.3
  68.2 1.8 %shard_map.94 = (f32[448,1024]{1,0:T(8,128)}, f32[448,128]{1,0:T(8,128)}, f32[448,128]{1,0:T(8,128)}) custom-call(s32[1]{0:T(128)} %bitcast.x_ref, f32[64,2,128]{2,1,0:T(2,128)S(1)} %all-to-all-done.squares_ref, f32[32,512]{1,0:T(8,128)S(1)} %collective-permute-done.13.lines0_ref, f32[32,512]{1,0:T(8,128)S(1)} %collective-permute-done.14.lines1_ref, ...), custom_call_target="tpu_custom_call" | custom-call | flops 117440512 | bytes 4194304 | tf_op jit(solution)/shard_map/pallas_call | solution.py:293
  (4 shorter events, 0.1 us)
Async XLA Ops:
  2.2 5.2 %collective-permute-start = (f32[32,256]{1,0:T(8,128)S(1)}, f32[32,256]{1,0:T(8,128)S(1)}, u32[]{:S(2)}, u32[]{:S(2)}) collective-permute-start(f32[32,256]{1,0:T(8,128)S(1)} %get-tuple-element.26), channel_id=1, source_target_pairs={{0,6},{2,4},{4,2},{6,0},{1,7},{3,5},{5,3},{7,1},{8,14},{10,12},{12... | collective-permute-start | bytes 98312 | tf_op jit(solution)/shard_map/ppermute | solution.py:30
  5.0 5.4 %collective-permute-start.1 = (f32[32,256]{1,0:T(8,128)S(1)}, f32[32,256]{1,0:T(8,128)S(1)}, u32[]{:S(2)}, u32[]{:S(2)}) collective-permute-start(f32[32,256]{1,0:T(8,128)S(1)} %get-tuple-element.27), channel_id=1, source_target_pairs={{0,4},{2,6},{4,0},{6,2},{1,5},{3,7},{5,1},{7,3},{8,12},{10,14},{12... | collective-permute-start | bytes 98312 | tf_op jit(solution)/shard_map/ppermute | solution.py:30
  5.8 4.6 %collective-permute-start.2 = (f32[32,256]{1,0:T(8,128)S(1)}, f32[32,256]{1,0:T(8,128)S(1)}, u32[]{:S(2)}, u32[]{:S(2)}) collective-permute-start(f32[32,256]{1,0:T(8,128)S(1)} %get-tuple-element.28), channel_id=1, source_target_pairs={{0,2},{2,0},{4,6},{6,4},{1,3},{3,1},{5,7},{7,5},{8,10},{10,8},{12,... | collective-permute-start | bytes 98312 | tf_op jit(solution)/shard_map/ppermute | solution.py:30
  10.4 10.5 %collective-permute-start.3 = (f32[16,256]{1,0:T(8,128)S(1)}, f32[16,256]{1,0:T(8,128)S(1)}, u32[]{:S(2)}, u32[]{:S(2)}) collective-permute-start(f32[16,256]{1,0:T(8,128)S(1)} %get-tuple-element.31), channel_id=1, source_target_pairs={{0,1},{1,0},{2,3},{3,2},{4,5},{5,4},{6,7},{7,6},{8,9},{9,8},{10,11... | collective-permute-start | bytes 49160 | tf_op jit(solution)/shard_map/ppermute | solution.py:26
  20.9 47.3 %copy-start = (bf16[1024,128]{1,0:T(8,128)(2,1)S(1)}, bf16[1024,128]{1,0:T(8,128)(2,1)}, u32[]{:S(2)}) copy-start(bf16[1024,128]{1,0:T(8,128)(2,1)} %proj_ref.1) | copy-start | bytes 786436
  20.9 47.3 %copy-start.1 = (bf16[1024,448]{0,1:T(8,128)(2,1)S(1)}, bf16[1024,448]{0,1:T(8,128)(2,1)}, u32[]{:S(2)}) copy-start(bf16[1024,448]{0,1:T(8,128)(2,1)} %param.9) | copy-start | bytes 2752516
  20.9 47.3 %copy-start.2 = (f32[128,448]{0,1:T(8,128)S(1)}, f32[128,448]{0,1:T(8,128)}, u32[]{:S(2)}) copy-start(f32[128,448]{0,1:T(8,128)} %param.10) | copy-start | bytes 688132
  20.9 47.3 %copy-start.3 = (f32[128,448]{0,1:T(8,128)S(1)}, f32[128,448]{0,1:T(8,128)}, u32[]{:S(2)}) copy-start(f32[128,448]{0,1:T(8,128)} %param.11) | copy-start | bytes 688132
  22.2 1.9 %collective-permute-start.4 = (f32[16,8,896]{2,1,0:T(8,128)S(1)}, f32[16,8,896]{2,1,0:T(8,128)S(1)}, u32[]{:S(2)}, u32[]{:S(2)}) collective-permute-start(f32[16,8,896]{2,1,0:T(8,128)S(1)} %get-tuple-element.33), channel_id=1, source_target_pairs={{0,8},{8,0},{1,9},{9,1},{2,10},{10,2},{3,11},{11,3},{4,12},{12,4},... | collective-permute-start | bytes 1376264 | tf_op jit(solution)/shard_map/ppermute | solution.py:26
  24.1 6.3 %collective-permute-start.5 = (f32[4,8,896]{2,1,0:T(8,128)S(1)}, f32[4,8,896]{2,1,0:T(8,128)S(1)}, u32[]{:S(2)}, u32[]{:S(2)}) collective-permute-start(f32[4,8,896]{2,1,0:T(8,128)S(1)} %get-tuple-element.34), channel_id=1, source_target_pairs={{0,192},{64,128},{128,64},{192,0},{1,193},{65,129},{129,65},{193,1... | collective-permute-start | bytes 344072 | tf_op jit(solution)/shard_map/ppermute | solution.py:30
  25.8 7.5 %collective-permute-start.6 = (f32[4,8,896]{2,1,0:T(8,128)S(1)}, f32[4,8,896]{2,1,0:T(8,128)S(1)}, u32[]{:S(2)}, u32[]{:S(2)}) collective-permute-start(f32[4,8,896]{2,1,0:T(8,128)S(1)} %get-tuple-element.35), channel_id=1, source_target_pairs={{0,128},{64,192},{128,0},{192,64},{1,129},{65,193},{129,1},{193,65... | collective-permute-start | bytes 344072 | tf_op jit(solution)/shard_map/ppermute | solution.py:30
  26.7 7.0 %collective-permute-start.7 = (f32[4,8,896]{2,1,0:T(8,128)S(1)}, f32[4,8,896]{2,1,0:T(8,128)S(1)}, u32[]{:S(2)}, u32[]{:S(2)}) collective-permute-start(f32[4,8,896]{2,1,0:T(8,128)S(1)} %get-tuple-element.36), channel_id=1, source_target_pairs={{0,64},{64,0},{128,192},{192,128},{1,65},{65,1},{129,193},{193,129... | collective-permute-start | bytes 344072 | tf_op jit(solution)/shard_map/ppermute | solution.py:30
  33.7 6.0 %collective-permute-start.10 = (f32[8,896]{1,0:T(8,128)S(1)}, f32[8,896]{1,0:T(8,128)S(1)}, u32[]{:S(2)}, u32[]{:S(2)}) collective-permute-start(f32[8,896]{1,0:T(8,128)S(1)} %get-tuple-element.40), channel_id=1, source_target_pairs={{0,48},{16,32},{32,16},{48,0},{1,49},{17,33},{33,17},{49,1},{2,50}... | collective-permute-start | bytes 86024 | tf_op jit(solution)/shard_map/ppermute | solution.py:30
  35.7 4.8 %collective-permute-start.8 = (f32[8,896]{1,0:T(8,128)S(1)}, f32[8,896]{1,0:T(8,128)S(1)}, u32[]{:S(2)}, u32[]{:S(2)}) collective-permute-start(f32[8,896]{1,0:T(8,128)S(1)} %get-tuple-element.38), channel_id=1, source_target_pairs={{0,32},{16,48},{32,0},{48,16},{1,33},{17,49},{33,1},{49,17},{2,34}... | collective-permute-start | bytes 86024 | tf_op jit(solution)/shard_map/ppermute | solution.py:30
  36.3 4.2 %collective-permute-start.9 = (f32[8,896]{1,0:T(8,128)S(1)}, f32[8,896]{1,0:T(8,128)S(1)}, u32[]{:S(2)}, u32[]{:S(2)}) collective-permute-start(f32[8,896]{1,0:T(8,128)S(1)} %get-tuple-element.39), channel_id=1, source_target_pairs={{0,16},{16,0},{32,48},{48,32},{1,17},{17,1},{33,49},{49,33},{2,18}... | collective-permute-start | bytes 86024 | tf_op jit(solution)/shard_map/ppermute | solution.py:30
  40.6 1.3 %collective-permute-start.11 = (f32[8,512]{1,0:T(8,128)S(1)}, f32[8,512]{1,0:T(8,128)S(1)}, u32[]{:S(2)}, u32[]{:S(2)}) collective-permute-start(f32[8,512]{1,0:T(8,128)S(1)} %get-tuple-element.43), channel_id=1, source_target_pairs={{0,8},{8,0},{1,9},{9,1},{2,10},{10,2},{3,11},{11,3},{4,12},{12,4},... | collective-permute-start | bytes 49160 | tf_op jit(solution)/shard_map/ppermute | solution.py:26
  41.9 7.9 %collective-permute-start.12 = (f32[16,512]{1,0:T(8,128)S(1)}, f32[16,512]{1,0:T(8,128)S(1)}, u32[]{:S(2)}, u32[]{:S(2)}) collective-permute-start(f32[16,512]{1,0:T(8,128)S(1)} %shard_map.92.keep_ref), channel_id=1, source_target_pairs={{0,1},{1,0},{2,3},{3,2},{4,5},{5,4},{6,7},{7,6},{8,9},{9,8},{10,11... | collective-permute-start | bytes 98312 | tf_op jit(solution)/shard_map/ppermute | solution.py:26
  50.5 17.7 %all-to-all-start = ((f32[64,2,128]{2,1,0:T(2,128)}), f32[64,2,128]{2,1,0:T(2,128)S(1)}, u32[]{:S(2)}, u32[]{:S(2)}) async-start(f32[64,2,128]{2,1,0:T(2,128)} %get-tuple-element.44), calls=%async_computation | async-start | bytes 131072 | tf_op jit(solution)/shard_map/all_to_all | solution.py:288
  58.9 6.5 %collective-permute-start.13 = (f32[32,512]{1,0:T(8,128)S(1)}, f32[32,512]{1,0:T(8,128)S(1)}, u32[]{:S(2)}, u32[]{:S(2)}) collective-permute-start(f32[32,512]{1,0:T(8,128)S(1)} %get-tuple-element.45.lines3_ref), channel_id=1, source_target_pairs={{0,6},{2,4},{4,2},{6,0},{1,7},{3,5},{5,3},{7,1},{8,14},{10,12},{12... | collective-permute-start | bytes 196616 | tf_op jit(solution)/shard_map/ppermute | solution.py:30
  61.7 5.8 %collective-permute-start.14 = (f32[32,512]{1,0:T(8,128)S(1)}, f32[32,512]{1,0:T(8,128)S(1)}, u32[]{:S(2)}, u32[]{:S(2)}) collective-permute-start(f32[32,512]{1,0:T(8,128)S(1)} %get-tuple-element.45.lines3_ref), channel_id=1, source_target_pairs={{0,4},{2,6},{4,0},{6,2},{1,5},{3,7},{5,1},{7,3},{8,12},{10,14},{12... | collective-permute-start | bytes 196616 | tf_op jit(solution)/shard_map/ppermute | solution.py:30
  62.5 4.9 %collective-permute-start.15 = (f32[32,512]{1,0:T(8,128)S(1)}, f32[32,512]{1,0:T(8,128)S(1)}, u32[]{:S(2)}, u32[]{:S(2)}) collective-permute-start(f32[32,512]{1,0:T(8,128)S(1)} %get-tuple-element.45.lines3_ref), channel_id=1, source_target_pairs={{0,2},{2,0},{4,6},{6,4},{1,3},{3,1},{5,7},{7,5},{8,10},{10,8},{12,... | collective-permute-start | bytes 196616 | tf_op jit(solution)/shard_map/ppermute | solution.py:30
